TPU v7x, 32 devices: a whole 2x2x4 slice. The times are simulated.
32 devices in a mesh: groups: 2 (over x), pts: 16 (over z, y, core).
Axes of the slice: x: 2, y: 2, z: 4, core: 2. Of those that a mesh axis runs over, the one named last changes fastest.
Arguments:
- spectra_in: float32 [1152, 4096], P(None, ('groups', 'pts')), parts along dimension 1, may hold values from 0.02 to 40, as said below
- coarse_spectra: float32 [2, 1152, 4096], P(None, None, ('groups', 'pts')), parts along dimension 2, may hold values from 0.2 to 4
- wind_speed: float32 [4096], P('groups'), parts along dimension 0, may hold values from 2 to 20
- wind_heading: float32 [4096], P('groups'), parts along dimension 0, may hold values from -3.140625 to 3.140625
- sea_mask: int32 [2048], replicated, may hold values 0 or 1
- neighbours: int32 [6, 2048], replicated, may hold values from 0 to 2047
- edge_x: float32 [6, 2048], replicated, may hold values from -1 to 1
- edge_y: float32 [6, 2048], replicated, may hold values from -1 to 1
- bound_points: int32 [32], replicated, may hold values from 0 to 2047, as said below
- bound_cells: int32 [4, 32], replicated, may hold values from 0 to 2047
- bound_weights: float32 [4, 32], replicated, may hold values from 0.1 to 1
Outputs:
- spectra_out: float32 [1152, 4096], P(None, ('groups', 'pts')), parts along dimension 1
There are 2 independent parts, one for each index of `groups`. A program takes and returns all parts, laid end to end along the dimension named above; an argument that names none is the same for every part. Nothing has to cross between parts.
Inputs may be any that keep to these rules, and one draw needn't show every extreme that they name: `spectra_in`: positive spectral densities. `bound_points`: 32 distinct fine point indices.
All inputs are finite; a program needn't handle non-finite values.
Results may differ from a plain program's by a relative error of at most 0.0003.
Values sent between devices are 32-bit elements; how exact they have to be, the bound alone decides.
No kernel may reach another device: no remote copies, remote signals or barrier semaphores. Data moves between devices by JAX's collectives and lax.ppermute only.
A program may use at most 256 MiB of HBM per device.

v0:
```python
import jax
import jax.numpy as jnp
from jax import lax
from jax.sharding import PartitionSpec as P

NDIR = 36
NFREQ = 32
SUB = 4
STEPS = 2


epsilon = 1e-06
courant = 0.1


def freq_tables(components):
    freq_index = (components // NDIR).astype(jnp.float32)
    dir_index = (components % NDIR).astype(jnp.float32)
    growth = jnp.log(jnp.asarray(1.1, jnp.float32))
    radian_freq = 0.25 * jnp.exp(freq_index * growth)
    freq_top = 0.25 * jnp.exp((NFREQ - 1) * growth)
    freq_total = NDIR * jnp.sum(0.25 * jnp.exp(jnp.arange(NFREQ).astype(jnp.float32) * growth))
    weight = radian_freq / freq_total
    dir_angle = dir_index * (2.0 * jnp.pi / NDIR)
    return (radian_freq, weight, dir_angle, freq_top)


def statistics(spectra, components):
    radian_freq, weight, dir_angle, freq_top = freq_tables(components)
    energy = jnp.sum(weight[:, None] * spectra, axis=0)
    inverse = jnp.sum((weight / radian_freq)[:, None] * spectra, axis=0)
    return (energy, inverse)


def apply_sources(spectra, components, energy, inverse, wind_speed, wind_heading, active):
    radian_freq, weight, dir_angle, freq_top = freq_tables(components)
    mean_freq = energy / (inverse + epsilon)
    mean_period = inverse / (energy + epsilon)
    steepness = energy * (0.5 * mean_freq) ** 2
    steep_ratio = steepness / (1.0 + steepness)
    relative = radian_freq / freq_top
    wind_in = (
        0.6
        * relative[:, None]
        * jax.nn.sigmoid(
            wind_speed[None, :]
            * jnp.cos(dir_angle[:, None] - wind_heading[None, :])
            * radian_freq[:, None]
            / 8.0
            - 1.0
        )
    )
    dissipation = (relative * relative)[:, None] * (mean_period * freq_top * steep_ratio)[None, :]
    return spectra * jnp.exp(wind_in - dissipation) * active[None, :]


def interpolate(coarse_block, bound_cells, bound_weights):
    norm_weights = bound_weights / jnp.sum(bound_weights, axis=0, keepdims=True)
    corners = coarse_block[:, :, bound_cells]
    return jnp.sum(norm_weights[None, None] * corners, axis=2)


def coefficients(components, edge_x, edge_y):
    radian_freq, weight, dir_angle, freq_top = freq_tables(components)
    group_speed = courant * 0.25 / radian_freq
    edge_coef = group_speed[None, :, None] * (
        jnp.cos(dir_angle)[None, :, None] * edge_x[:, None, :]
        + jnp.sin(dir_angle)[None, :, None] * edge_y[:, None, :]
    )
    return (jnp.sum(jnp.maximum(edge_coef, 0.0), axis=0), jnp.minimum(edge_coef, 0.0))


def advect(spectra, outflow, inflow, neighbours, active, bound_values, bound_points, start):
    edge_count = neighbours.shape[0]
    for sub_step in range(SUB):
        upwind = inflow[0] * spectra[:, neighbours[0]]
        for edge in range(1, edge_count):
            upwind = upwind + inflow[edge] * spectra[:, neighbours[edge]]
        spectra = (spectra - outflow * spectra - upwind) * active[None, :]
        time_frac = (start + sub_step + 1) / (STEPS * SUB)
        edge_values = (1.0 - time_frac) * bound_values[0] + time_frac * bound_values[1]
        spectra = spectra.at[:, bound_points].set(edge_values)
    return spectra


def to_components(spectra):
    return lax.all_to_all(spectra, "pts", split_axis=0, concat_axis=1, tiled=True)


def to_points(spectra):
    return lax.all_to_all(spectra, "pts", split_axis=1, concat_axis=0, tiled=True)


def shards(
    spectra_in,
    coarse_spectra,
    wind_speed,
    wind_heading,
    sea_mask,
    neighbours,
    edge_x,
    edge_y,
    bound_points,
    bound_cells,
    bound_weights,
):
    device_count = lax.axis_size("pts")
    device_place = lax.axis_index("pts")
    point_count = spectra_in.shape[1]
    comp_total = spectra_in.shape[0]
    local_count = comp_total // device_count
    active = sea_mask.astype(jnp.float32)
    all_comp = jnp.arange(comp_total, dtype=jnp.int32)
    my_comp = device_place * local_count + jnp.arange(local_count, dtype=jnp.int32)
    first_point = device_place * point_count
    own_speed = lax.dynamic_slice_in_dim(wind_speed, first_point, point_count)
    own_heading = lax.dynamic_slice_in_dim(wind_heading, first_point, point_count)
    own_active = lax.dynamic_slice_in_dim(active, first_point, point_count)
    coarse_here = lax.all_to_all(coarse_spectra, "pts", split_axis=1, concat_axis=2, tiled=True)
    bound_values = interpolate(coarse_here, bound_cells, bound_weights)
    outflow, inflow = coefficients(my_comp, edge_x, edge_y)
    spectra = spectra_in
    for coarse_step in range(STEPS):
        energy, inverse = statistics(spectra, all_comp)
        spectra = apply_sources(
            spectra, all_comp, energy, inverse, own_speed, own_heading, own_active
        )
        comp_field = to_components(spectra)
        comp_field = advect(
            comp_field,
            outflow,
            inflow,
            neighbours,
            active,
            bound_values,
            bound_points,
            coarse_step * SUB,
        )
        spectra = to_points(comp_field)
    return spectra


def solution(mesh):
    in_specs = (
        P(None, ("groups", "pts")),
        P(None, None, ("groups", "pts")),
        P("groups"),
        P("groups"),
        P(),
        P(),
        P(),
        P(),
        P(),
        P(),
        P(),
    )
    out_specs = P(None, ("groups", "pts"))
    return jax.shard_map(shards, mesh=mesh, in_specs=in_specs, out_specs=out_specs, check_vma=False)
```

profile of v0, /device:TPU:0, one launch (start us, length us, event | category | flops | bytes accessed | tf_op | source)
XLA Modules:
  0.0 530.4 jit_solution(4198341641119002324)
XLA Ops:
  101.7 7.6 %gather_fusion.10 = f32[2048,72]{1,0:T(8,128)} fusion(f32[72,2048]{0,1:T(8,128)S(1)} %scatter_custom_fusion, s32[2048]{0:T(1024)S(1)} %broadcast_clamp_fusion.2), kind=kCustom, calls=%fused_computation.10 | custom fusion | bytes 1187840 | tf_op jit(solution)/shard_map/gather | solution.py:78
  109.3 7.6 %gather_fusion.11 = f32[2048,72]{1,0:T(8,128)} fusion(f32[72,2048]{0,1:T(8,128)S(1)} %scatter_custom_fusion, s32[2048]{0:T(1024)S(1)} %broadcast_clamp_fusion.1), kind=kCustom, calls=%fused_computation.11 | custom fusion | bytes 1187840 | tf_op jit(solution)/shard_map/gather | solution.py:78
  116.8 7.6 %gather_fusion.7 = f32[2048,72]{1,0:T(8,128)} fusion(f32[72,2048]{0,1:T(8,128)S(1)} %scatter_custom_fusion, s32[2048]{0:T(1024)S(1)} %broadcast_clamp_fusion.5), kind=kCustom, calls=%fused_computation.7 | custom fusion | bytes 1187840 | tf_op jit(solution)/shard_map/gather | solution.py:76
  153.1 7.6 %gather_fusion.13 = f32[2048,72]{1,0:T(8,128)} fusion(f32[72,2048]{0,1:T(8,128)S(1)} %scatter_custom_fusion.1, s32[2048]{0:T(1024)S(1)} %broadcast_clamp_fusion.5), kind=kCustom, calls=%fused_computation.13 | custom fusion | bytes 1187840 | tf_op jit(solution)/shard_map/gather | solution.py:76
  175.8 7.6 %gather_fusion.16 = f32[2048,72]{1,0:T(8,128)} fusion(f32[72,2048]{0,1:T(8,128)S(1)} %scatter_custom_fusion.1, s32[2048]{0:T(1024)S(1)} %broadcast_clamp_fusion.2), kind=kCustom, calls=%fused_computation.16 | custom fusion | bytes 1187840 | tf_op jit(solution)/shard_map/gather | solution.py:78
  183.4 7.6 %gather_fusion.17 = f32[2048,72]{1,0:T(8,128)} fusion(f32[72,2048]{0,1:T(8,128)S(1)} %scatter_custom_fusion.1, s32[2048]{0:T(1024)S(1)} %broadcast_clamp_fusion.1), kind=kCustom, calls=%fused_computation.17 | custom fusion | bytes 1187840 | tf_op jit(solution)/shard_map/gather | solution.py:78
  204.6 7.6 %gather_fusion.19 = f32[2048,72]{1,0:T(8,128)} fusion(f32[72,2048]{0,1:T(8,128)S(1)} %scatter_custom_fusion.2, s32[2048]{0:T(1024)S(1)} %broadcast_clamp_fusion.5), kind=kCustom, calls=%fused_computation.19 | custom fusion | bytes 1187840 | tf_op jit(solution)/shard_map/gather | solution.py:76
  227.2 7.6 %gather_fusion.22 = f32[2048,72]{1,0:T(8,128)} fusion(f32[72,2048]{0,1:T(8,128)S(1)} %scatter_custom_fusion.2, s32[2048]{0:T(1024)S(1)} %broadcast_clamp_fusion.2), kind=kCustom, calls=%fused_computation.22 | custom fusion | bytes 1187840 | tf_op jit(solution)/shard_map/gather | solution.py:78
  234.8 7.6 %gather_fusion.23 = f32[2048,72]{1,0:T(8,128)} fusion(f32[72,2048]{0,1:T(8,128)S(1)} %scatter_custom_fusion.2, s32[2048]{0:T(1024)S(1)} %broadcast_clamp_fusion.1), kind=kCustom, calls=%fused_computation.23 | custom fusion | bytes 1187840 | tf_op jit(solution)/shard_map/gather | solution.py:78
  263.4 15.5 %all-to-all-done.2 = f32[72,16,128]{2,0,1:T(8,128)S(1)} async-done(((f32[72,16,128]{2,0,1:T(8,128)}), f32[72,16,128]{2,0,1:T(8,128)S(1)}, u32[]{:S(2)}, u32[]{:S(2)}) %all-to-all-start.2) | async-done | bytes 589856 | tf_op jit(solution)/shard_map/all_to_all | solution.py:91
  281.6 21.5 %all_to_all.88 = f32[16,72,128]{2,1,0:T(8,128)S(1)} all-to-all(f32[16,72,128]{2,1,0:T(8,128)S(1)} %fusion.59), channel_id=1, replica_groups=mesh['groups'=2,'pts'=16] {'pts'}, dimensions={0} | all-to-all | bytes 1179648 | tf_op jit(solution)/shard_map/all_to_all | solution.py:87
  303.5 7.6 %gather_fusion.25 = f32[2048,72]{1,0:T(8,128)} fusion(f32[72,2048]{0,1:T(8,128)S(1)} %bitcast.461, s32[2048]{0:T(1024)S(1)} %broadcast_clamp_fusion.5), kind=kCustom, calls=%fused_computation.25 | custom fusion | bytes 1187840 | tf_op jit(solution)/shard_map/gather | solution.py:76
  326.2 7.6 %gather_fusion.28 = f32[2048,72]{1,0:T(8,128)} fusion(f32[72,2048]{0,1:T(8,128)S(1)} %bitcast.464, s32[2048]{0:T(1024)S(1)} %broadcast_clamp_fusion.2), kind=kCustom, calls=%fused_computation.28 | custom fusion | bytes 1187840 | tf_op jit(solution)/shard_map/gather | solution.py:78
  333.7 7.6 %gather_fusion.29 = f32[2048,72]{1,0:T(8,128)} fusion(f32[72,2048]{0,1:T(8,128)S(1)} %bitcast.465, s32[2048]{0:T(1024)S(1)} %broadcast_clamp_fusion.1), kind=kCustom, calls=%fused_computation.29 | custom fusion | bytes 1187840 | tf_op jit(solution)/shard_map/gather | solution.py:78
  354.9 7.6 %gather_fusion.31 = f32[2048,72]{1,0:T(8,128)} fusion(f32[72,2048]{0,1:T(8,128)S(1)} %scatter_custom_fusion.4, s32[2048]{0:T(1024)S(1)} %broadcast_clamp_fusion.5), kind=kCustom, calls=%fused_computation.31 | custom fusion | bytes 1187840 | tf_op jit(solution)/shard_map/gather | solution.py:76
  377.6 7.6 %gather_fusion.34 = f32[2048,72]{1,0:T(8,128)} fusion(f32[72,2048]{0,1:T(8,128)S(1)} %scatter_custom_fusion.4, s32[2048]{0:T(1024)S(1)} %broadcast_clamp_fusion.2), kind=kCustom, calls=%fused_computation.34 | custom fusion | bytes 1187840 | tf_op jit(solution)/shard_map/gather | solution.py:78
  385.2 7.6 %gather_fusion.35 = f32[2048,72]{1,0:T(8,128)} fusion(f32[72,2048]{0,1:T(8,128)S(1)} %scatter_custom_fusion.4, s32[2048]{0:T(1024)S(1)} %broadcast_clamp_fusion.1), kind=kCustom, calls=%fused_computation.35 | custom fusion | bytes 1187840 | tf_op jit(solution)/shard_map/gather | solution.py:78
  406.3 7.6 %gather_fusion.37 = f32[2048,72]{1,0:T(8,128)} fusion(f32[72,2048]{0,1:T(8,128)S(1)} %scatter_custom_fusion.5, s32[2048]{0:T(1024)S(1)} %broadcast_clamp_fusion.5), kind=kCustom, calls=%fused_computation.37 | custom fusion | bytes 1187840 | tf_op jit(solution)/shard_map/gather | solution.py:76
  429.0 7.6 %gather_fusion.40 = f32[2048,72]{1,0:T(8,128)} fusion(f32[72,2048]{0,1:T(8,128)S(1)} %scatter_custom_fusion.5, s32[2048]{0:T(1024)S(1)} %broadcast_clamp_fusion.2), kind=kCustom, calls=%fused_computation.40 | custom fusion | bytes 1187840 | tf_op jit(solution)/shard_map/gather | solution.py:78
  436.6 7.6 %gather_fusion.41 = f32[2048,72]{1,0:T(8,128)} fusion(f32[72,2048]{0,1:T(8,128)S(1)} %scatter_custom_fusion.5, s32[2048]{0:T(1024)S(1)} %broadcast_clamp_fusion.1), kind=kCustom, calls=%fused_computation.41 | custom fusion | bytes 1187840 | tf_op jit(solution)/shard_map/gather | solution.py:78
  457.8 7.6 %gather_fusion.43 = f32[2048,72]{1,0:T(8,128)} fusion(f32[72,2048]{0,1:T(8,128)S(1)} %scatter_custom_fusion.6, s32[2048]{0:T(1024)S(1)} %broadcast_clamp_fusion.5), kind=kCustom, calls=%fused_computation.43 | custom fusion | bytes 1187840 | tf_op jit(solution)/shard_map/gather | solution.py:76
  480.5 7.6 %gather_fusion.46 = f32[2048,72]{1,0:T(8,128)} fusion(f32[72,2048]{0,1:T(8,128)S(1)} %scatter_custom_fusion.6, s32[2048]{0:T(1024)S(1)} %broadcast_clamp_fusion.2), kind=kCustom, calls=%fused_computation.46 | custom fusion | bytes 1187840 | tf_op jit(solution)/shard_map/gather | solution.py:78
  488.0 7.6 %gather_fusion.47 = f32[2048,72]{1,0:T(8,128)} fusion(f32[72,2048]{0,1:T(8,128)S(1)} %scatter_custom_fusion.6, s32[2048]{0:T(1024)S(1)} %broadcast_clamp_fusion.1), kind=kCustom, calls=%fused_computation.47 | custom fusion | bytes 1187840 | tf_op jit(solution)/shard_map/gather | solution.py:78
  509.5 20.1 %all_to_all.89 = f32[72,16,128]{2,0,1:T(8,128)S(1)} all-to-all(f32[72,16,128]{2,0,1:T(8,128)S(1)} %copy.25), channel_id=1, replica_groups=mesh['groups'=2,'pts'=16] {'pts'}, dimensions={1} | all-to-all | bytes 1179648 | tf_op jit(solution)/shard_map/all_to_all | solution.py:91
  (98 shorter events, 312.6 us)
Async XLA Ops:
  0.0 37.8 %copy-start.2 = (s32[32]{0:T(128)S(1)}, s32[32]{0:T(128)}, u32[]{:S(2)}) copy-start(s32[32]{0:T(128)} %param.19) | copy-start | bytes 388
  0.0 37.8 %copy-start.1 = (f32[6,2048]{1,0:T(8,128)S(1)}, f32[6,2048]{1,0:T(8,128)}, u32[]{:S(2)}) copy-start(f32[6,2048]{1,0:T(8,128)} %param.17) | copy-start | bytes 147460
  0.0 37.8 %copy-start = (f32[6,2048]{1,0:T(8,128)S(1)}, f32[6,2048]{1,0:T(8,128)}, u32[]{:S(2)}) copy-start(f32[6,2048]{1,0:T(8,128)} %param.18) | copy-start | bytes 147460
  10.3 22.9 %all-to-all-start = ((f32[16,72,128]{2,1,0:T(8,128)}), f32[16,72,128]{2,1,0:T(8,128)S(1)}, u32[]{:S(2)}, u32[]{:S(2)}) async-start(f32[16,72,128]{2,1,0:T(8,128)} %bitcast), calls=%async_computation | async-start | bytes 1179648 | tf_op jit(solution)/shard_map/all_to_all | solution.py:87
  33.3 61.2 %all-to-all-start.1 = ((f32[2,1152,128]{2,0,1:T(2,128)}), f32[2,1152,128]{2,0,1:T(2,128)}, u32[]{:S(2)}, u32[]{:S(2)}) async-start(f32[2,1152,128]{2,0,1:T(2,128)} %copy.19), calls=%async_computation.1 | async-start | bytes 2359296 | tf_op jit(solution)/shard_map/all_to_all | solution.py:119
  257.1 21.7 %all-to-all-start.2 = ((f32[72,16,128]{2,0,1:T(8,128)}), f32[72,16,128]{2,0,1:T(8,128)S(1)}, u32[]{:S(2)}, u32[]{:S(2)}) async-start(f32[72,16,128]{2,0,1:T(8,128)} %copy.23), calls=%async_computation.2 | async-start | bytes 1179648 | tf_op jit(solution)/shard_map/all_to_all | solution.py:91
where the time goes:
time: 531 us; the launch traced here: 530 us
  local copies, waits for them, and re-layouts  379 us (71%)
  other arithmetic  68.2 us (13%)
  blocking collectives  41.6 us (8%)
  waiting for transfers between devices  21.9 us (4%)
  starting transfers between devices  18 us (3%)
    gather x40, local copies, waits for them, and re-layouts, advect(): upwind = upwind + inflow[edge] * spectra[:, neighbours[edge]]  302 us
    gather x8, local copies, waits for them, and re-layouts, advect(): upwind = inflow[0] * spectra[:, neighbours[0]]  60.6 us
    mul x8, other arithmetic, advect(): spectra = (spectra - outflow * spectra - upwind) * active[None, :]  39.6 us
    all_to_all x1, blocking collectives, to_components(): lax.all_to_all(spectra, 'pts', split_axis=0, concat_axis=1, tiled=True)  21.5 us
    all_to_all x1, blocking collectives, to_points(): lax.all_to_all(spectra, 'pts', split_axis=1, concat_axis=0, tiled=True)  20.1 us
    all_to_all x1, waiting for transfers between devices, to_points(): lax.all_to_all(spectra, 'pts', split_axis=1, concat_axis=0, tiled=True)  15.5 us
  transfers between devices with their start and end apart: 3, of which 2 were waited for; matrix products, arithmetic and copies ran while one was open for 12% of the time, Pallas kernels for 0%

commit v1 on v0

--- a/solution.py
+++ b/solution.py
@@ -1,12 +1,19 @@
+import functools
+import math
+
 import jax
 import jax.numpy as jnp
+import numpy as np
 from jax import lax
+from jax.experimental import pallas as pl
+from jax.experimental.pallas import tpu as pltpu
 from jax.sharding import PartitionSpec as P
 
 NDIR = 36
 NFREQ = 32
 SUB = 4
 STEPS = 2
+LANES = 128
 
 
 epsilon = 1e-06
@@ -91,6 +98,365 @@
     return lax.all_to_all(spectra, "pts", split_axis=1, concat_axis=0, tiled=True)
 
 
+GROUPS = 9
+GROUP_ROWS = 8
+BASE_GROUP = (0, 1, 2, 3, 0, 1, 2, 3, 4)
+
+
+def row_layout():
+    dirs = np.zeros((GROUPS * GROUP_ROWS,), np.int32)
+    upper = np.zeros((GROUPS * GROUP_ROWS,), np.int32)
+    for row in range(GROUPS * GROUP_ROWS):
+        group, sub = divmod(row, GROUP_ROWS)
+        if group < 8:
+            dirs[row] = 8 * (group % 4) + sub
+            upper[row] = group // 4
+        else:
+            dirs[row] = 32 + sub % 4
+            upper[row] = sub // 4
+    return dirs, upper
+
+
+def group_rows(group):
+    return pl.ds(GROUP_ROWS * group, GROUP_ROWS)
+
+
+def load_natural(ref, block):
+    lower = [ref[block, group_rows(group), :] for group in range(4)]
+    upper = [ref[block, pl.ds(NDIR + GROUP_ROWS * group, GROUP_ROWS), :] for group in range(4)]
+    sub = lax.broadcasted_iota(jnp.int32, (GROUP_ROWS, LANES), 0)
+    last = jnp.where(sub < 4, ref[block, pl.ds(32, 8), :], ref[block, pl.ds(64, 8), :])
+    return lower + upper + [last]
+
+
+def store_natural(ref, block, values):
+    for group in range(4):
+        ref[block, group_rows(group), :] = values[group]
+    for group in range(4):
+        ref[block, pl.ds(NDIR + GROUP_ROWS * group, GROUP_ROWS), :] = values[4 + group]
+    ref[block, pl.ds(32, 4), :] = values[8][0:4]
+    ref[block, pl.ds(68, 4), :] = values[8][4:8]
+
+
+def row_tables(device_place):
+    dirs, upper = row_layout()
+    freq = (2 * device_place + jnp.asarray(upper)).astype(jnp.int32)
+    radian_freq, weight, _, freq_top = freq_tables(freq * NDIR)
+    relative = radian_freq / freq_top
+    group_speed = courant * 0.25 / radian_freq
+    table = jnp.stack([radian_freq, 0.6 * relative, relative * relative * freq_top, group_speed, weight, weight / radian_freq])
+    return jnp.broadcast_to(table[:, :, None], table.shape + (LANES,))
+
+
+def direction_tables():
+    dirs, _ = row_layout()
+    angle = dirs.astype(np.float64) * (2.0 * np.pi / NDIR)
+    table = np.stack([np.cos(angle), np.sin(angle)]).astype(np.float32)
+    return jnp.asarray(np.broadcast_to(table[:, :, None], table.shape + (LANES,)))
+
+
+def setup_kernel(points_ref, edge_ref, rows_ref, dirs_ref, keep_ref, base_ref, growth_ref):
+    edge_count = edge_ref.shape[0]
+
+    def block(place, _):
+        speed = jnp.broadcast_to(points_ref[place, 0:1, :], (GROUP_ROWS, LANES)) * 0.125
+        heading = jnp.broadcast_to(points_ref[place, 1:2, :], (GROUP_ROWS, LANES))
+        active = jnp.broadcast_to(points_ref[place, 2:3, :], (GROUP_ROWS, LANES))
+        free = jnp.broadcast_to(points_ref[place, 3:4, :], (GROUP_ROWS, LANES))
+        along, across = speed * jnp.cos(heading), speed * jnp.sin(heading)
+        total = []
+        for base_group, group in enumerate((0, 1, 2, 3, 8)):
+            cosine, sine = dirs_ref[0, group_rows(group), :], dirs_ref[1, group_rows(group), :]
+            out = jnp.zeros((GROUP_ROWS, LANES), jnp.float32)
+            for edge in range(edge_count):
+                x = jnp.broadcast_to(edge_ref[edge, place, 0:1, :], (GROUP_ROWS, LANES))
+                y = jnp.broadcast_to(edge_ref[edge, place, 1:2, :], (GROUP_ROWS, LANES))
+                flow = cosine * x + sine * y
+                out = out + jnp.maximum(flow, 0.0)
+                base_ref[place, edge, group_rows(base_group), :] = jnp.minimum(flow, 0.0) * free
+            total.append(out)
+        for group in range(GROUPS):
+            rows = group_rows(group)
+            cosine, sine = dirs_ref[0, rows, :], dirs_ref[1, rows, :]
+            wind = (along * cosine + across * sine) * rows_ref[0, rows, :] - 1.0
+            growth_ref[place, rows, :] = jnp.exp(rows_ref[1, rows, :] * jax.nn.sigmoid(wind)) * active
+            keep_ref[place, rows, :] = (1.0 - rows_ref[3, rows, :] * total[BASE_GROUP[group]]) * free
+        return 0
+
+    lax.fori_loop(0, keep_ref.shape[0], block, 0)
+
+
+def boundary_kernel(bound_ref, select_ref, start_ref, slope_ref):
+    total = bound_ref[0]
+    for source in range(1, bound_ref.shape[0]):
+        total = total + bound_ref[source]
+    sub = lax.broadcasted_iota(jnp.int32, (GROUP_ROWS, LANES), 0)
+
+    def block(place, _):
+        pieces = []
+        for piece in range(4):
+            pieces.append(
+                jnp.dot(
+                    total,
+                    select_ref[piece, place],
+                    preferred_element_type=jnp.float32,
+                    precision=lax.Precision.HIGHEST,
+                )
+            )
+        for out_ref, values in (
+            (start_ref, (pieces[0], pieces[2])),
+            (slope_ref, (pieces[1] - pieces[0], pieces[3] - pieces[2])),
+        ):
+            for half in range(2):
+                for group in range(4):
+                    out_ref[place, group_rows(4 * half + group), :] = values[half][8 * group : 8 * group + 8]
+            out_ref[place, pl.ds(64, 4), :] = values[0][32:36]
+            out_ref[place, pl.ds(68, 4), :] = values[1][32:36]
+        return 0
+
+    lax.fori_loop(0, start_ref.shape[0], block, 0)
+
+
+def take_lanes(values, lanes):
+    return jnp.take_along_axis(values, lanes, axis=1, mode="promise_in_bounds")
+
+
+def fine_kernel(
+    first,
+    state_ref,
+    moments_ref,
+    index_ref,
+    keep_ref,
+    base_ref,
+    growth_ref,
+    start_ref,
+    slope_ref,
+    rows_ref,
+    out_ref,
+    *rest,
+):
+    if first:
+        sums_ref, field, words, speed = rest
+    else:
+        field, words, speed = rest
+    blocks = keep_ref.shape[0]
+    half = blocks // 2
+    edge_count = base_ref.shape[1]
+    first_step = 0 if first else SUB
+
+    if first:
+
+        def enter(place, _):
+            for group, value in enumerate(load_natural(state_ref, place)):
+                field[0, place, group_rows(group), :] = value
+            return 0
+
+    else:
+
+        def enter(place, _):
+            energy = jnp.broadcast_to(moments_ref[2 * place : 2 * place + 1, :], (GROUP_ROWS, LANES))
+            inverse = jnp.broadcast_to(moments_ref[2 * place + 1 : 2 * place + 2, :], (GROUP_ROWS, LANES))
+            mean_freq = energy / (inverse + epsilon)
+            steepness = energy * (0.5 * mean_freq) * (0.5 * mean_freq)
+            loss = inverse / (energy + epsilon) * (steepness / (1.0 + steepness))
+            lower = jnp.exp(-rows_ref[2, group_rows(0), :] * loss)
+            upper = jnp.exp(-rows_ref[2, group_rows(4), :] * loss)
+            last = jnp.exp(-rows_ref[2, group_rows(8), :] * loss)
+            decay = [lower] * 4 + [upper] * 4 + [last]
+            for group in range(GROUPS):
+                rows = group_rows(group)
+                field[0, place, rows, :] = state_ref[place, rows, :] * growth_ref[place, rows, :] * decay[group]
+            return 0
+
+    if first:
+        lax.fori_loop(0, blocks, enter, 0)
+    else:
+        for place in range(blocks):
+            enter(place, 0)
+
+    def fine_step(number, _):
+        source = lax.rem(number, 2)
+        time_frac = (number + (first_step + 1)).astype(jnp.float32) * (1.0 / (STEPS * SUB))
+        for group in range(GROUPS):
+            rows = group_rows(group)
+            values = [field[source, place, rows, :] for place in range(blocks)]
+            top = functools.reduce(jnp.maximum, values)
+            top = jnp.maximum(jnp.max(top, axis=1, keepdims=True), 1e-30)
+            scale = jnp.broadcast_to(65535.0 / top, (GROUP_ROWS, LANES))
+            speed[rows, :] = rows_ref[3, rows, :] * (top * (1.0 / 65535.0))
+            coded = [(value * scale + 0.5).astype(jnp.int32) for value in values]
+            for place in range(half):
+                words[place, rows, :] = (coded[place + half] << 16) | coded[place]
+
+        def block(place, _):
+            inflow = [None] * GROUPS
+            for edge in range(edge_count):
+                index = index_ref[place, edge]
+                lanes = index & (LANES - 1)
+                masks = [(index & (LANES << level)) != 0 for level in range(half.bit_length() - 1)]
+                shift = (index >> (half.bit_length() + 6)) << 4
+
+                def pick(low, level, rows):
+                    if level == 0:
+                        return take_lanes(words[low, rows, :], lanes)
+                    step = 1 << (level - 1)
+                    below = pick(low, level - 1, rows)
+                    above = pick(low + step, level - 1, rows)
+                    return jnp.where(masks[level - 1], above, below)
+
+                for group in range(GROUPS):
+                    word = pick(0, half.bit_length() - 1, group_rows(group))
+                    value = (lax.shift_right_logical(word, shift) & 65535).astype(jnp.float32)
+                    term = base_ref[place, edge, group_rows(BASE_GROUP[group]), :] * value
+                    inflow[group] = term if inflow[group] is None else inflow[group] + term
+            for group in range(GROUPS):
+                rows = group_rows(group)
+                field[1 - source, place, rows, :] = (
+                    field[source, place, rows, :] * keep_ref[place, rows, :]
+                    - speed[rows, :] * inflow[group]
+                    + (start_ref[place, rows, :] + time_frac * slope_ref[place, rows, :])
+                )
+            return 0
+
+        lax.fori_loop(0, blocks, block, 0)
+        return 0
+
+    lax.fori_loop(0, SUB, fine_step, 0)
+
+    def leave(place, _):
+        values = [field[SUB % 2, place, group_rows(group), :] for group in range(GROUPS)]
+        if first:
+            energy, inverse = None, None
+            for group in range(GROUPS):
+                rows = group_rows(group)
+                out_ref[place, rows, :] = values[group]
+                part = rows_ref[4, rows, :] * values[group]
+                energy = part if energy is None else energy + part
+                part = rows_ref[5, rows, :] * values[group]
+                inverse = part if inverse is None else inverse + part
+            sums_ref[place, 0:1, :] = jnp.sum(energy, axis=0, keepdims=True)
+            sums_ref[place, 1:2, :] = jnp.sum(inverse, axis=0, keepdims=True)
+        else:
+            store_natural(out_ref, place, values)
+        return 0
+
+    lax.fori_loop(0, blocks, leave, 0)
+
+
+def in_vmem(count):
+    return [pl.BlockSpec(memory_space=pltpu.VMEM)] * count
+
+
+def params():
+    return pltpu.CompilerParams(vmem_limit_bytes=56 << 20)
+
+
+def whole_frequencies(
+    spectra_in,
+    coarse_spectra,
+    wind_speed,
+    wind_heading,
+    active,
+    neighbours,
+    edge_x,
+    edge_y,
+    bound_points,
+    bound_cells,
+    bound_weights,
+):
+    device_count = lax.axis_size("pts")
+    device_place = lax.axis_index("pts")
+    comp_total, point_count = spectra_in.shape
+    local_count = comp_total // device_count
+    edge_count, grid_points = neighbours.shape
+    blocks = grid_points // LANES
+    bound_count = bound_points.shape[0]
+    f32 = jnp.float32
+    all_comp = jnp.arange(comp_total, dtype=jnp.int32)
+    first_point = device_place * point_count
+    own_speed = lax.dynamic_slice_in_dim(wind_speed, first_point, point_count)
+    own_heading = lax.dynamic_slice_in_dim(wind_heading, first_point, point_count)
+    own_active = lax.dynamic_slice_in_dim(active, first_point, point_count)
+
+    energy, inverse = statistics(spectra_in, all_comp)
+    spectra = apply_sources(spectra_in, all_comp, energy, inverse, own_speed, own_heading, own_active)
+    field = lax.all_to_all(
+        spectra.reshape(device_count, local_count, LANES), "pts", split_axis=0, concat_axis=0, tiled=True
+    )
+
+    norm_weights = bound_weights / jnp.sum(bound_weights, axis=0, keepdims=True)
+    own_cells = first_point + jnp.arange(point_count, dtype=jnp.int32)
+    cell_weights = jnp.sum(
+        jnp.where(bound_cells[:, None, :] == own_cells[None, :, None], norm_weights[:, None, :], 0.0), axis=0
+    )
+    shares = jnp.einsum(
+        "tifdq,qj->idftj",
+        coarse_spectra.reshape(2, device_count, 2, NDIR, point_count),
+        cell_weights,
+        precision=lax.Precision.HIGHEST,
+    ).reshape(device_count, NDIR, 4 * bound_count)
+    shares = jnp.pad(shares, ((0, 0), (0, 4), (0, 0)))
+    shares = lax.all_to_all(shares, "pts", split_axis=0, concat_axis=0, tiled=True)
+    spread = (bound_points[:, None] == jnp.arange(grid_points, dtype=jnp.int32)[None, :]).astype(f32)
+    select = jnp.einsum("ab,jp->abjp", jnp.eye(4, dtype=f32), spread).reshape(4, 4 * bound_count, blocks, LANES)
+    select = select.transpose(0, 2, 1, 3)
+    start, slope = pl.pallas_call(
+        boundary_kernel,
+        out_shape=[jax.ShapeDtypeStruct((blocks, local_count, LANES), f32)] * 2,
+        in_specs=in_vmem(2),
+        out_specs=in_vmem(2),
+        compiler_params=params(),
+    )(shares, select)
+
+    free = active * (1.0 - jnp.sum(spread, axis=0))
+    per_point = jnp.stack([wind_speed, wind_heading, active, free]).reshape(4, blocks, LANES).transpose(1, 0, 2)
+    edges = jnp.stack([edge_x, edge_y], axis=1).reshape(edge_count, 2, blocks, LANES).transpose(0, 2, 1, 3)
+    rows = row_tables(device_place)
+    keep, base, growth = pl.pallas_call(
+        setup_kernel,
+        out_shape=[
+            jax.ShapeDtypeStruct((blocks, local_count, LANES), f32),
+            jax.ShapeDtypeStruct((blocks, edge_count, 40, LANES), f32),
+            jax.ShapeDtypeStruct((blocks, local_count, LANES), f32),
+        ],
+        in_specs=in_vmem(4),
+        out_specs=in_vmem(3),
+        compiler_params=params(),
+    )(per_point, edges, rows, direction_tables())
+
+    index = neighbours.reshape(edge_count, blocks, 1, LANES).transpose(1, 0, 2, 3)
+    index = jnp.broadcast_to(index, (blocks, edge_count, GROUP_ROWS, LANES))
+
+    def fine(first, state, moments):
+        state_shape = jax.ShapeDtypeStruct((blocks, local_count, LANES), f32)
+        out_shape = [state_shape]
+        if first:
+            out_shape.append(jax.ShapeDtypeStruct((blocks, 2, LANES), f32))
+        return pl.pallas_call(
+            functools.partial(fine_kernel, first),
+            out_shape=out_shape,
+            in_specs=in_vmem(9),
+            out_specs=in_vmem(len(out_shape)),
+            scratch_shapes=[
+                pltpu.VMEM((2, blocks, local_count, LANES), f32),
+                pltpu.VMEM((blocks // 2, local_count, LANES), jnp.int32),
+                pltpu.VMEM((local_count, LANES), f32),
+            ],
+            compiler_params=params(),
+        )(state, moments, index, keep, base, growth, start, slope, rows)
+
+    field, sums = fine(True, field, jnp.zeros((2 * blocks, LANES), f32))
+    sums = sums.reshape(2 * blocks, LANES)
+    distance = 1
+    while distance < device_count:
+        pairs = [(place, place ^ distance) for place in range(device_count)]
+        sums = sums + lax.ppermute(sums, "pts", pairs)
+        distance *= 2
+    (field,) = fine(False, field, sums)
+    field = lax.all_to_all(field, "pts", split_axis=0, concat_axis=0, tiled=True)
+    return field.reshape(comp_total, point_count)
+
+
 def shards(
     spectra_in,
     coarse_spectra,
@@ -110,6 +476,28 @@
     comp_total = spectra_in.shape[0]
     local_count = comp_total // device_count
     active = sea_mask.astype(jnp.float32)
+    blocks = neighbours.shape[1] // LANES
+    if (
+        local_count == 2 * NDIR
+        and point_count == LANES
+        and 4 * bound_points.shape[0] == LANES
+        and coarse_spectra.shape[2] == LANES
+        and blocks == device_count
+        and blocks & (blocks - 1) == 0
+    ):
+        return whole_frequencies(
+            spectra_in,
+            coarse_spectra,
+            wind_speed,
+            wind_heading,
+            active,
+            neighbours,
+            edge_x,
+            edge_y,
+            bound_points,
+            bound_cells,
+            bound_weights,
+        )
     all_comp = jnp.arange(comp_total, dtype=jnp.int32)
     my_comp = device_place * local_count + jnp.arange(local_count, dtype=jnp.int32)
     first_point = device_place * point_count

time: 531 us -> 184 us (0.35)
  local copies, waits for them, and re-layouts: 379 us -> 17.9 us
  Pallas kernels: 0 us -> 94.3 us
  other arithmetic: 68.2 us -> 11.4 us
  blocking collectives: 41.6 us -> 23.2 us
  waiting for transfers between devices: 21.9 us -> 12.5 us
    gather x49 -> x0, local copies, waits for them, and re-layouts: 365 us -> none  [the longest x40 302 us: advect(): upwind = upwind + inflow[edge] * spectra[:, neighbours[edge]]]
    pallas_call x0 -> x4, Pallas kernels: none -> 94.3 us  [the longest x2 81.2 us: fine(): pl.pallas_call(functools.partial(fine_kernel, first), out_shape=out_shape...]
    mul x8 -> x1, other arithmetic: 39.6 us -> 0.01 us  [whole_frequencies(): free = active * (1.0 - jnp.sum(spread, axis=0))]
    all_to_all x2 -> x1, blocking collectives: 41.6 us -> 23.2 us  [whole_frequencies(): lax.all_to_all(field, 'pts', split_axis=0, concat_axis=0, tiled=True)]
    all_to_all x3 -> x2, waiting for transfers between devices: 21.9 us -> 4.96 us  [the longest x1 4.96 us: whole_frequencies(): lax.all_to_all(shares, 'pts', split_axis=0, concat_axis=0, tiled=True)]
    scatter x8 -> x0, other arithmetic: 8.66 us -> none  [advect(): spectra = spectra.at[:, bound_points].set(edge_values)]
    ppermute x0 -> x4, waiting for transfers between devices: none -> 7.57 us  [whole_frequencies(): sums = sums + lax.ppermute(sums, 'pts', pairs)]
    all_to_all x3 -> x2, starting transfers between devices: 18 us -> 11.2 us  [the longest x1 7.39 us: whole_frequencies(): lax.all_to_all(shares, 'pts', split_axis=0, concat_axis=0, tiled=True)]
  transfers between devices with their start and end apart: 3 -> 6, of which waited for: 2 -> 5; matrix products, arithmetic and copies ran while one was open for 12% -> 9% of each run, Pallas kernels for 0% -> 7%
where the time goes in v1:
time: 184 us; the launch traced here: 183 us
  Pallas kernels  94.3 us (51%)
  blocking collectives  23.2 us (13%)
  local copies, waits for them, and re-layouts  17.9 us (10%)
  starting transfers between devices  17.1 us (9%)
  waiting for transfers between devices  12.5 us (7%)
  other arithmetic  11.4 us (6%)
  matrix products  5.01 us (3%)
    pallas_call x2, Pallas kernels, fine(): pl.pallas_call(functools.partial(fine_kernel, first), out_shape=out_shape...  81.2 us
    all_to_all x1, blocking collectives, whole_frequencies(): lax.all_to_all(field, 'pts', split_axis=0, concat_axis=0, tiled=True)  23.2 us
    pallas_call x1, Pallas kernels, whole_frequencies(): pl.pallas_call(boundary_kernel, out_shape=[jax.ShapeDtypeStruct((blocks,...  8.91 us
    unnamed x29, local copies, waits for them, and re-layouts  8.75 us
    ppermute x4, waiting for transfers between devices, whole_frequencies(): sums = sums + lax.ppermute(sums, 'pts', pairs)  7.57 us
    all_to_all x1, starting transfers between devices, whole_frequencies(): lax.all_to_all(shares, 'pts', split_axis=0, concat_axis=0, tiled=True)  7.39 us
    ppermute x4, starting transfers between devices, whole_frequencies(): sums = sums + lax.ppermute(sums, 'pts', pairs)  5.94 us
    dot_general x1, matrix products, whole_frequencies(): jnp.einsum('tifdq,qj->idftj', coarse_spectra.reshape(2, device_count, 2,...  5.01 us
  transfers between devices with their start and end apart: 6, of which 5 were waited for; matrix products, arithmetic and copies ran while one was open for 9% of the time, Pallas kernels for 7%

profile of v1, /device:TPU:0, one launch (start us, length us, event | category | flops | bytes accessed | tf_op | source)
XLA Modules:
  0.0 183.0 jit_solution(13997773940885197040)
XLA Ops:
  1.4 4.7 %copy.23 = f32[2,1152,128]{2,0,1:T(2,128)S(1)} copy(f32[2,1152,128]{2,1,0:T(8,128)} %param.14) | data formatting | bytes 2359296 | tf_op args[1]
  6.3 5.0 %convolution_bitcast_fusion = f32[16,36,2,2,32]{1,4,2,0,3:T(8,128)S(1)} fusion(f32[2,16,2,36,128]{4,0,3,2,1:T(2,128)S(1)} %bitcast.47, f32[128,32]{0,1:T(8,128)S(1)} %select_reduce_fusion), kind=kOutput, calls=%fused_computation.2 | convolution fusion | flops 113246208 | bytes 1490944 | tf_op jit(solution)/shard_map/tifdq,qj->idftj/dot_general | solution.py:392
  11.3 0.9 copy.29
  12.2 0.9 reshape.110
  13.9 7.4 %all-to-all-start.1 = ((f32[16,40,128]{2,1,0:T(8,128)}), f32[16,40,128]{2,1,0:T(8,128)S(1)}, u32[]{:S(2)}, u32[]{:S(2)}) async-start(f32[16,40,128]{2,1,0:T(8,128)} %pad.4), calls=%async_computation.1 | async-start | bytes 655360 | tf_op jit(solution)/shard_map/all_to_all | solution.py:399
  24.1 3.4 %multiply_multiply_fusion = f32[1152,128]{1,0:T(8,128)} fusion(f32[1152,128]{1,0:T(8,128)S(1)} %copy-done, f32[128]{0:T(128)S(1)} %dynamic_slice.11, f32[128]{0:T(128)S(1)} %fusion.17, f32[1152]{0:T(1024)S(1)} %get-tuple-element.31, f32[1152]{0:T(1024)S(1)} %get-tuple-element.32, f32[128]{0:T(128)S(1)} %dynamic_slice.10, f32[1152]{0:T(1024)S(1)} %get-tuple-element.30, ...), kind=kLoop, calls=%fused_computation.4 | loop fusion | flops 1916928 | bytes 1200128 | tf_op jit(solution)/shard_map/mul | solution.py:61
  27.5 5.0 %all-to-all-done.1.bound_ref = f32[16,40,128]{2,1,0:T(8,128)S(1)} async-done(((f32[16,40,128]{2,1,0:T(8,128)}), f32[16,40,128]{2,1,0:T(8,128)S(1)}, u32[]{:S(2)}, u32[]{:S(2)}) %all-to-all-start.1) | async-done | bytes 327712 | tf_op jit(solution)/shard_map/all_to_all | solution.py:399
  32.4 3.8 %all-to-all-start = ((f32[16,72,128]{2,1,0:T(8,128)}), f32[16,72,128]{2,1,0:T(8,128)S(1)}, u32[]{:S(2)}, u32[]{:S(2)}) async-start(f32[16,72,128]{2,1,0:T(8,128)} %bitcast), calls=%async_computation | async-start | bytes 1179648 | tf_op jit(solution)/shard_map/all_to_all | solution.py:383
  36.2 2.5 %broadcast_multiply_fusion = f32[4,4,32,2048]{3,2,1,0:T(8,128)} fusion(f32[32,2048]{1,0:T(8,128)S(1)} %fusion.1, f32[4,4]{1,0:T(4,128)S(1)} %fusion.16), kind=kLoop, calls=%fused_computation.1 | loop fusion | flops 1048576 | bytes 4456512 | tf_op jit(solution)/shard_map/ab,jp->abjp/dot_general | solution.py:401
  38.9 3.1 %copy.31 = f32[64,8,16,128]{3,2,1,0:T(8,128)S(1)} copy(f32[64,8,16,128]{3,1,2,0:T(8,128)} %bitcast.45) | data formatting | bytes 8388608
  42.0 3.2 %copy.35 = f32[4,128,16,128]{3,1,2,0:T(8,128)} copy(f32[4,128,16,128]{3,2,1,0:T(8,128)S(1)} %bitcast.46) | data formatting | bytes 8388608 | tf_op jit(solution)/shard_map/reshape | solution.py:401
  46.8 0.8 broadcast_in_dim.23.rows_ref
  48.4 4.2 %shard_map.127 = (f32[16,72,128]{2,1,0:T(8,128)}, f32[16,6,40,128]{3,2,1,0:T(8,128)}, f32[16,72,128]{2,1,0:T(8,128)}) custom-call(f32[16,4,128]{2,1,0:T(4,128)} %maximum_bitcast_fusion.1.points_ref, f32[6,16,2,128]{3,2,1,0:T(2,128)} %maximum_bitcast_fusion.edge_ref, f32[6,72,128]{2,1,0:T(8,128)} %broadcast_in_dim.23.rows_ref, ...), custom_call_target="tpu_custom_call" | custom-call | tf_op jit(solution)/shard_map/pallas_call | solution.py:415
  52.6 8.9 %shard_map.128 = (f32[16,72,128]{2,1,0:T(8,128)}, f32[16,72,128]{2,1,0:T(8,128)}) custom-call(f32[16,40,128]{2,1,0:T(8,128)} %copy-done.2, f32[4,16,128,128]{3,2,1,0:T(8,128)} %bitcast.44), custom_call_target="tpu_custom_call" | custom-call | tf_op jit(solution)/shard_map/pallas_call | solution.py:403
  62.9 40.7 %shard_map.129 = (f32[16,72,128]{2,1,0:T(8,128)}, f32[16,2,128]{2,1,0:T(2,128)}) custom-call(f32[16,72,128]{2,1,0:T(8,128)} %copy-done.1, f32[32,128]{1,0:T(8,128)} %broadcast_in_dim.16.moments_ref, s32[16,6,8,128]{3,2,1,0:T(8,128)} %broadcast_in_dim.18.index_ref, f32[16,72,128]{2,1,0:T(8,128)} %get-tuple-element.12.keep_ref, ...), custom_call_target="tpu_custom_call" | custom-call | tf_op jit(solution)/shard_map/pallas_call | solution.py:435
  103.7 1.3 collective-permute-done
  105.8 1.6 collective-permute-start.1
  107.4 2.1 %collective-permute-done.1 = f32[32,128]{1,0:T(8,128)S(1)} collective-permute-done((f32[32,128]{1,0:T(8,128)S(1)}, f32[32,128]{1,0:T(8,128)S(1)}, u32[]{:S(2)}, u32[]{:S(2)}) %collective-permute-start.1) | collective-permute-done | bytes 16416 | tf_op jit(solution)/shard_map/ppermute | solution.py:453
  109.5 1.6 collective-permute-start.2
  111.1 2.1 %collective-permute-done.2 = f32[32,128]{1,0:T(8,128)S(1)} collective-permute-done((f32[32,128]{1,0:T(8,128)S(1)}, f32[32,128]{1,0:T(8,128)S(1)}, u32[]{:S(2)}, u32[]{:S(2)}) %collective-permute-start.2) | collective-permute-done | bytes 16416 | tf_op jit(solution)/shard_map/ppermute | solution.py:453
  113.2 2.6 %collective-permute-start.3 = (f32[32,128]{1,0:T(8,128)S(1)}, f32[32,128]{1,0:T(8,128)S(1)}, u32[]{:S(2)}, u32[]{:S(2)}) collective-permute-start(f32[32,128]{1,0:T(8,128)S(1)} %add.104), channel_id=1, source_target_pairs={{0,8},{1,9},{2,10},{3,11},{4,12},{5,13},{6,14},{7,15},{8,0},{9,1},... | collective-permute-start | bytes 49160 | tf_op jit(solution)/shard_map/ppermute | solution.py:453
  115.8 2.1 %collective-permute-done.3 = f32[32,128]{1,0:T(8,128)S(1)} collective-permute-done((f32[32,128]{1,0:T(8,128)S(1)}, f32[32,128]{1,0:T(8,128)S(1)}, u32[]{:S(2)}, u32[]{:S(2)}) %collective-permute-start.3) | collective-permute-done | bytes 16416 | tf_op jit(solution)/shard_map/ppermute | solution.py:453
  118.5 40.5 %shard_map.130 = f32[16,72,128]{2,1,0:T(8,128)} custom-call(f32[16,72,128]{2,1,0:T(8,128)} %get-tuple-element.17.state_ref, f32[32,128]{1,0:T(8,128)} %add.105.moments_ref, s32[16,6,8,128]{3,2,1,0:T(8,128)} %broadcast_in_dim.18.index_ref, f32[16,72,128]{2,1,0:T(8,128)} %get-tuple-element.12.keep_ref, f32[16,6,40,128]{3,2,1,0:T(8,128)} %get-tuple-element.13.base_ref, ...), custom_call_target="tpu_custom_call" | custom-call | tf_op jit(solution)/shard_map/pallas_call | solution.py:435
  159.0 23.2 %all_to_all.15 = f32[16,72,128]{2,1,0:T(8,128)S(1)} all-to-all(f32[16,72,128]{2,1,0:T(8,128)} %shard_map.130), channel_id=1, replica_groups=mesh['groups'=2,'pts'=16] {'pts'}, dimensions={0} | all-to-all | bytes 1179648 | tf_op jit(solution)/shard_map/all_to_all | solution.py:456
  (62 shorter events, 9.8 us)
Async XLA Ops:
  0.0 6.2 %copy-start.10 = (s32[4,32]{1,0:T(4,128)S(1)}, s32[4,32]{1,0:T(4,128)}, u32[]{:S(2)}) copy-start(s32[4,32]{1,0:T(4,128)} %param.22) | copy-start | bytes 1540
  12.2 11.1 %copy-start.6 = (s32[2048]{0:T(1024)S(1)}, s32[2048]{0:T(1024)}, u32[]{:S(2)}) copy-start(s32[2048]{0:T(1024)} %param.17) | copy-start | bytes 24580
  12.2 11.2 %copy-start.7 = (f32[2048]{0:T(1024)S(1)}, f32[2048]{0:T(1024)}, u32[]{:S(2)}) copy-start(f32[2048]{0:T(1024)} %param.16) | copy-start | bytes 24580
  12.2 11.2 %copy-start.8 = (f32[2048]{0:T(1024)S(1)}, f32[2048]{0:T(1024)}, u32[]{:S(2)}) copy-start(f32[2048]{0:T(1024)} %param.15) | copy-start | bytes 24580
  12.2 11.3 %copy-start.9 = (s32[32]{0:T(128)S(1)}, s32[32]{0:T(128)}, u32[]{:S(2)}) copy-start(s32[32]{0:T(128)} %param.21) | copy-start | bytes 388
  12.2 11.4 %copy-start = (f32[1152,128]{1,0:T(8,128)S(1)}, f32[1152,128]{1,0:T(8,128)}, u32[]{:S(2)}) copy-start(f32[1152,128]{1,0:T(8,128)} %param.13) | copy-start | bytes 1769476
  13.9 18.5 %all-to-all-start.1 = ((f32[16,40,128]{2,1,0:T(8,128)}), f32[16,40,128]{2,1,0:T(8,128)S(1)}, u32[]{:S(2)}, u32[]{:S(2)}) async-start(f32[16,40,128]{2,1,0:T(8,128)} %pad.4), calls=%async_computation.1 | async-start | bytes 655360 | tf_op jit(solution)/shard_map/all_to_all | solution.py:399
  32.4 6.3 %copy-start.2 = (f32[16,40,128]{2,1,0:T(8,128)}, f32[16,40,128]{2,1,0:T(8,128)S(1)}, u32[]{:S(2)}) copy-start(f32[16,40,128]{2,1,0:T(8,128)S(1)} %all-to-all-done.1.bound_ref) | copy-start | bytes 983044
  32.4 29.1 %all-to-all-start = ((f32[16,72,128]{2,1,0:T(8,128)}), f32[16,72,128]{2,1,0:T(8,128)S(1)}, u32[]{:S(2)}, u32[]{:S(2)}) async-start(f32[16,72,128]{2,1,0:T(8,128)} %bitcast), calls=%async_computation | async-start | bytes 1179648 | tf_op jit(solution)/shard_map/all_to_all | solution.py:383
  36.2 2.5 %copy-start.4 = (f32[6,2048]{1,0:T(8,128)S(1)}, f32[6,2048]{1,0:T(8,128)}, u32[]{:S(2)}) copy-start(f32[6,2048]{1,0:T(8,128)} %param.19) | copy-start | bytes 147460
  36.2 2.6 %copy-start.5 = (f32[6,2048]{1,0:T(8,128)S(1)}, f32[6,2048]{1,0:T(8,128)}, u32[]{:S(2)}) copy-start(f32[6,2048]{1,0:T(8,128)} %param.20) | copy-start | bytes 147460
  42.0 3.3 %copy-start.12 = (s32[72]{0:T(128)S(1)}, s32[72]{0:T(128)}, u32[]{:S(2)}) copy-start(s32[72]{0:T(128)} %constant.92.clone) | copy-start | bytes 868
  42.0 5.7 %copy-start.11 = (f32[2,72]{1,0:T(2,128)S(1)}, f32[2,72]{1,0:T(2,128)}, u32[]{:S(2)}) copy-start(f32[2,72]{1,0:T(2,128)} %constant.93.clone) | copy-start | bytes 1732
  52.6 8.9 %copy-start.3 = (s32[6,2048]{1,0:T(8,128)S(1)}, s32[6,2048]{1,0:T(8,128)}, u32[]{:S(2)}) copy-start(s32[6,2048]{1,0:T(8,128)} %param.18) | copy-start | bytes 147460
  61.5 1.4 copy-start.1
  103.6 1.4 collective-permute-start
  105.8 3.7 %collective-permute-start.1 = (f32[32,128]{1,0:T(8,128)S(1)}, f32[32,128]{1,0:T(8,128)S(1)}, u32[]{:S(2)}, u32[]{:S(2)}) collective-permute-start(f32[32,128]{1,0:T(8,128)S(1)} %add.102), channel_id=1, source_target_pairs={{0,2},{1,3},{2,0},{3,1},{4,6},{5,7},{6,4},{7,5},{8,10},{9,11},{10,... | collective-permute-start | bytes 49160 | tf_op jit(solution)/shard_map/ppermute | solution.py:453
  109.5 3.7 %collective-permute-start.2 = (f32[32,128]{1,0:T(8,128)S(1)}, f32[32,128]{1,0:T(8,128)S(1)}, u32[]{:S(2)}, u32[]{:S(2)}) collective-permute-start(f32[32,128]{1,0:T(8,128)S(1)} %add.103), channel_id=1, source_target_pairs={{0,4},{1,5},{2,6},{3,7},{4,0},{5,1},{6,2},{7,3},{8,12},{9,13},{10,... | collective-permute-start | bytes 49160 | tf_op jit(solution)/shard_map/ppermute | solution.py:453
  113.2 4.6 %collective-permute-start.3 = (f32[32,128]{1,0:T(8,128)S(1)}, f32[32,128]{1,0:T(8,128)S(1)}, u32[]{:S(2)}, u32[]{:S(2)}) collective-permute-start(f32[32,128]{1,0:T(8,128)S(1)} %add.104), channel_id=1, source_target_pairs={{0,8},{1,9},{2,10},{3,11},{4,12},{5,13},{6,14},{7,15},{8,0},{9,1},... | collective-permute-start | bytes 49160 | tf_op jit(solution)/shard_map/ppermute | solution.py:453

commit v2 on v1

--- a/solution.py
+++ b/solution.py
@@ -186,35 +186,73 @@
     lax.fori_loop(0, keep_ref.shape[0], block, 0)
 
 
-def boundary_kernel(bound_ref, select_ref, start_ref, slope_ref):
-    total = bound_ref[0]
-    for source in range(1, bound_ref.shape[0]):
-        total = total + bound_ref[source]
-    sub = lax.broadcasted_iota(jnp.int32, (GROUP_ROWS, LANES), 0)
-
-    def block(place, _):
-        pieces = []
-        for piece in range(4):
-            pieces.append(
-                jnp.dot(
-                    total,
-                    select_ref[piece, place],
-                    preferred_element_type=jnp.float32,
-                    precision=lax.Precision.HIGHEST,
-                )
-            )
-        for out_ref, values in (
-            (start_ref, (pieces[0], pieces[2])),
-            (slope_ref, (pieces[1] - pieces[0], pieces[3] - pieces[2])),
-        ):
-            for half in range(2):
-                for group in range(4):
-                    out_ref[place, group_rows(4 * half + group), :] = values[half][8 * group : 8 * group + 8]
-            out_ref[place, pl.ds(64, 4), :] = values[0][32:36]
-            out_ref[place, pl.ds(68, 4), :] = values[1][32:36]
-        return 0
-
-    lax.fori_loop(0, start_ref.shape[0], block, 0)
+def frequency(place):
+    return 0.25 * 1.1**place
+
+
+FREQ_TOP = frequency(NFREQ - 1)
+FREQ_TOTAL = NDIR * sum(frequency(place) for place in range(NFREQ))
+
+
+def dissipation_rate(energy, inverse):
+    mean_freq = energy / (inverse + epsilon)
+    steepness = energy * (0.5 * mean_freq) * (0.5 * mean_freq)
+    return inverse / (energy + epsilon) * (steepness / (1.0 + steepness))
+
+
+def split_bf16(values):
+    high = values.astype(jnp.bfloat16).astype(jnp.float32)
+    return high, values - high
+
+
+def pack_kernel(first_ref, spectra_ref, coarse_ref, cells_ref, weights_ref, send_ref, shares):
+    destinations = send_ref.shape[0]
+    f32 = jnp.float32
+    lane = lax.broadcasted_iota(jnp.int32, (LANES, LANES), 1)
+    cell = lax.broadcasted_iota(jnp.int32, (LANES, LANES), 0) + first_ref[0]
+    norm = weights_ref[...] / jnp.sum(weights_ref[...], axis=0, keepdims=True)
+    table = jnp.zeros((LANES, LANES), f32)
+    for corner in range(cells_ref.shape[0]):
+        hit = jnp.broadcast_to(cells_ref[corner : corner + 1, :], (LANES, LANES)) == cell
+        table = table + jnp.where(hit, jnp.broadcast_to(norm[corner : corner + 1, :], (LANES, LANES)), 0.0)
+    later = (lane & 32) != 0
+    bf16 = jnp.bfloat16
+    parts = [split_bf16(jnp.where(later, 0.0, table)), split_bf16(jnp.where(later, table, 0.0))]
+    parts = [(high.astype(bf16), low.astype(bf16)) for high, low in parts]
+    chunk = 8 * NDIR
+
+    for start in range(0, spectra_ref.shape[0], chunk):
+        result = None
+        for time in range(2):
+            high, low = split_bf16(coarse_ref[time, pl.ds(start, chunk), :])
+            high, low = high.astype(bf16), low.astype(bf16)
+            weight_high, weight_low = parts[time]
+            for left, right in ((high, weight_high), (low, weight_high), (high, weight_low)):
+                term = jnp.dot(left, right, preferred_element_type=f32)
+                result = term if result is None else result + term
+        shares[pl.ds(start, chunk), :] = result
+
+    sub = lax.broadcasted_iota(jnp.int32, (GROUP_ROWS, LANES), 0) < 4
+    energy = jnp.zeros((GROUP_ROWS, LANES), f32)
+    inverse = jnp.zeros((GROUP_ROWS, LANES), f32)
+    lower_lanes = lax.broadcasted_iota(jnp.int32, (NDIR, LANES), 1) < 64
+    for place in range(destinations):
+        start = 2 * NDIR * place
+        values = [spectra_ref[pl.ds(start + GROUP_ROWS * group, GROUP_ROWS), :] for group in range(GROUPS)]
+        for group in range(GROUPS):
+            send_ref[place, group_rows(group), :] = values[group]
+        lower = values[0] + values[1] + values[2] + values[3] + jnp.where(sub, values[4], 0.0)
+        upper = values[5] + values[6] + values[7] + values[8] + jnp.where(sub, 0.0, values[4])
+        energy = energy + frequency(2 * place) * lower + frequency(2 * place + 1) * upper
+        inverse = inverse + (lower + upper)
+        send_ref[place, pl.ds(2 * NDIR, NDIR), :] = jnp.where(
+            lower_lanes, shares[pl.ds(start, NDIR), :], shares[pl.ds(start + NDIR, NDIR), :]
+        )
+    energy = jnp.sum(energy, axis=0, keepdims=True) * (1.0 / FREQ_TOTAL)
+    inverse = jnp.sum(inverse, axis=0, keepdims=True) * (1.0 / FREQ_TOTAL)
+    rate = jnp.broadcast_to(dissipation_rate(energy, inverse), (4, LANES))
+    for place in range(destinations):
+        send_ref[place, pl.ds(3 * NDIR, 4), :] = rate
 
 
 def take_lanes(values, lanes):
@@ -224,55 +262,63 @@
 def fine_kernel(
     first,
     state_ref,
-    moments_ref,
+    extra_ref,
     index_ref,
     keep_ref,
     base_ref,
     growth_ref,
-    start_ref,
-    slope_ref,
     rows_ref,
-    out_ref,
     *rest,
 ):
     if first:
-        sums_ref, field, words, speed = rest
+        out_ref, sums_ref, start_ref, slope_ref, field, words, speed = rest
     else:
-        field, words, speed = rest
+        start_ref, slope_ref, out_ref, field, words, speed = rest
     blocks = keep_ref.shape[0]
     half = blocks // 2
     edge_count = base_ref.shape[1]
     first_step = 0 if first else SUB
 
     if first:
-
-        def enter(place, _):
-            for group, value in enumerate(load_natural(state_ref, place)):
-                field[0, place, group_rows(group), :] = value
-            return 0
-
-    else:
-
-        def enter(place, _):
-            energy = jnp.broadcast_to(moments_ref[2 * place : 2 * place + 1, :], (GROUP_ROWS, LANES))
-            inverse = jnp.broadcast_to(moments_ref[2 * place + 1 : 2 * place + 2, :], (GROUP_ROWS, LANES))
-            mean_freq = energy / (inverse + epsilon)
-            steepness = energy * (0.5 * mean_freq) * (0.5 * mean_freq)
-            loss = inverse / (energy + epsilon) * (steepness / (1.0 + steepness))
-            lower = jnp.exp(-rows_ref[2, group_rows(0), :] * loss)
-            upper = jnp.exp(-rows_ref[2, group_rows(4), :] * loss)
-            last = jnp.exp(-rows_ref[2, group_rows(8), :] * loss)
-            decay = [lower] * 4 + [upper] * 4 + [last]
-            for group in range(GROUPS):
-                rows = group_rows(group)
-                field[0, place, rows, :] = state_ref[place, rows, :] * growth_ref[place, rows, :] * decay[group]
-            return 0
-
-    if first:
-        lax.fori_loop(0, blocks, enter, 0)
-    else:
-        for place in range(blocks):
-            enter(place, 0)
+        total = state_ref[0, pl.ds(2 * NDIR, 40), :]
+        for source in range(1, blocks):
+            total = total + state_ref[source, pl.ds(2 * NDIR, 40), :]
+        rolled = [total] + [pltpu.roll(total, LANES - 32 * piece, 1) for piece in range(1, 4)]
+        high, low = split_bf16(jnp.concatenate(rolled, axis=0))
+        bound = jnp.concatenate([high, low], axis=0).astype(jnp.bfloat16)
+
+    def spread(place):
+        values = jnp.dot(bound, extra_ref[place], preferred_element_type=jnp.float32)
+        values = values[0:160] + values[160:320]
+        pieces = [values[40 * piece : 40 * piece + 40] for piece in range(4)]
+        for out, pair in (
+            (start_ref, (pieces[0], pieces[2])),
+            (slope_ref, (pieces[1] - pieces[0], pieces[3] - pieces[2])),
+        ):
+            for side in range(2):
+                for group in range(4):
+                    out[place, group_rows(4 * side + group), :] = pair[side][8 * group : 8 * group + 8]
+            out[place, pl.ds(64, 4), :] = pair[0][32:36]
+            out[place, pl.ds(68, 4), :] = pair[1][32:36]
+
+    def enter(place, _):
+        if first:
+            loss = jnp.broadcast_to(state_ref[place, pl.ds(3 * NDIR, 1), :], (GROUP_ROWS, LANES))
+            values = load_natural(state_ref, place)
+            spread(place)
+        else:
+            energy = jnp.broadcast_to(extra_ref[place, 0:1, :], (GROUP_ROWS, LANES))
+            inverse = jnp.broadcast_to(extra_ref[place, 1:2, :], (GROUP_ROWS, LANES))
+            loss = dissipation_rate(energy, inverse)
+            values = [state_ref[place, group_rows(group), :] for group in range(GROUPS)]
+        lower, upper, last = [jnp.exp(-rows_ref[2, group_rows(group), :] * loss) for group in (0, 4, 8)]
+        decay = [lower] * 4 + [upper] * 4 + [last]
+        for group in range(GROUPS):
+            rows = group_rows(group)
+            field[0, place, rows, :] = values[group] * growth_ref[place, rows, :] * decay[group]
+        return 0
+
+    lax.fori_loop(0, blocks, enter, 0)
 
     def fine_step(number, _):
         source = lax.rem(number, 2)
@@ -372,43 +418,21 @@
     blocks = grid_points // LANES
     bound_count = bound_points.shape[0]
     f32 = jnp.float32
-    all_comp = jnp.arange(comp_total, dtype=jnp.int32)
-    first_point = device_place * point_count
-    own_speed = lax.dynamic_slice_in_dim(wind_speed, first_point, point_count)
-    own_heading = lax.dynamic_slice_in_dim(wind_heading, first_point, point_count)
-    own_active = lax.dynamic_slice_in_dim(active, first_point, point_count)
-
-    energy, inverse = statistics(spectra_in, all_comp)
-    spectra = apply_sources(spectra_in, all_comp, energy, inverse, own_speed, own_heading, own_active)
-    field = lax.all_to_all(
-        spectra.reshape(device_count, local_count, LANES), "pts", split_axis=0, concat_axis=0, tiled=True
-    )
-
-    norm_weights = bound_weights / jnp.sum(bound_weights, axis=0, keepdims=True)
-    own_cells = first_point + jnp.arange(point_count, dtype=jnp.int32)
-    cell_weights = jnp.sum(
-        jnp.where(bound_cells[:, None, :] == own_cells[None, :, None], norm_weights[:, None, :], 0.0), axis=0
-    )
-    shares = jnp.einsum(
-        "tifdq,qj->idftj",
-        coarse_spectra.reshape(2, device_count, 2, NDIR, point_count),
-        cell_weights,
-        precision=lax.Precision.HIGHEST,
-    ).reshape(device_count, NDIR, 4 * bound_count)
-    shares = jnp.pad(shares, ((0, 0), (0, 4), (0, 0)))
-    shares = lax.all_to_all(shares, "pts", split_axis=0, concat_axis=0, tiled=True)
-    spread = (bound_points[:, None] == jnp.arange(grid_points, dtype=jnp.int32)[None, :]).astype(f32)
-    select = jnp.einsum("ab,jp->abjp", jnp.eye(4, dtype=f32), spread).reshape(4, 4 * bound_count, blocks, LANES)
-    select = select.transpose(0, 2, 1, 3)
-    start, slope = pl.pallas_call(
-        boundary_kernel,
-        out_shape=[jax.ShapeDtypeStruct((blocks, local_count, LANES), f32)] * 2,
-        in_specs=in_vmem(2),
-        out_specs=in_vmem(2),
+    first_point = (device_place * point_count).astype(jnp.int32).reshape(1)
+    send = pl.pallas_call(
+        pack_kernel,
+        out_shape=jax.ShapeDtypeStruct((device_count, 112, LANES), f32),
+        in_specs=[pl.BlockSpec(memory_space=pltpu.SMEM)] + in_vmem(4),
+        out_specs=pl.BlockSpec(memory_space=pltpu.VMEM),
+        scratch_shapes=[pltpu.VMEM((comp_total, LANES), f32)],
         compiler_params=params(),
-    )(shares, select)
-
-    free = active * (1.0 - jnp.sum(spread, axis=0))
+    )(first_point, spectra_in, coarse_spectra, jnp.tile(bound_cells, (1, 4)), jnp.tile(bound_weights, (1, 4)))
+    received = lax.all_to_all(send, "pts", split_axis=0, concat_axis=0, tiled=True)
+
+    spread = bound_points[:, None] == jnp.arange(grid_points, dtype=jnp.int32)[None, :]
+    select = jnp.pad(spread.astype(jnp.bfloat16), ((0, LANES - bound_count), (0, 0)))
+    select = select.reshape(LANES, blocks, LANES).transpose(1, 0, 2)
+    free = jnp.where(jnp.any(spread, axis=0), 0.0, active)
     per_point = jnp.stack([wind_speed, wind_heading, active, free]).reshape(4, blocks, LANES).transpose(1, 0, 2)
     edges = jnp.stack([edge_x, edge_y], axis=1).reshape(edge_count, 2, blocks, LANES).transpose(0, 2, 1, 3)
     rows = row_tables(device_place)
@@ -422,20 +446,21 @@
         in_specs=in_vmem(4),
         out_specs=in_vmem(3),
         compiler_params=params(),
+        cost_estimate=pl.CostEstimate(flops=100_000_000, bytes_accessed=4_000_000, transcendentals=1_000_000),
     )(per_point, edges, rows, direction_tables())
 
     index = neighbours.reshape(edge_count, blocks, 1, LANES).transpose(1, 0, 2, 3)
     index = jnp.broadcast_to(index, (blocks, edge_count, GROUP_ROWS, LANES))
 
-    def fine(first, state, moments):
+    def fine(first, state, extra, bound):
         state_shape = jax.ShapeDtypeStruct((blocks, local_count, LANES), f32)
         out_shape = [state_shape]
         if first:
-            out_shape.append(jax.ShapeDtypeStruct((blocks, 2, LANES), f32))
+            out_shape += [jax.ShapeDtypeStruct((blocks, 2, LANES), f32), state_shape, state_shape]
         return pl.pallas_call(
             functools.partial(fine_kernel, first),
             out_shape=out_shape,
-            in_specs=in_vmem(9),
+            in_specs=in_vmem(7 + len(bound)),
             out_specs=in_vmem(len(out_shape)),
             scratch_shapes=[
                 pltpu.VMEM((2, blocks, local_count, LANES), f32),
@@ -443,16 +468,15 @@
                 pltpu.VMEM((local_count, LANES), f32),
             ],
             compiler_params=params(),
-        )(state, moments, index, keep, base, growth, start, slope, rows)
-
-    field, sums = fine(True, field, jnp.zeros((2 * blocks, LANES), f32))
-    sums = sums.reshape(2 * blocks, LANES)
+        )(state, extra, index, keep, base, growth, rows, *bound)
+
+    field, sums, start, slope = fine(True, received, select, ())
     distance = 1
     while distance < device_count:
         pairs = [(place, place ^ distance) for place in range(device_count)]
         sums = sums + lax.ppermute(sums, "pts", pairs)
         distance *= 2
-    (field,) = fine(False, field, sums)
+    (field,) = fine(False, field, sums, (start, slope))
     field = lax.all_to_all(field, "pts", split_axis=0, concat_axis=0, tiled=True)
     return field.reshape(comp_total, point_count)
 

time: 184 us -> 160 us (0.87)
  local copies, waits for them, and re-layouts: 17.9 us -> 7.3 us
  other arithmetic: 11.4 us -> 3.89 us
  matrix products: 5.01 us -> 0 us
  waiting for transfers between devices: 12.5 us -> 16.4 us
  Pallas kernels: 94.3 us -> 92 us
    unnamed x29 -> x21, local copies, waits for them, and re-layouts: 8.75 us -> 1.09 us
    pallas_call x1, Pallas kernels: 8.91 us -> 3.07 us  [whole_frequencies(): pl.pallas_call(pack_kernel, out_shape=jax.ShapeDtypeStruct((device_count,...]
    reshape x3 -> x0, local copies, waits for them, and re-layouts: 5.05 us -> none  [the longest x1 3.24 us: whole_frequencies(): jnp.einsum('ab,jp->abjp', jnp.eye(4, dtype=f32), spread)]
    all_to_all x2 -> x1, waiting for transfers between devices: 4.96 us -> 10 us  [whole_frequencies(): lax.all_to_all(send, 'pts', split_axis=0, concat_axis=0, tiled=True)]
    dot_general x1 -> x0, matrix products: 5.01 us -> none  [whole_frequencies(): jnp.einsum('tifdq,qj->idftj', coarse_spectra.reshape(2, device_count, 2,...]
    all_to_all x2 -> x1, starting transfers between devices: 11.2 us -> 7.53 us  [whole_frequencies(): lax.all_to_all(send, 'pts', split_axis=0, concat_axis=0, tiled=True)]
    pallas_call x2, Pallas kernels: 81.2 us -> 84.8 us  [fine(): pl.pallas_call(functools.partial(fine_kernel, first), out_shape=out_shape...]
    mul x5 -> x0, other arithmetic: 3.44 us -> none  [the longest x1 3.39 us: apply_sources(): return spectra * jnp.exp(wind_in - dissipation) * active[None, :]]
  transfers between devices with their start and end apart: 6 -> 5, of which waited for: 5 -> 5; matrix products, arithmetic and copies ran while one was open for 9% -> 3% of each run, Pallas kernels for 7% -> 3%
where the time goes in v2:
time: 160 us; the launch traced here: 159 us
  Pallas kernels  92 us (58%)
  blocking collectives  22.1 us (14%)
  waiting for transfers between devices  16.4 us (10%)
  starting transfers between devices  16.3 us (10%)
  local copies, waits for them, and re-layouts  7.3 us (5%)
  other arithmetic  3.89 us (2%)
    pallas_call x2, Pallas kernels, fine(): pl.pallas_call(functools.partial(fine_kernel, first), out_shape=out_shape...  84.8 us
    all_to_all x1, blocking collectives, whole_frequencies(): lax.all_to_all(field, 'pts', split_axis=0, concat_axis=0, tiled=True)  22.1 us
    all_to_all x1, waiting for transfers between devices, whole_frequencies(): lax.all_to_all(send, 'pts', split_axis=0, concat_axis=0, tiled=True)  10 us
    ppermute x4, starting transfers between devices, whole_frequencies(): sums = sums + lax.ppermute(sums, 'pts', pairs)  8.73 us
    all_to_all x1, starting transfers between devices, whole_frequencies(): lax.all_to_all(send, 'pts', split_axis=0, concat_axis=0, tiled=True)  7.53 us
    ppermute x4, waiting for transfers between devices, whole_frequencies(): sums = sums + lax.ppermute(sums, 'pts', pairs)  6.43 us
    pallas_call x1, Pallas kernels, whole_frequencies(): pl.pallas_call(setup_kernel, out_shape=[jax.ShapeDtypeStruct((blocks, loc...  4.16 us
  transfers between devices with their start and end apart: 5, of which 5 were waited for; matrix products, arithmetic and copies ran while one was open for 3% of the time, Pallas kernels for 3%

profile of v2, /device:TPU:0, one launch (start us, length us, event | category | flops | bytes accessed | tf_op | source)
XLA Modules:
  0.0 159.4 jit_solution(1226293102098376730)
XLA Ops:
  0.0 0.7 tile.8
  0.7 0.7 tile.9.cells_ref
  1.3 0.7 tile.20
  2.7 3.1 %shard_map.127 = f32[16,112,128]{2,1,0:T(8,128)} custom-call(s32[1]{0:T(128)} %bitcast.first_ref, f32[1152,128]{1,0:T(8,128)} %spectra_ref.1, f32[2,1152,128]{2,1,0:T(8,128)} %coarse_ref.1, s32[4,128]{1,0:T(4,128)} %tile.9.cells_ref, f32[4,128]{1,0:T(4,128)} %tile.21.weights_ref), custom_call_target="tpu_custom_call" | custom-call | tf_op jit(solution)/shard_map/pallas_call | solution.py:422
  5.8 7.5 %all-to-all-start = ((f32[16,112,128]{2,1,0:T(8,128)}), f32[16,112,128]{2,1,0:T(8,128)S(1)}, u32[]{:S(2)}, u32[]{:S(2)}) async-start(f32[16,112,128]{2,1,0:T(8,128)} %shard_map.127), calls=%async_computation | async-start | bytes 1835008 | tf_op jit(solution)/shard_map/all_to_all | solution.py:430
  15.9 1.0 copy.15
  17.7 0.7 maximum_bitcast_fusion.edge_ref
  18.5 0.8 broadcast_in_dim.22.rows_ref
  19.3 0.7 jit_solution_.3.dirs_ref
  20.0 4.2 %shard_map.128 = (f32[16,72,128]{2,1,0:T(8,128)}, f32[16,6,40,128]{3,2,1,0:T(8,128)}, f32[16,72,128]{2,1,0:T(8,128)}) custom-call(f32[16,4,128]{2,1,0:T(4,128)} %maximum_bitcast_fusion.1.points_ref, f32[6,16,2,128]{3,2,1,0:T(2,128)} %maximum_bitcast_fusion.edge_ref, f32[6,72,128]{2,1,0:T(8,128)} %broadcast_in_dim.22.rows_ref, ...), custom_call_target="tpu_custom_call" | custom-call | flops 100000000 | bytes 4000000 | tf_op jit(solution)/shard_map/pallas_call | solution.py:439
  24.1 10.0 %all-to-all-done.state_ref = f32[16,112,128]{2,1,0:T(8,128)S(1)} async-done(((f32[16,112,128]{2,1,0:T(8,128)}), f32[16,112,128]{2,1,0:T(8,128)S(1)}, u32[]{:S(2)}, u32[]{:S(2)}) %all-to-all-start) | async-done | bytes 917536 | tf_op jit(solution)/shard_map/all_to_all | solution.py:430
  34.1 0.8 broadcast_in_dim.20.index_ref
  35.2 43.8 %shard_map.129 = (f32[16,72,128]{2,1,0:T(8,128)}, f32[16,2,128]{2,1,0:T(2,128)}, f32[16,72,128]{2,1,0:T(8,128)}, f32[16,72,128]{2,1,0:T(8,128)}) custom-call(f32[16,112,128]{2,1,0:T(8,128)} %copy-done, bf16[16,128,128]{2,1,0:T(8,128)(2,1)} %bitcast.30, s32[16,6,8,128]{3,2,1,0:T(8,128)} %broadcast_in_dim.20.index_ref, ...), custom_call_target="tpu_custom_call" | custom-call | tf_op jit(solution)/shard_map/pallas_call | solution.py:460
  79.4 1.0 collective-permute-done
  80.4 0.7 add.21
  81.2 1.9 %collective-permute-start.1 = (f32[16,2,128]{2,1,0:T(2,128)S(1)}, f32[16,2,128]{2,1,0:T(2,128)S(1)}, u32[]{:S(2)}, u32[]{:S(2)}) collective-permute-start(f32[16,2,128]{2,1,0:T(2,128)S(1)} %add.21), channel_id=1, source_target_pairs={{0,2},{1,3},{2,0},{3,1},{4,6},{5,7},{6,4},{7,5},{8,10},{9,11},{10,... | collective-permute-start | bytes 49160 | tf_op jit(solution)/shard_map/ppermute | solution.py:477
  83.0 1.9 %collective-permute-done.1 = f32[16,2,128]{2,1,0:T(2,128)S(1)} collective-permute-done((f32[16,2,128]{2,1,0:T(2,128)S(1)}, f32[16,2,128]{2,1,0:T(2,128)S(1)}, u32[]{:S(2)}, u32[]{:S(2)}) %collective-permute-start.1) | collective-permute-done | bytes 16416 | tf_op jit(solution)/shard_map/ppermute | solution.py:477
  85.0 3.1 %collective-permute-start.2 = (f32[16,2,128]{2,1,0:T(2,128)S(1)}, f32[16,2,128]{2,1,0:T(2,128)S(1)}, u32[]{:S(2)}, u32[]{:S(2)}) collective-permute-start(f32[16,2,128]{2,1,0:T(2,128)S(1)} %add.22), channel_id=1, source_target_pairs={{0,4},{1,5},{2,6},{3,7},{4,0},{5,1},{6,2},{7,3},{8,12},{9,13},{10,... | collective-permute-start | bytes 49160 | tf_op jit(solution)/shard_map/ppermute | solution.py:477
  88.1 1.7 %collective-permute-done.2 = f32[16,2,128]{2,1,0:T(2,128)S(1)} collective-permute-done((f32[16,2,128]{2,1,0:T(2,128)S(1)}, f32[16,2,128]{2,1,0:T(2,128)S(1)}, u32[]{:S(2)}, u32[]{:S(2)}) %collective-permute-start.2) | collective-permute-done | bytes 16416 | tf_op jit(solution)/shard_map/ppermute | solution.py:477
  89.8 3.4 %collective-permute-start.3 = (f32[16,2,128]{2,1,0:T(2,128)S(1)}, f32[16,2,128]{2,1,0:T(2,128)S(1)}, u32[]{:S(2)}, u32[]{:S(2)}) collective-permute-start(f32[16,2,128]{2,1,0:T(2,128)S(1)} %add.23), channel_id=1, source_target_pairs={{0,8},{1,9},{2,10},{3,11},{4,12},{5,13},{6,14},{7,15},{8,0},{9,1},... | collective-permute-start | bytes 49160 | tf_op jit(solution)/shard_map/ppermute | solution.py:477
  93.2 1.7 %collective-permute-done.3 = f32[16,2,128]{2,1,0:T(2,128)S(1)} collective-permute-done((f32[16,2,128]{2,1,0:T(2,128)S(1)}, f32[16,2,128]{2,1,0:T(2,128)S(1)}, u32[]{:S(2)}, u32[]{:S(2)}) %collective-permute-start.3) | collective-permute-done | bytes 16416 | tf_op jit(solution)/shard_map/ppermute | solution.py:477
  95.5 41.0 %shard_map.130 = f32[16,72,128]{2,1,0:T(8,128)} custom-call(f32[16,72,128]{2,1,0:T(8,128)} %get-tuple-element.15.state_ref, f32[16,2,128]{2,1,0:T(2,128)} %add.24.extra_ref, s32[16,6,8,128]{3,2,1,0:T(8,128)} %broadcast_in_dim.20.index_ref, f32[16,72,128]{2,1,0:T(8,128)} %get-tuple-element.12.keep_ref, f32[16,6,40,128]{3,2,1,0:T(8,128)} %get-tuple-element.13.base_ref, ...), custom_call_target="tpu_custom_call" | custom-call | tf_op jit(solution)/shard_map/pallas_call | solution.py:460
  136.5 22.1 %all_to_all.10 = f32[16,72,128]{2,1,0:T(8,128)S(1)} all-to-all(f32[16,72,128]{2,1,0:T(8,128)} %shard_map.130), channel_id=1, replica_groups=mesh['groups'=2,'pts'=16] {'pts'}, dimensions={0} | all-to-all | bytes 1179648 | tf_op jit(solution)/shard_map/all_to_all | solution.py:480
  158.6 0.8 copy.18
  (36 shorter events, 3.9 us)
Async XLA Ops:
  2.7 12.5 %copy-start.4 = (s32[2048]{0:T(1024)S(1)}, s32[2048]{0:T(1024)}, u32[]{:S(2)}) copy-start(s32[2048]{0:T(1024)} %param.17) | copy-start | bytes 24580
  2.7 12.6 %copy-start.2 = (f32[6,2048]{1,0:T(8,128)S(1)}, f32[6,2048]{1,0:T(8,128)}, u32[]{:S(2)}) copy-start(f32[6,2048]{1,0:T(8,128)} %param.19) | copy-start | bytes 147460
  2.7 12.6 %copy-start.3 = (f32[6,2048]{1,0:T(8,128)S(1)}, f32[6,2048]{1,0:T(8,128)}, u32[]{:S(2)}) copy-start(f32[6,2048]{1,0:T(8,128)} %param.20) | copy-start | bytes 147460
  2.7 12.7 %copy-start.8 = (s32[32]{0:T(128)S(1)}, s32[32]{0:T(128)}, u32[]{:S(2)}) copy-start(s32[32]{0:T(128)} %param.21) | copy-start | bytes 388
  5.8 11.2 %copy-start.9 = (s32[72]{0:T(128)S(1)}, s32[72]{0:T(128)}, u32[]{:S(2)}) copy-start(s32[72]{0:T(128)} %constant.52.clone) | copy-start | bytes 868
  5.8 11.3 %copy-start.5 = (f32[2048]{0:T(1024)S(1)}, f32[2048]{0:T(1024)}, u32[]{:S(2)}) copy-start(f32[2048]{0:T(1024)} %param.16) | copy-start | bytes 24580
  5.8 11.3 %copy-start.6 = (f32[2048]{0:T(1024)S(1)}, f32[2048]{0:T(1024)}, u32[]{:S(2)}) copy-start(f32[2048]{0:T(1024)} %param.15) | copy-start | bytes 24580
  5.8 13.5 %copy-start.7 = (f32[2,72]{1,0:T(2,128)S(1)}, f32[2,72]{1,0:T(2,128)}, u32[]{:S(2)}) copy-start(f32[2,72]{1,0:T(2,128)} %constant.53.clone) | copy-start | bytes 1732
  5.8 28.4 %all-to-all-start = ((f32[16,112,128]{2,1,0:T(8,128)}), f32[16,112,128]{2,1,0:T(8,128)S(1)}, u32[]{:S(2)}, u32[]{:S(2)}) async-start(f32[16,112,128]{2,1,0:T(8,128)} %shard_map.127), calls=%async_computation | async-start | bytes 1835008 | tf_op jit(solution)/shard_map/all_to_all | solution.py:430
  15.9 18.2 %copy-start.1 = (s32[6,2048]{1,0:T(8,128)S(1)}, s32[6,2048]{1,0:T(8,128)}, u32[]{:S(2)}) copy-start(s32[6,2048]{1,0:T(8,128)} %param.18) | copy-start | bytes 147460
  34.1 1.1 copy-start
  79.0 1.5 collective-permute-start
  81.2 3.8 %collective-permute-start.1 = (f32[16,2,128]{2,1,0:T(2,128)S(1)}, f32[16,2,128]{2,1,0:T(2,128)S(1)}, u32[]{:S(2)}, u32[]{:S(2)}) collective-permute-start(f32[16,2,128]{2,1,0:T(2,128)S(1)} %add.21), channel_id=1, source_target_pairs={{0,2},{1,3},{2,0},{3,1},{4,6},{5,7},{6,4},{7,5},{8,10},{9,11},{10,... | collective-permute-start | bytes 49160 | tf_op jit(solution)/shard_map/ppermute | solution.py:477
  85.0 4.8 %collective-permute-start.2 = (f32[16,2,128]{2,1,0:T(2,128)S(1)}, f32[16,2,128]{2,1,0:T(2,128)S(1)}, u32[]{:S(2)}, u32[]{:S(2)}) collective-permute-start(f32[16,2,128]{2,1,0:T(2,128)S(1)} %add.22), channel_id=1, source_target_pairs={{0,4},{1,5},{2,6},{3,7},{4,0},{5,1},{6,2},{7,3},{8,12},{9,13},{10,... | collective-permute-start | bytes 49160 | tf_op jit(solution)/shard_map/ppermute | solution.py:477
  89.8 5.1 %collective-permute-start.3 = (f32[16,2,128]{2,1,0:T(2,128)S(1)}, f32[16,2,128]{2,1,0:T(2,128)S(1)}, u32[]{:S(2)}, u32[]{:S(2)}) collective-permute-start(f32[16,2,128]{2,1,0:T(2,128)S(1)} %add.23), channel_id=1, source_target_pairs={{0,8},{1,9},{2,10},{3,11},{4,12},{5,13},{6,14},{7,15},{8,0},{9,1},... | collective-permute-start | bytes 49160 | tf_op jit(solution)/shard_map/ppermute | solution.py:477

commit v3 on v2

--- a/solution.py
+++ b/solution.py
@@ -101,6 +101,8 @@
 GROUPS = 9
 GROUP_ROWS = 8
 BASE_GROUP = (0, 1, 2, 3, 0, 1, 2, 3, 4)
+LISTED = 1024
+CHUNK = 256
 
 
 def row_layout():
@@ -155,25 +157,22 @@
     return jnp.asarray(np.broadcast_to(table[:, :, None], table.shape + (LANES,)))
 
 
-def setup_kernel(points_ref, edge_ref, rows_ref, dirs_ref, keep_ref, base_ref, growth_ref):
-    edge_count = edge_ref.shape[0]
+def setup_kernel(points_ref, x_ref, y_ref, rows_ref, dirs_ref, keep_ref, growth_ref):
+    edge_count = x_ref.shape[0]
 
     def block(place, _):
-        speed = jnp.broadcast_to(points_ref[place, 0:1, :], (GROUP_ROWS, LANES)) * 0.125
-        heading = jnp.broadcast_to(points_ref[place, 1:2, :], (GROUP_ROWS, LANES))
-        active = jnp.broadcast_to(points_ref[place, 2:3, :], (GROUP_ROWS, LANES))
-        free = jnp.broadcast_to(points_ref[place, 3:4, :], (GROUP_ROWS, LANES))
+        speed = spread_row(points_ref, 0, place) * 0.125
+        heading = spread_row(points_ref, 1, place)
+        active = spread_row(points_ref, 2, place)
+        free = spread_row(points_ref, 3, place)
         along, across = speed * jnp.cos(heading), speed * jnp.sin(heading)
         total = []
-        for base_group, group in enumerate((0, 1, 2, 3, 8)):
+        for group in (0, 1, 2, 3, 8):
             cosine, sine = dirs_ref[0, group_rows(group), :], dirs_ref[1, group_rows(group), :]
             out = jnp.zeros((GROUP_ROWS, LANES), jnp.float32)
             for edge in range(edge_count):
-                x = jnp.broadcast_to(edge_ref[edge, place, 0:1, :], (GROUP_ROWS, LANES))
-                y = jnp.broadcast_to(edge_ref[edge, place, 1:2, :], (GROUP_ROWS, LANES))
-                flow = cosine * x + sine * y
+                flow = cosine * spread_row(x_ref, edge, place) + sine * spread_row(y_ref, edge, place)
                 out = out + jnp.maximum(flow, 0.0)
-                base_ref[place, edge, group_rows(base_group), :] = jnp.minimum(flow, 0.0) * free
             total.append(out)
         for group in range(GROUPS):
             rows = group_rows(group)
@@ -184,6 +183,156 @@
         return 0
 
     lax.fori_loop(0, keep_ref.shape[0], block, 0)
+
+
+def spread_row(ref, *place):
+    row = ref[place[:-1] + (pl.ds(place[-1], 1), slice(None))]
+    return jnp.broadcast_to(row, (GROUP_ROWS, LANES))
+
+
+def split_three(values):
+    high = values.astype(jnp.bfloat16).astype(jnp.float32)
+    rest = values - high
+    middle = rest.astype(jnp.bfloat16).astype(jnp.float32)
+    return high, middle, rest - middle
+
+
+def plan_kernel(
+    near_ref,
+    x_ref,
+    y_ref,
+    points_ref,
+    dirs_ref,
+    first_out,
+    base_out,
+    gather_out,
+    scatter_out,
+    listed_ref,
+    fits_ref,
+    first,
+    base,
+    gather,
+    scatter,
+    marks,
+    places,
+    values,
+    picked,
+    sems,
+):
+    f32, bf16 = jnp.float32, jnp.bfloat16
+    edge_count, blocks, _ = near_ref.shape
+    free = points_ref[3]
+    high = [near_ref[edge] >> 7 for edge in range(edge_count)]
+
+    def block(place, _):
+        wanted = lax.broadcasted_iota(jnp.int32, (blocks, LANES), 0)
+        lanes = jnp.zeros((blocks, LANES), jnp.int32)
+        x = jnp.zeros((blocks, LANES), f32)
+        y = jnp.zeros((blocks, LANES), f32)
+        for edge in reversed(range(edge_count)):
+            near = jnp.broadcast_to(near_ref[edge, pl.ds(place, 1), :], (blocks, LANES))
+            hit = (near >> 7) == wanted
+            lanes = jnp.where(hit, near & (LANES - 1), lanes)
+            x = jnp.where(hit, jnp.broadcast_to(x_ref[edge, pl.ds(place, 1), :], (blocks, LANES)), x)
+            y = jnp.where(hit, jnp.broadcast_to(y_ref[edge, pl.ds(place, 1), :], (blocks, LANES)), y)
+        open_row = spread_row(points_ref, 3, place)
+        for source in range(blocks):
+            first[place, source] = jnp.broadcast_to(lanes[source : source + 1], (GROUP_ROWS, LANES))
+            x_row = jnp.broadcast_to(x[source : source + 1], (GROUP_ROWS, LANES))
+            y_row = jnp.broadcast_to(y[source : source + 1], (GROUP_ROWS, LANES))
+            for group, rows in enumerate((0, 1, 2, 3, 8)):
+                flow = dirs_ref[0, group_rows(rows), :] * x_row + dirs_ref[1, group_rows(rows), :] * y_row
+                base[place, source, group_rows(group), :] = jnp.minimum(flow, 0.0) * open_row
+        return 0
+
+    lax.fori_loop(0, blocks, block, 0)
+    copies = [pltpu.make_async_copy(first, first_out, sems.at[0]), pltpu.make_async_copy(base, base_out, sems.at[1])]
+    for copy in copies:
+        copy.start()
+
+    marks[...] = jnp.zeros_like(marks)
+    for edge in range(edge_count):
+        again = jnp.zeros((blocks, LANES), jnp.bool_)
+        for before in range(edge):
+            again = again | (high[before] == high[edge])
+        marks[pl.ds(blocks * edge, blocks), :] = jnp.where(again, free, 0.0)
+        x_parts, y_parts = split_three(x_ref[edge]), split_three(y_ref[edge])
+        rows = ((near_ref[edge] & (LANES - 1)).astype(f32), high[edge].astype(f32)) + x_parts + y_parts
+        for place in range(blocks):
+            side, column = divmod(place, blocks // 2)
+            for number, row in enumerate(rows):
+                values[side, pl.ds(8 * edge + number, 1), pl.ds(LANES * column, LANES)] = row[place : place + 1]
+    left = lax.broadcasted_iota(jnp.int32, (LANES, LANES), 0)
+    right = lax.broadcasted_iota(jnp.int32, (LANES, LANES), 1)
+    mark = marks[...].astype(bf16)
+    within = jnp.dot(mark, jnp.where(left < right, 1.0, 0.0).astype(bf16), preferred_element_type=f32)
+    count = jnp.dot(mark, jnp.ones((LANES, LANES), bf16), preferred_element_type=f32)
+    earlier = (right < left) & ((left & (blocks // 2)) == (right & (blocks // 2)))
+    offset = jnp.dot(jnp.where(earlier, 1.0, 0.0).astype(bf16), count.astype(bf16), preferred_element_type=f32)
+    position = jnp.where(marks[...] > 0.0, within + offset, -1.0)
+    places[0] = position
+    places[1] = offset
+    fits_ref[0] = (jnp.max(position) < LISTED).astype(jnp.int32)
+
+    rank = lax.broadcasted_iota(jnp.int32, (16, LANES), 0).astype(f32)
+
+    def scatter_block(place, _):
+        rows = [
+            jnp.broadcast_to(places[0, pl.ds(blocks * edge + place, 1), :], (16, LANES)) for edge in range(edge_count)
+        ]
+        for tile in range(LISTED // 16):
+            here = rank + float(16 * tile)
+            hit = rows[0] == here
+            for row in rows[1:]:
+                hit = hit | (row == here)
+            value = jnp.where(hit, 1.0, 0.0).astype(bf16)
+            scatter[place // 2, pl.ds(16 * tile, 16), pl.ds(pl.multiple_of((place % 2) * LANES, LANES), LANES)] = value
+        return 0
+
+    lax.fori_loop(0, blocks, scatter_block, 0)
+    copies.append(pltpu.make_async_copy(scatter, scatter_out, sems.at[2]))
+    copies[-1].start()
+
+    chunks = LISTED // CHUNK
+    for side in range(2):
+        wide = None
+        for column in range(chunks):
+            term = lax.dot_general(
+                values[side, :, pl.ds(CHUNK * column, CHUNK)].astype(bf16),
+                scatter[chunks * side + column],
+                (((1,), (1,)), ((), ())),
+                preferred_element_type=f32,
+            )
+            wide = term if wide is None else wide + term
+        for column in range(LISTED // LANES):
+            here = lax.broadcasted_iota(jnp.int32, (8, LANES), 1).astype(f32) + float(LANES * column)
+            chosen = wide[0:8, LANES * column : LANES * (column + 1)]
+            for edge in range(1, edge_count):
+                begin = spread_row(places, 1, blocks * edge + (blocks // 2) * side)
+                chosen = jnp.where(
+                    here >= begin, wide[8 * edge : 8 * edge + 8, LANES * column : LANES * (column + 1)], chosen
+                )
+            spot = (LISTED // LANES) * side + column
+            x_row = jnp.broadcast_to(chosen[2:3] + chosen[3:4] + chosen[4:5], (GROUP_ROWS, LANES))
+            y_row = jnp.broadcast_to(chosen[5:6] + chosen[6:7] + chosen[7:8], (GROUP_ROWS, LANES))
+            picked[pl.ds(spot, 1), :] = chosen[0:1] + float(LANES) * chosen[1:2]
+            lane = slice(LANES * (column % 2), LANES * (column % 2) + LANES)
+            for group, rows in enumerate((0, 1, 2, 3, 8)):
+                flow = dirs_ref[0, group_rows(rows), :] * x_row + dirs_ref[1, group_rows(rows), :] * y_row
+                listed_ref[spot // 2, group_rows(group), lane] = jnp.minimum(flow, 0.0)
+
+    def gather_block(spot, _):
+        source = jnp.broadcast_to(picked[pl.ds(spot, 1), :], (16, LANES))
+        for tile in range(gather.shape[1] // 16):
+            value = jnp.where(rank + float(16 * tile) == source, 1.0, 0.0).astype(bf16)
+            gather[spot // 2, pl.ds(16 * tile, 16), pl.ds(pl.multiple_of((spot % 2) * LANES, LANES), LANES)] = value
+        return 0
+
+    lax.fori_loop(0, 2 * LISTED // LANES, gather_block, 0)
+    copies.append(pltpu.make_async_copy(gather, gather_out, sems.at[3]))
+    copies[-1].start()
+    for copy in copies:
+        copy.wait()
 
 
 def frequency(place):
@@ -261,23 +410,43 @@
 
 def fine_kernel(
     first,
+    fits_ref,
     state_ref,
     extra_ref,
-    index_ref,
+    near_ref,
+    x_ref,
+    y_ref,
+    points_ref,
+    dirs_ref,
     keep_ref,
-    base_ref,
     growth_ref,
     rows_ref,
+    listed_ref,
+    first_in,
+    base_in,
+    gather_in,
+    scatter_in,
     *rest,
 ):
     if first:
-        out_ref, sums_ref, start_ref, slope_ref, field, words, speed = rest
+        out_ref, sums_ref, start_ref, slope_ref = rest[:4]
     else:
-        start_ref, slope_ref, out_ref, field, words, speed = rest
+        start_ref, slope_ref, out_ref = rest[:3]
+    scratch = rest[4:] if first else rest[3:]
+    field, words, speed, first_ref, base_ref, gather_ref, scatter_ref, pairs, inflow_ref, terms, sems = scratch
+    f32, bf16 = jnp.float32, jnp.bfloat16
     blocks = keep_ref.shape[0]
     half = blocks // 2
-    edge_count = base_ref.shape[1]
+    edge_count = near_ref.shape[0]
     first_step = 0 if first else SUB
+    copies = [
+        pltpu.make_async_copy(source, target, sems.at[number])
+        for number, (source, target) in enumerate(
+            ((first_in, first_ref), (base_in, base_ref), (gather_in, gather_ref), (scatter_in, scatter_ref))
+        )
+    ]
+    for copy in copies:
+        copy.start()
 
     if first:
         total = state_ref[0, pl.ds(2 * NDIR, 40), :]
@@ -320,57 +489,127 @@
 
     lax.fori_loop(0, blocks, enter, 0)
 
+    def boundary(place, rows, number):
+        time_frac = (number + (first_step + 1)).astype(f32) * (1.0 / (STEPS * SUB))
+        return start_ref[place, rows, :] + time_frac * slope_ref[place, rows, :]
+
+    def encode(group, top_code):
+        rows = group_rows(group)
+        values = [field[0, place, rows, :] for place in range(blocks)]
+        top = functools.reduce(jnp.maximum, values)
+        top = jnp.maximum(jnp.max(top, axis=1, keepdims=True), 1e-30)
+        scale = jnp.broadcast_to(top_code / top, (GROUP_ROWS, LANES))
+        speed[rows, :] = rows_ref[3, rows, :] * (top * (1.0 / top_code))
+        return [(value * scale + 0.5).astype(jnp.int32) for value in values]
+
     def fine_step(number, _):
-        source = lax.rem(number, 2)
-        time_frac = (number + (first_step + 1)).astype(jnp.float32) * (1.0 / (STEPS * SUB))
-        for group in range(GROUPS):
-            rows = group_rows(group)
-            values = [field[source, place, rows, :] for place in range(blocks)]
-            top = functools.reduce(jnp.maximum, values)
-            top = jnp.maximum(jnp.max(top, axis=1, keepdims=True), 1e-30)
-            scale = jnp.broadcast_to(65535.0 / top, (GROUP_ROWS, LANES))
-            speed[rows, :] = rows_ref[3, rows, :] * (top * (1.0 / 65535.0))
-            coded = [(value * scale + 0.5).astype(jnp.int32) for value in values]
-            for place in range(half):
-                words[place, rows, :] = (coded[place + half] << 16) | coded[place]
-
+        for group in range(4):
+            lower, upper = encode(group, 65535.0), encode(group + 4, 65535.0)
+            for place in range(blocks):
+                pairs[place, group_rows(group), :] = (upper[place] << 16) | lower[place]
+        for place in range(blocks):
+            for group in range(GROUPS):
+                high, low = split_bf16(field[0, place, group_rows(group), :])
+                both = jnp.concatenate([high, low], axis=0).astype(bf16)
+                words[pl.ds(16 * group, 16), pl.ds(LANES * place, LANES)] = both
+
+        def collect(chunk, _):
+            found = jnp.dot(words[...], gather_ref[chunk], preferred_element_type=f32)
+            for group in range(GROUPS):
+                value = found[16 * group : 16 * group + 8] + found[16 * group + 8 : 16 * group + 16]
+                high, low = split_bf16(value * listed_ref[chunk, group_rows(BASE_GROUP[group]), :])
+                terms[chunk, pl.ds(16 * group, 16), :] = jnp.concatenate([high, low], axis=0).astype(bf16)
+            for side in range(2):
+                place = 2 * chunk + side
+                inflow = [jnp.zeros((GROUP_ROWS, LANES), f32)] * GROUPS
+                for source in range(blocks):
+                    lanes = first_ref[place, source]
+                    for group in range(4):
+                        base = base_ref[place, source, group_rows(group), :]
+                        word = take_lanes(pairs[source, group_rows(group), :], lanes)
+                        lower = (word & 65535).astype(f32)
+                        upper = lax.shift_right_logical(word, 16).astype(f32)
+                        inflow[group] = inflow[group] + base * lower
+                        inflow[group + 4] = inflow[group + 4] + base * upper
+                    last = take_lanes(field[0, source, group_rows(8), :], lanes)
+                    inflow[8] = inflow[8] + base_ref[place, source, group_rows(4), :] * last
+                for group in range(GROUPS):
+                    factor = speed[group_rows(group), :] if group < 8 else rows_ref[3, group_rows(8), :]
+                    inflow_ref[place, group_rows(group), :] = factor * inflow[group]
+            return 0
+
+        lax.fori_loop(0, blocks // 2, collect, 0)
+
+        def update(chunk, _):
+            chunks = LISTED // CHUNK
+            begin = (chunk // chunks) * chunks
+            moved = None
+            for part in range(chunks):
+                term = jnp.dot(
+                    terms[begin + part],
+                    scatter_ref[chunk, pl.ds(CHUNK * part, CHUNK), :],
+                    preferred_element_type=f32,
+                )
+                moved = term if moved is None else moved + term
+            for side in range(2):
+                place = 2 * chunk + side
+                lanes = slice(LANES * side, LANES * (side + 1))
+                for group in range(GROUPS):
+                    rows = group_rows(group)
+                    more = moved[16 * group : 16 * group + 8, lanes] + moved[16 * group + 8 : 16 * group + 16, lanes]
+                    field[0, place, rows, :] = (
+                        field[0, place, rows, :] * keep_ref[place, rows, :]
+                        - inflow_ref[place, rows, :]
+                        - rows_ref[3, rows, :] * more
+                        + boundary(place, rows, number)
+                    )
+            return 0
+
+        lax.fori_loop(0, blocks // 2, update, 0)
+        return 0
+
+    def plain_step(number, _):
         def block(place, _):
-            inflow = [None] * GROUPS
+            free = spread_row(points_ref, 3, place)
+            inflow = [jnp.zeros((GROUP_ROWS, LANES), f32)] * GROUPS
             for edge in range(edge_count):
-                index = index_ref[place, edge]
-                lanes = index & (LANES - 1)
-                masks = [(index & (LANES << level)) != 0 for level in range(half.bit_length() - 1)]
-                shift = (index >> (half.bit_length() + 6)) << 4
-
-                def pick(low, level, rows):
-                    if level == 0:
-                        return take_lanes(words[low, rows, :], lanes)
-                    step = 1 << (level - 1)
-                    below = pick(low, level - 1, rows)
-                    above = pick(low + step, level - 1, rows)
-                    return jnp.where(masks[level - 1], above, below)
-
+                near = spread_row(near_ref, edge, place)
+                lanes, home = near & (LANES - 1), near >> 7
+                x, y = spread_row(x_ref, edge, place), spread_row(y_ref, edge, place)
                 for group in range(GROUPS):
-                    word = pick(0, half.bit_length() - 1, group_rows(group))
-                    value = (lax.shift_right_logical(word, shift) & 65535).astype(jnp.float32)
-                    term = base_ref[place, edge, group_rows(BASE_GROUP[group]), :] * value
-                    inflow[group] = term if inflow[group] is None else inflow[group] + term
+                    rows = group_rows(group)
+                    value = jnp.zeros((GROUP_ROWS, LANES), f32)
+                    for source in range(blocks):
+                        value = jnp.where(home == source, take_lanes(field[0, source, rows, :], lanes), value)
+                    flow = dirs_ref[0, rows, :] * x + dirs_ref[1, rows, :] * y
+                    inflow[group] = inflow[group] + jnp.minimum(flow, 0.0) * free * value
             for group in range(GROUPS):
                 rows = group_rows(group)
-                field[1 - source, place, rows, :] = (
-                    field[source, place, rows, :] * keep_ref[place, rows, :]
-                    - speed[rows, :] * inflow[group]
-                    + (start_ref[place, rows, :] + time_frac * slope_ref[place, rows, :])
+                field[1, place, rows, :] = (
+                    field[0, place, rows, :] * keep_ref[place, rows, :]
+                    - rows_ref[3, rows, :] * inflow[group]
+                    + boundary(place, rows, number)
                 )
             return 0
 
         lax.fori_loop(0, blocks, block, 0)
+        field[0] = field[1]
         return 0
 
-    lax.fori_loop(0, SUB, fine_step, 0)
+    for copy in copies:
+        copy.wait()
+    fits = fits_ref[0]
+
+    @pl.when(fits != 0)
+    def _():
+        lax.fori_loop(0, SUB, fine_step, 0)
+
+    @pl.when(fits == 0)
+    def _():
+        lax.fori_loop(0, SUB, plain_step, 0)
 
     def leave(place, _):
-        values = [field[SUB % 2, place, group_rows(group), :] for group in range(GROUPS)]
+        values = [field[0, place, group_rows(group), :] for group in range(GROUPS)]
         if first:
             energy, inverse = None, None
             for group in range(GROUPS):
@@ -433,42 +672,89 @@
     select = jnp.pad(spread.astype(jnp.bfloat16), ((0, LANES - bound_count), (0, 0)))
     select = select.reshape(LANES, blocks, LANES).transpose(1, 0, 2)
     free = jnp.where(jnp.any(spread, axis=0), 0.0, active)
-    per_point = jnp.stack([wind_speed, wind_heading, active, free]).reshape(4, blocks, LANES).transpose(1, 0, 2)
-    edges = jnp.stack([edge_x, edge_y], axis=1).reshape(edge_count, 2, blocks, LANES).transpose(0, 2, 1, 3)
-    rows = row_tables(device_place)
-    keep, base, growth = pl.pallas_call(
+    points = jnp.stack([wind_speed, wind_heading, active, free]).reshape(4, blocks, LANES)
+    near, edge_x, edge_y = [array.reshape(edge_count, blocks, LANES) for array in (neighbours, edge_x, edge_y)]
+    rows, dirs = row_tables(device_place), direction_tables()
+    state_shape = jax.ShapeDtypeStruct((blocks, local_count, LANES), f32)
+    keep, growth = pl.pallas_call(
         setup_kernel,
-        out_shape=[
-            jax.ShapeDtypeStruct((blocks, local_count, LANES), f32),
-            jax.ShapeDtypeStruct((blocks, edge_count, 40, LANES), f32),
-            jax.ShapeDtypeStruct((blocks, local_count, LANES), f32),
-        ],
-        in_specs=in_vmem(4),
-        out_specs=in_vmem(3),
+        out_shape=[state_shape] * 2,
+        in_specs=in_vmem(5),
+        out_specs=in_vmem(2),
         compiler_params=params(),
         cost_estimate=pl.CostEstimate(flops=100_000_000, bytes_accessed=4_000_000, transcendentals=1_000_000),
-    )(per_point, edges, rows, direction_tables())
-
-    index = neighbours.reshape(edge_count, blocks, 1, LANES).transpose(1, 0, 2, 3)
-    index = jnp.broadcast_to(index, (blocks, edge_count, GROUP_ROWS, LANES))
-
-    def fine(first, state, extra, bound):
-        state_shape = jax.ShapeDtypeStruct((blocks, local_count, LANES), f32)
+    )(points, edge_x, edge_y, rows, dirs)
+
+    shapes = [
+        ((blocks, blocks, GROUP_ROWS, LANES), jnp.int32),
+        ((blocks, blocks, 40, LANES), f32),
+        ((2 * LISTED // CHUNK, grid_points, CHUNK), jnp.bfloat16),
+        ((grid_points // CHUNK, LISTED, CHUNK), jnp.bfloat16),
+    ]
+    tables = [pltpu.VMEM(shape, dtype) for shape, dtype in shapes]
+    first_edge, base, gather, scatter, listed, fits = pl.pallas_call(
+        plan_kernel,
+        out_shape=[jax.ShapeDtypeStruct(shape, dtype) for shape, dtype in shapes]
+        + [jax.ShapeDtypeStruct((2 * LISTED // CHUNK, 40, CHUNK), f32), jax.ShapeDtypeStruct((1,), jnp.int32)],
+        in_specs=in_vmem(5),
+        out_specs=[pl.BlockSpec(memory_space=pl.ANY)] * 4
+        + [pl.BlockSpec(memory_space=pltpu.VMEM), pl.BlockSpec(memory_space=pltpu.SMEM)],
+        scratch_shapes=tables
+        + [
+            pltpu.VMEM((LANES, LANES), f32),
+            pltpu.VMEM((2, LANES, LANES), f32),
+            pltpu.VMEM((2, 8 * edge_count, LISTED), f32),
+            pltpu.VMEM((16, LANES), f32),
+            pltpu.SemaphoreType.DMA((4,)),
+        ],
+        compiler_params=params(),
+        cost_estimate=pl.CostEstimate(flops=1_000_000_000, bytes_accessed=20_000_000, transcendentals=0),
+    )(near, edge_x, edge_y, points, dirs)
+
+    def fine(is_first, state, extra, bound):
         out_shape = [state_shape]
-        if first:
+        if is_first:
             out_shape += [jax.ShapeDtypeStruct((blocks, 2, LANES), f32), state_shape, state_shape]
         return pl.pallas_call(
-            functools.partial(fine_kernel, first),
+            functools.partial(fine_kernel, is_first),
             out_shape=out_shape,
-            in_specs=in_vmem(7 + len(bound)),
+            in_specs=[pl.BlockSpec(memory_space=pltpu.SMEM)]
+            + in_vmem(11)
+            + [pl.BlockSpec(memory_space=pl.ANY)] * 4
+            + in_vmem(len(bound)),
             out_specs=in_vmem(len(out_shape)),
             scratch_shapes=[
                 pltpu.VMEM((2, blocks, local_count, LANES), f32),
-                pltpu.VMEM((blocks // 2, local_count, LANES), jnp.int32),
+                pltpu.VMEM((2 * local_count, grid_points), jnp.bfloat16),
                 pltpu.VMEM((local_count, LANES), f32),
+            ]
+            + tables
+            + [
+                pltpu.VMEM((blocks, 32, LANES), jnp.int32),
+                pltpu.VMEM((blocks, local_count, LANES), f32),
+                pltpu.VMEM((2 * LISTED // CHUNK, 2 * local_count, CHUNK), jnp.bfloat16),
+                pltpu.SemaphoreType.DMA((4,)),
             ],
             compiler_params=params(),
-        )(state, extra, index, keep, base, growth, rows, *bound)
+        )(
+            fits,
+            state,
+            extra,
+            near,
+            edge_x,
+            edge_y,
+            points,
+            dirs,
+            keep,
+            growth,
+            rows,
+            listed,
+            first_edge,
+            base,
+            gather,
+            scatter,
+            *bound,
+        )
 
     field, sums, start, slope = fine(True, received, select, ())
     distance = 1
@@ -507,7 +793,8 @@
         and 4 * bound_points.shape[0] == LANES
         and coarse_spectra.shape[2] == LANES
         and blocks == device_count
-        and blocks & (blocks - 1) == 0
+        and blocks == 16
+        and neighbours.shape[0] * blocks <= LANES
     ):
         return whole_frequencies(
             spectra_in,

time: 160 us -> 148 us (0.925)
  waiting for transfers between devices: 16.4 us -> 6.66 us
  Pallas kernels: 92 us -> 88.3 us
  local copies, waits for them, and re-layouts: 7.3 us -> 9.24 us
  starting transfers between devices: 16.3 us -> 14.6 us
    all_to_all x1, waiting for transfers between devices: 10 us -> 0.01 us  [whole_frequencies(): lax.all_to_all(send, 'pts', split_axis=0, concat_axis=0, tiled=True)]
    pallas_call x3 -> x4, Pallas kernels: 88.9 us -> 85.2 us  [the longest x2 66.2 us: fine(): pl.pallas_call(functools.partial(fine_kernel, is_first), out_shape=out_sh...]
    unnamed x21 -> x18, local copies, waits for them, and re-layouts: 1.09 us -> 3.24 us
  transfers between devices with their start and end apart: 5 -> 5, of which waited for: 5 -> 4; matrix products, arithmetic and copies ran while one was open for 3% -> 5% of each run, Pallas kernels for 3% -> 13%
where the time goes in v3:
time: 148 us; the launch traced here: 147 us
  Pallas kernels  88.3 us (60%)
  blocking collectives  23.4 us (16%)
  starting transfers between devices  14.6 us (10%)
  local copies, waits for them, and re-layouts  9.24 us (6%)
  waiting for transfers between devices  6.66 us (4%)
  other arithmetic  3.76 us (3%)
    pallas_call x2, Pallas kernels, fine(): pl.pallas_call(functools.partial(fine_kernel, is_first), out_shape=out_sh...  66.2 us
    all_to_all x1, blocking collectives, whole_frequencies(): lax.all_to_all(field, 'pts', split_axis=0, concat_axis=0, tiled=True)  23.4 us
    pallas_call x1, Pallas kernels, whole_frequencies(): pl.pallas_call(plan_kernel, out_shape=[jax.ShapeDtypeStruct(shape, dtype)...  15.8 us
    all_to_all x1, starting transfers between devices, whole_frequencies(): lax.all_to_all(send, 'pts', split_axis=0, concat_axis=0, tiled=True)  7.38 us
    ppermute x4, starting transfers between devices, whole_frequencies(): sums = sums + lax.ppermute(sums, 'pts', pairs)  7.18 us
    ppermute x4, waiting for transfers between devices, whole_frequencies(): sums = sums + lax.ppermute(sums, 'pts', pairs)  6.66 us
    unnamed x18, local copies, waits for them, and re-layouts  3.24 us
    pallas_call x1, Pallas kernels, whole_frequencies(): pl.pallas_call(setup_kernel, out_shape=[state_shape] * 2, in_specs=in_vme...  3.19 us
  transfers between devices with their start and end apart: 5, of which 4 were waited for; matrix products, arithmetic and copies ran while one was open for 5% of the time, Pallas kernels for 13%

profile of v3, /device:TPU:0, one launch (start us, length us, event | category | flops | bytes accessed | tf_op | source)
XLA Modules:
  0.0 147.4 jit_solution(7117704446498085246)
XLA Ops:
  0.0 0.8 tile.8
  1.5 0.7 tile.20
  2.8 3.0 %shard_map.128 = f32[16,112,128]{2,1,0:T(8,128)} custom-call(s32[1]{0:T(128)} %bitcast.4.first_ref, f32[1152,128]{1,0:T(8,128)} %spectra_ref.1, f32[2,1152,128]{2,1,0:T(8,128)} %coarse_ref.1, s32[4,128]{1,0:T(4,128)} %tile.9.cells_ref, f32[4,128]{1,0:T(4,128)} %tile.21.weights_ref), custom_call_target="tpu_custom_call" | custom-call | tf_op jit(solution)/shard_map/pallas_call | solution.py:661
  5.9 7.4 %all-to-all-start = ((f32[16,112,128]{2,1,0:T(8,128)}), f32[16,112,128]{2,1,0:T(8,128)S(1)}, u32[]{:S(2)}, u32[]{:S(2)}) async-start(f32[16,112,128]{2,1,0:T(8,128)} %shard_map.128), calls=%async_computation | async-start | bytes 1835008 | tf_op jit(solution)/shard_map/all_to_all | solution.py:669
  15.2 1.5 copy.21
  16.6 1.0 iota_compare_fusion
  17.8 1.0 copy.14
  20.2 0.8 broadcast_in_dim.7.rows_ref
  21.0 0.7 jit_solution_.3.dirs_ref
  21.7 3.2 %shard_map.129 = (f32[16,72,128]{2,1,0:T(8,128)}, f32[16,72,128]{2,1,0:T(8,128)}) custom-call(f32[4,16,128]{2,1,0:T(8,128)} %pad_maximum_fusion.points_ref, f32[6,16,128]{2,1,0:T(8,128)} %get-tuple-element.39.x_ref, f32[6,16,128]{2,1,0:T(8,128)} %get-tuple-element.38.y_ref, f32[6,72,128]{2,1,0:T(8,128)} %broadcast_in_dim.7.rows_ref, ...), custom_call_target="tpu_custom_call" | custom-call | flops 100000000 | bytes 4000000 | tf_op jit(solution)/shard_map/pallas_call | solution.py:679
  24.9 15.8 %shard_map.127 = (s32[16,16,8,128]{3,2,1,0:T(8,128)}, f32[16,16,40,128]{3,2,1,0:T(8,128)}, bf16[8,2048,256]{2,1,0:T(8,128)(2,1)}, bf16[8,1024,256]{2,1,0:T(8,128...) custom-call(s32[6,16,128]{2,1,0:T(8,128)} %bitcast.35, f32[6,16,128]{2,1,0:T(8,128)} %get-tuple-element.39.x_ref, ...), custom_call_target="tpu_custom_call" | custom-call | flops 1000000000 | bytes 20000000 | tf_op jit(solution)/shard_map/pallas_call | solution.py:695
  40.8 0.9 copy-done
  41.7 33.4 %shard_map.130 = (f32[16,72,128]{2,1,0:T(8,128)}, f32[16,2,128]{2,1,0:T(2,128)}, f32[16,72,128]{2,1,0:T(8,128)}, f32[16,72,128]{2,1,0:T(8,128)}) custom-call(s32[1]{0:T(128)} %get-tuple-element.17.fits_ref, f32[16,112,128]{2,1,0:T(8,128)} %copy-done, bf16[16,128,128]{2,1,0:T(8,128)(2,1)} %bitcast.33, s32[6,16,128]{2,1,0:T(8,128)} %bitcast.36, ...), custom_call_target="tpu_custom_call" | custom-call | tf_op jit(solution)/shard_map/pallas_call | solution.py:718
  75.5 1.0 collective-permute-done
  76.6 0.7 add.21
  77.3 1.9 %collective-permute-start.1 = (f32[16,2,128]{2,1,0:T(2,128)S(1)}, f32[16,2,128]{2,1,0:T(2,128)S(1)}, u32[]{:S(2)}, u32[]{:S(2)}) collective-permute-start(f32[16,2,128]{2,1,0:T(2,128)S(1)} %add.21), channel_id=1, source_target_pairs={{0,2},{1,3},{2,0},{3,1},{4,6},{5,7},{6,4},{7,5},{8,10},{9,11},{10,... | collective-permute-start | bytes 49160 | tf_op jit(solution)/shard_map/ppermute | solution.py:763
  79.2 1.9 %collective-permute-done.1 = f32[16,2,128]{2,1,0:T(2,128)S(1)} collective-permute-done((f32[16,2,128]{2,1,0:T(2,128)S(1)}, f32[16,2,128]{2,1,0:T(2,128)S(1)}, u32[]{:S(2)}, u32[]{:S(2)}) %collective-permute-start.1) | collective-permute-done | bytes 16416 | tf_op jit(solution)/shard_map/ppermute | solution.py:763
  81.1 1.9 %collective-permute-start.2 = (f32[16,2,128]{2,1,0:T(2,128)S(1)}, f32[16,2,128]{2,1,0:T(2,128)S(1)}, u32[]{:S(2)}, u32[]{:S(2)}) collective-permute-start(f32[16,2,128]{2,1,0:T(2,128)S(1)} %add.22), channel_id=1, source_target_pairs={{0,4},{1,5},{2,6},{3,7},{4,0},{5,1},{6,2},{7,3},{8,12},{9,13},{10,... | collective-permute-start | bytes 49160 | tf_op jit(solution)/shard_map/ppermute | solution.py:763
  83.1 1.9 %collective-permute-done.2 = f32[16,2,128]{2,1,0:T(2,128)S(1)} collective-permute-done((f32[16,2,128]{2,1,0:T(2,128)S(1)}, f32[16,2,128]{2,1,0:T(2,128)S(1)}, u32[]{:S(2)}, u32[]{:S(2)}) %collective-permute-start.2) | collective-permute-done | bytes 16416 | tf_op jit(solution)/shard_map/ppermute | solution.py:763
  84.9 2.8 %collective-permute-start.3 = (f32[16,2,128]{2,1,0:T(2,128)S(1)}, f32[16,2,128]{2,1,0:T(2,128)S(1)}, u32[]{:S(2)}, u32[]{:S(2)}) collective-permute-start(f32[16,2,128]{2,1,0:T(2,128)S(1)} %add.23), channel_id=1, source_target_pairs={{0,8},{1,9},{2,10},{3,11},{4,12},{5,13},{6,14},{7,15},{8,0},{9,1},... | collective-permute-start | bytes 49160 | tf_op jit(solution)/shard_map/ppermute | solution.py:763
  87.8 1.9 %collective-permute-done.3 = f32[16,2,128]{2,1,0:T(2,128)S(1)} collective-permute-done((f32[16,2,128]{2,1,0:T(2,128)S(1)}, f32[16,2,128]{2,1,0:T(2,128)S(1)}, u32[]{:S(2)}, u32[]{:S(2)}) %collective-permute-start.3) | collective-permute-done | bytes 16416 | tf_op jit(solution)/shard_map/ppermute | solution.py:763
  90.3 32.9 %shard_map.131 = f32[16,72,128]{2,1,0:T(8,128)} custom-call(s32[1]{0:T(128)} %get-tuple-element.17.fits_ref, f32[16,72,128]{2,1,0:T(8,128)} %get-tuple-element.25.state_ref, f32[16,2,128]{2,1,0:T(2,128)} %add.24.extra_ref, s32[6,16,128]{2,1,0:T(8,128)} %bitcast.37, f32[6,16,128]{2,1,0:T(8,128)} %get-tuple-element.39.x_ref, ...), custom_call_target="tpu_custom_call" | custom-call | tf_op jit(solution)/shard_map/pallas_call | solution.py:718
  123.1 23.4 %all_to_all.10 = f32[16,72,128]{2,1,0:T(8,128)S(1)} all-to-all(f32[16,72,128]{2,1,0:T(8,128)} %shard_map.131), channel_id=1, replica_groups=mesh['groups'=2,'pts'=16] {'pts'}, dimensions={0} | all-to-all | bytes 1179648 | tf_op jit(solution)/shard_map/all_to_all | solution.py:766
  146.6 0.8 copy.23
  (31 shorter events, 4.5 us)
Async XLA Ops:
  0.0 18.8 %copy-start.7 = (s32[72]{0:T(128)S(1)}, s32[72]{0:T(128)}, u32[]{:S(2)}) copy-start(s32[72]{0:T(128)} %constant.52.clone) | copy-start | bytes 868
  0.0 21.0 %copy-start.6 = (f32[2,72]{1,0:T(2,128)S(1)}, f32[2,72]{1,0:T(2,128)}, u32[]{:S(2)}) copy-start(f32[2,72]{1,0:T(2,128)} %constant.53.clone) | copy-start | bytes 1732
  0.0 18.9 %copy-start.3 = (s32[2048]{0:T(1024)S(1)}, s32[2048]{0:T(1024)}, u32[]{:S(2)}) copy-start(s32[2048]{0:T(1024)} %param.17) | copy-start | bytes 24580
  0.0 18.9 %copy-start.4 = (f32[2048]{0:T(1024)S(1)}, f32[2048]{0:T(1024)}, u32[]{:S(2)}) copy-start(f32[2048]{0:T(1024)} %param.16) | copy-start | bytes 24580
  0.0 18.9 %copy-start.5 = (f32[2048]{0:T(1024)S(1)}, f32[2048]{0:T(1024)}, u32[]{:S(2)}) copy-start(f32[2048]{0:T(1024)} %param.15) | copy-start | bytes 24580
  0.0 19.5 %copy-start.1 = (f32[6,2048]{1,0:T(8,128)S(1)}, f32[6,2048]{1,0:T(8,128)}, u32[]{:S(2)}) copy-start(f32[6,2048]{1,0:T(8,128)} %param.20) | copy-start | bytes 147460
  0.0 19.5 %copy-start.2 = (f32[6,2048]{1,0:T(8,128)S(1)}, f32[6,2048]{1,0:T(8,128)}, u32[]{:S(2)}) copy-start(f32[6,2048]{1,0:T(8,128)} %param.19) | copy-start | bytes 147460
  5.9 34.9 %all-to-all-start = ((f32[16,112,128]{2,1,0:T(8,128)}), f32[16,112,128]{2,1,0:T(8,128)S(1)}, u32[]{:S(2)}, u32[]{:S(2)}) async-start(f32[16,112,128]{2,1,0:T(8,128)} %shard_map.128), calls=%async_computation | async-start | bytes 1835008 | tf_op jit(solution)/shard_map/all_to_all | solution.py:669
  40.8 0.9 copy-start
  75.1 1.5 %collective-permute-start = (f32[16,2,128]{2,1,0:T(2,128)}, f32[16,2,128]{2,1,0:T(2,128)S(1)}, u32[]{:S(2)}, u32[]{:S(2)}) collective-permute-start(f32[16,2,128]{2,1,0:T(2,128)} %get-tuple-element.26), channel_id=1, source_target_pairs={{0,1},{1,0},{2,3},{3,2},{4,5},{5,4},{6,7},{7,6},{8,9},{9,8},{10,11... | collective-permute-start | bytes 49160 | tf_op jit(solution)/shard_map/ppermute | solution.py:763
  77.3 3.8 %collective-permute-start.1 = (f32[16,2,128]{2,1,0:T(2,128)S(1)}, f32[16,2,128]{2,1,0:T(2,128)S(1)}, u32[]{:S(2)}, u32[]{:S(2)}) collective-permute-start(f32[16,2,128]{2,1,0:T(2,128)S(1)} %add.21), channel_id=1, source_target_pairs={{0,2},{1,3},{2,0},{3,1},{4,6},{5,7},{6,4},{7,5},{8,10},{9,11},{10,... | collective-permute-start | bytes 49160 | tf_op jit(solution)/shard_map/ppermute | solution.py:763
  81.1 3.8 %collective-permute-start.2 = (f32[16,2,128]{2,1,0:T(2,128)S(1)}, f32[16,2,128]{2,1,0:T(2,128)S(1)}, u32[]{:S(2)}, u32[]{:S(2)}) collective-permute-start(f32[16,2,128]{2,1,0:T(2,128)S(1)} %add.22), channel_id=1, source_target_pairs={{0,4},{1,5},{2,6},{3,7},{4,0},{5,1},{6,2},{7,3},{8,12},{9,13},{10,... | collective-permute-start | bytes 49160 | tf_op jit(solution)/shard_map/ppermute | solution.py:763
  84.9 4.7 %collective-permute-start.3 = (f32[16,2,128]{2,1,0:T(2,128)S(1)}, f32[16,2,128]{2,1,0:T(2,128)S(1)}, u32[]{:S(2)}, u32[]{:S(2)}) collective-permute-start(f32[16,2,128]{2,1,0:T(2,128)S(1)} %add.23), channel_id=1, source_target_pairs={{0,8},{1,9},{2,10},{3,11},{4,12},{5,13},{6,14},{7,15},{8,0},{9,1},... | collective-permute-start | bytes 49160 | tf_op jit(solution)/shard_map/ppermute | solution.py:763

commit v4 on v3

--- a/solution.py
+++ b/solution.py
@@ -101,22 +101,8 @@
 GROUPS = 9
 GROUP_ROWS = 8
 BASE_GROUP = (0, 1, 2, 3, 0, 1, 2, 3, 4)
-LISTED = 1024
+LISTED = 768
 CHUNK = 256
-
-
-def row_layout():
-    dirs = np.zeros((GROUPS * GROUP_ROWS,), np.int32)
-    upper = np.zeros((GROUPS * GROUP_ROWS,), np.int32)
-    for row in range(GROUPS * GROUP_ROWS):
-        group, sub = divmod(row, GROUP_ROWS)
-        if group < 8:
-            dirs[row] = 8 * (group % 4) + sub
-            upper[row] = group // 4
-        else:
-            dirs[row] = 32 + sub % 4
-            upper[row] = sub // 4
-    return dirs, upper
 
 
 def group_rows(group):
@@ -140,36 +126,86 @@
     ref[block, pl.ds(68, 4), :] = values[8][4:8]
 
 
-def row_tables(device_place):
-    dirs, upper = row_layout()
-    freq = (2 * device_place + jnp.asarray(upper)).astype(jnp.int32)
-    radian_freq, weight, _, freq_top = freq_tables(freq * NDIR)
-    relative = radian_freq / freq_top
-    group_speed = courant * 0.25 / radian_freq
-    table = jnp.stack([radian_freq, 0.6 * relative, relative * relative * freq_top, group_speed, weight, weight / radian_freq])
-    return jnp.broadcast_to(table[:, :, None], table.shape + (LANES,))
-
-
-def direction_tables():
-    dirs, _ = row_layout()
-    angle = dirs.astype(np.float64) * (2.0 * np.pi / NDIR)
-    table = np.stack([np.cos(angle), np.sin(angle)]).astype(np.float32)
-    return jnp.asarray(np.broadcast_to(table[:, :, None], table.shape + (LANES,)))
-
-
-def setup_kernel(points_ref, x_ref, y_ref, rows_ref, dirs_ref, keep_ref, growth_ref):
-    edge_count = x_ref.shape[0]
+def frequency(place):
+    return 0.25 * 1.1**place
+
+
+FREQ_TOP = frequency(NFREQ - 1)
+FREQ_TOTAL = NDIR * sum(frequency(place) for place in range(NFREQ))
+
+
+def setup_kernel(
+    place_ref,
+    bound_ref,
+    speed_ref,
+    heading_ref,
+    mask_ref,
+    near_in,
+    x_in,
+    y_in,
+    keep_ref,
+    growth_ref,
+    rows_ref,
+    dirs_ref,
+    points_ref,
+    select_ref,
+    near_ref,
+    x_ref,
+    y_ref,
+):
+    f32 = jnp.float32
+    edge_count = near_ref.shape[0]
+    blocks = keep_ref.shape[0]
+    sub = lax.broadcasted_iota(jnp.int32, (GROUP_ROWS, LANES), 0)
+    for group in range(GROUPS):
+        rows = group_rows(group)
+        upper = jnp.where(sub < 4, 0, 1) if group == 8 else jnp.full((GROUP_ROWS, LANES), group // 4, jnp.int32)
+        number = 32 + (sub & 3) if group == 8 else 8 * (group % 4) + sub
+        radian_freq = 0.25 * jnp.exp((2 * place_ref[0] + upper).astype(f32) * math.log(1.1))
+        relative = radian_freq * (1.0 / FREQ_TOP)
+        rows_ref[0, rows, :] = radian_freq
+        rows_ref[1, rows, :] = 0.6 * relative
+        rows_ref[2, rows, :] = relative * relative * FREQ_TOP
+        rows_ref[3, rows, :] = courant * 0.25 / radian_freq
+        rows_ref[4, rows, :] = radian_freq * (1.0 / FREQ_TOTAL)
+        rows_ref[5, rows, :] = jnp.full((GROUP_ROWS, LANES), 1.0 / FREQ_TOTAL, f32)
+        angle = number.astype(f32) * (2.0 * math.pi / NDIR)
+        dirs_ref[0, rows, :] = jnp.cos(angle)
+        dirs_ref[1, rows, :] = jnp.sin(angle)
+
+    for place in range(blocks):
+        lanes = slice(LANES * place, LANES * (place + 1))
+        for source, target in ((near_in, near_ref), (x_in, x_ref), (y_in, y_ref)):
+            tile = source[:, lanes]
+            for edge in range(edge_count):
+                target[edge, place : place + 1, :] = tile[edge : edge + 1]
+
+    count = bound_ref.shape[0]
+    order = lax.broadcasted_iota(jnp.int32, (count, LANES), 0)
+    lane = lax.broadcasted_iota(jnp.int32, (count, LANES), 1)
+    spots = jnp.zeros((count, LANES), jnp.int32)
+    for number in range(count):
+        spots = jnp.where(order == number, bound_ref[number], spots)
+    rest = jnp.zeros((LANES - count, LANES), f32)
 
     def block(place, _):
-        speed = spread_row(points_ref, 0, place) * 0.125
-        heading = spread_row(points_ref, 1, place)
-        active = spread_row(points_ref, 2, place)
-        free = spread_row(points_ref, 3, place)
+        hit = jnp.where(spots == lane + LANES * place, 1.0, 0.0)
+        select_ref[place] = jnp.concatenate([hit, rest], axis=0).astype(jnp.bfloat16)
+        fixed = jnp.max(hit, axis=0, keepdims=True) > 0.0
+        sea = mask_ref[pl.ds(place, 1), :].astype(f32)
+        open_row = jnp.where(fixed, 0.0, sea)
+        points_ref[0, pl.ds(place, 1), :] = sea
+        points_ref[1, pl.ds(place, 1), :] = open_row
+        points_ref[2, pl.ds(place, 1), :] = jnp.where(fixed, 1.0, sea)
+        active = jnp.broadcast_to(sea, (GROUP_ROWS, LANES))
+        free = jnp.broadcast_to(open_row, (GROUP_ROWS, LANES))
+        speed = spread_row(speed_ref, place) * 0.125
+        heading = spread_row(heading_ref, place)
         along, across = speed * jnp.cos(heading), speed * jnp.sin(heading)
         total = []
         for group in (0, 1, 2, 3, 8):
             cosine, sine = dirs_ref[0, group_rows(group), :], dirs_ref[1, group_rows(group), :]
-            out = jnp.zeros((GROUP_ROWS, LANES), jnp.float32)
+            out = jnp.zeros((GROUP_ROWS, LANES), f32)
             for edge in range(edge_count):
                 flow = cosine * spread_row(x_ref, edge, place) + sine * spread_row(y_ref, edge, place)
                 out = out + jnp.maximum(flow, 0.0)
@@ -182,7 +218,7 @@
             keep_ref[place, rows, :] = (1.0 - rows_ref[3, rows, :] * total[BASE_GROUP[group]]) * free
         return 0
 
-    lax.fori_loop(0, keep_ref.shape[0], block, 0)
+    lax.fori_loop(0, blocks, block, 0)
 
 
 def spread_row(ref, *place):
@@ -217,12 +253,21 @@
     places,
     values,
     picked,
+    homes,
     sems,
 ):
     f32, bf16 = jnp.float32, jnp.bfloat16
     edge_count, blocks, _ = near_ref.shape
-    free = points_ref[3]
-    high = [near_ref[edge] >> 7 for edge in range(edge_count)]
+    for edge in range(edge_count):
+        for part in range(blocks // GROUP_ROWS):
+            rows = pl.ds(GROUP_ROWS * part, GROUP_ROWS)
+            near = near_ref[edge, rows, :]
+            lanes, home = near & (LANES - 1), near >> 7
+            alive = jnp.zeros((GROUP_ROWS, LANES), f32)
+            for source in range(blocks):
+                alive = jnp.where(home == source, take_lanes(spread_row(points_ref, 2, source), lanes), alive)
+            homes[edge, rows, :] = jnp.where(alive * points_ref[1, rows, :] > 0.0, home, -1)
+    high = [homes[edge] for edge in range(edge_count)]
 
     def block(place, _):
         wanted = lax.broadcasted_iota(jnp.int32, (blocks, LANES), 0)
@@ -231,18 +276,17 @@
         y = jnp.zeros((blocks, LANES), f32)
         for edge in reversed(range(edge_count)):
             near = jnp.broadcast_to(near_ref[edge, pl.ds(place, 1), :], (blocks, LANES))
-            hit = (near >> 7) == wanted
+            hit = jnp.broadcast_to(homes[edge, pl.ds(place, 1), :], (blocks, LANES)) == wanted
             lanes = jnp.where(hit, near & (LANES - 1), lanes)
             x = jnp.where(hit, jnp.broadcast_to(x_ref[edge, pl.ds(place, 1), :], (blocks, LANES)), x)
             y = jnp.where(hit, jnp.broadcast_to(y_ref[edge, pl.ds(place, 1), :], (blocks, LANES)), y)
-        open_row = spread_row(points_ref, 3, place)
         for source in range(blocks):
             first[place, source] = jnp.broadcast_to(lanes[source : source + 1], (GROUP_ROWS, LANES))
             x_row = jnp.broadcast_to(x[source : source + 1], (GROUP_ROWS, LANES))
             y_row = jnp.broadcast_to(y[source : source + 1], (GROUP_ROWS, LANES))
             for group, rows in enumerate((0, 1, 2, 3, 8)):
                 flow = dirs_ref[0, group_rows(rows), :] * x_row + dirs_ref[1, group_rows(rows), :] * y_row
-                base[place, source, group_rows(group), :] = jnp.minimum(flow, 0.0) * open_row
+                base[place, source, group_rows(group), :] = jnp.minimum(flow, 0.0)
         return 0
 
     lax.fori_loop(0, blocks, block, 0)
@@ -252,12 +296,12 @@
 
     marks[...] = jnp.zeros_like(marks)
     for edge in range(edge_count):
-        again = jnp.zeros((blocks, LANES), jnp.bool_)
+        again = jnp.zeros((blocks, LANES), f32)
         for before in range(edge):
-            again = again | (high[before] == high[edge])
-        marks[pl.ds(blocks * edge, blocks), :] = jnp.where(again, free, 0.0)
+            again = jnp.where(high[before] == high[edge], 1.0, again)
+        marks[pl.ds(blocks * edge, blocks), :] = jnp.where(high[edge] >= 0, again, 0.0)
         x_parts, y_parts = split_three(x_ref[edge]), split_three(y_ref[edge])
-        rows = ((near_ref[edge] & (LANES - 1)).astype(f32), high[edge].astype(f32)) + x_parts + y_parts
+        rows = ((near_ref[edge] & (LANES - 1)).astype(f32), (near_ref[edge] >> 7).astype(f32)) + x_parts + y_parts
         for place in range(blocks):
             side, column = divmod(place, blocks // 2)
             for number, row in enumerate(rows):
@@ -293,7 +337,7 @@
     copies.append(pltpu.make_async_copy(scatter, scatter_out, sems.at[2]))
     copies[-1].start()
 
-    chunks = LISTED // CHUNK
+    chunks = blocks * LANES // (2 * CHUNK)
     for side in range(2):
         wide = None
         for column in range(chunks):
@@ -335,14 +379,6 @@
         copy.wait()
 
 
-def frequency(place):
-    return 0.25 * 1.1**place
-
-
-FREQ_TOP = frequency(NFREQ - 1)
-FREQ_TOTAL = NDIR * sum(frequency(place) for place in range(NFREQ))
-
-
 def dissipation_rate(energy, inverse):
     mean_freq = energy / (inverse + epsilon)
     steepness = energy * (0.5 * mean_freq) * (0.5 * mean_freq)
@@ -359,11 +395,13 @@
     f32 = jnp.float32
     lane = lax.broadcasted_iota(jnp.int32, (LANES, LANES), 1)
     cell = lax.broadcasted_iota(jnp.int32, (LANES, LANES), 0) + first_ref[0]
-    norm = weights_ref[...] / jnp.sum(weights_ref[...], axis=0, keepdims=True)
+    weights = jnp.concatenate([weights_ref[...]] * 4, axis=1)
+    norm = weights / jnp.sum(weights, axis=0, keepdims=True)
+    cells = jnp.concatenate([cells_ref[...]] * 4, axis=1)
     table = jnp.zeros((LANES, LANES), f32)
     for corner in range(cells_ref.shape[0]):
-        hit = jnp.broadcast_to(cells_ref[corner : corner + 1, :], (LANES, LANES)) == cell
-        table = table + jnp.where(hit, jnp.broadcast_to(norm[corner : corner + 1, :], (LANES, LANES)), 0.0)
+        hit = jnp.broadcast_to(cells[corner : corner + 1], (LANES, LANES)) == cell
+        table = table + jnp.where(hit, jnp.broadcast_to(norm[corner : corner + 1], (LANES, LANES)), 0.0)
     later = (lane & 32) != 0
     bf16 = jnp.bfloat16
     parts = [split_bf16(jnp.where(later, 0.0, table)), split_bf16(jnp.where(later, table, 0.0))]
@@ -433,19 +471,32 @@
     else:
         start_ref, slope_ref, out_ref = rest[:3]
     scratch = rest[4:] if first else rest[3:]
-    field, words, speed, first_ref, base_ref, gather_ref, scatter_ref, pairs, inflow_ref, terms, sems = scratch
+    field, words, speed, first_ref, base_ref, gather_ref, scatter_ref, pairs, ends, inflow_ref, terms, sems = scratch
     f32, bf16 = jnp.float32, jnp.bfloat16
     blocks = keep_ref.shape[0]
     half = blocks // 2
     edge_count = near_ref.shape[0]
     first_step = 0 if first else SUB
-    copies = [
-        pltpu.make_async_copy(source, target, sems.at[number])
-        for number, (source, target) in enumerate(
-            ((first_in, first_ref), (base_in, base_ref), (gather_in, gather_ref), (scatter_in, scatter_ref))
+    halves = []
+    for side in range(2):
+        points = pl.ds(half * side, half)
+        chunks = pl.ds(LISTED // CHUNK * side, LISTED // CHUNK)
+        columns = pl.ds(half * LANES // CHUNK * side, half * LANES // CHUNK)
+        halves.append(
+            [
+                pltpu.make_async_copy(source.at[part], target.at[part], sems.at[side, number])
+                for number, (source, target, part) in enumerate(
+                    (
+                        (first_in, first_ref, points),
+                        (base_in, base_ref, points),
+                        (gather_in, gather_ref, chunks),
+                        (scatter_in, scatter_ref, columns),
+                    )
+                )
+            ]
         )
-    ]
-    for copy in copies:
+    order = halves[0][:3] + halves[1][:3] + halves[0][3:] + halves[1][3:]
+    for copy in order:
         copy.start()
 
     if first:
@@ -502,58 +553,43 @@
         speed[rows, :] = rows_ref[3, rows, :] * (top * (1.0 / top_code))
         return [(value * scale + 0.5).astype(jnp.int32) for value in values]
 
-    def fine_step(number, _):
-        for group in range(4):
-            lower, upper = encode(group, 65535.0), encode(group + 4, 65535.0)
-            for place in range(blocks):
-                pairs[place, group_rows(group), :] = (upper[place] << 16) | lower[place]
-        for place in range(blocks):
-            for group in range(GROUPS):
-                high, low = split_bf16(field[0, place, group_rows(group), :])
-                both = jnp.concatenate([high, low], axis=0).astype(bf16)
-                words[pl.ds(16 * group, 16), pl.ds(LANES * place, LANES)] = both
-
-        def collect(chunk, _):
+    def collect(side):
+        for chunk in range(LISTED // CHUNK * side, LISTED // CHUNK * (side + 1)):
             found = jnp.dot(words[...], gather_ref[chunk], preferred_element_type=f32)
             for group in range(GROUPS):
                 value = found[16 * group : 16 * group + 8] + found[16 * group + 8 : 16 * group + 16]
                 high, low = split_bf16(value * listed_ref[chunk, group_rows(BASE_GROUP[group]), :])
                 terms[chunk, pl.ds(16 * group, 16), :] = jnp.concatenate([high, low], axis=0).astype(bf16)
-            for side in range(2):
-                place = 2 * chunk + side
-                inflow = [jnp.zeros((GROUP_ROWS, LANES), f32)] * GROUPS
-                for source in range(blocks):
-                    lanes = first_ref[place, source]
-                    for group in range(4):
-                        base = base_ref[place, source, group_rows(group), :]
-                        word = take_lanes(pairs[source, group_rows(group), :], lanes)
-                        lower = (word & 65535).astype(f32)
-                        upper = lax.shift_right_logical(word, 16).astype(f32)
-                        inflow[group] = inflow[group] + base * lower
-                        inflow[group + 4] = inflow[group + 4] + base * upper
-                    last = take_lanes(field[0, source, group_rows(8), :], lanes)
-                    inflow[8] = inflow[8] + base_ref[place, source, group_rows(4), :] * last
-                for group in range(GROUPS):
-                    factor = speed[group_rows(group), :] if group < 8 else rows_ref[3, group_rows(8), :]
-                    inflow_ref[place, group_rows(group), :] = factor * inflow[group]
-            return 0
-
-        lax.fori_loop(0, blocks // 2, collect, 0)
-
-        def update(chunk, _):
-            chunks = LISTED // CHUNK
-            begin = (chunk // chunks) * chunks
+        for place in range(half * side, half * (side + 1)):
+            inflow = [jnp.zeros((GROUP_ROWS, LANES), f32)] * GROUPS
+            for source in range(blocks):
+                lanes = first_ref[place, source]
+                for group in range(4):
+                    base = base_ref[place, source, group_rows(group), :]
+                    word = take_lanes(pairs[source, group_rows(group), :], lanes)
+                    lower = (word & 65535).astype(f32)
+                    upper = lax.shift_right_logical(word, 16).astype(f32)
+                    inflow[group] = inflow[group] + base * lower
+                    inflow[group + 4] = inflow[group + 4] + base * upper
+                inflow[8] = inflow[8] + base_ref[place, source, group_rows(4), :] * take_lanes(ends[source], lanes)
+            for group in range(GROUPS):
+                factor = speed[group_rows(group), :] if group < 8 else rows_ref[3, group_rows(8), :]
+                inflow_ref[place, group_rows(group), :] = factor * inflow[group]
+
+    def update(side, number):
+        parts = LISTED // CHUNK
+        for chunk in range(half // 2 * side, half // 2 * (side + 1)):
             moved = None
-            for part in range(chunks):
+            for part in range(parts):
                 term = jnp.dot(
-                    terms[begin + part],
+                    terms[parts * side + part],
                     scatter_ref[chunk, pl.ds(CHUNK * part, CHUNK), :],
                     preferred_element_type=f32,
                 )
                 moved = term if moved is None else moved + term
-            for side in range(2):
-                place = 2 * chunk + side
-                lanes = slice(LANES * side, LANES * (side + 1))
+            for column in range(2):
+                place = 2 * chunk + column
+                lanes = slice(LANES * column, LANES * (column + 1))
                 for group in range(GROUPS):
                     rows = group_rows(group)
                     more = moved[16 * group : 16 * group + 8, lanes] + moved[16 * group + 8 : 16 * group + 16, lanes]
@@ -563,14 +599,37 @@
                         - rows_ref[3, rows, :] * more
                         + boundary(place, rows, number)
                     )
-            return 0
-
-        lax.fori_loop(0, blocks // 2, update, 0)
+
+    def fine_step(number, _):
+        for group in range(4):
+            lower, upper = encode(group, 65535.0), encode(group + 4, 65535.0)
+            for place in range(blocks):
+                pairs[place, group_rows(group), :] = (upper[place] << 16) | lower[place]
+        for place in range(blocks):
+            ends[place] = field[0, place, group_rows(8), :]
+            for group in range(GROUPS):
+                high, low = split_bf16(field[0, place, group_rows(group), :])
+                both = jnp.concatenate([high, low], axis=0).astype(bf16)
+                words[pl.ds(16 * group, 16), pl.ds(LANES * place, LANES)] = both
+
+        def arrive(copies):
+            @pl.when(number == 0)
+            def _():
+                for copy in copies:
+                    copy.wait()
+
+        arrive(order[:3])
+        collect(0)
+        arrive(order[3:7])
+        update(0, number)
+        collect(1)
+        arrive(order[7:])
+        update(1, number)
         return 0
 
     def plain_step(number, _):
         def block(place, _):
-            free = spread_row(points_ref, 3, place)
+            free = spread_row(points_ref, 1, place)
             inflow = [jnp.zeros((GROUP_ROWS, LANES), f32)] * GROUPS
             for edge in range(edge_count):
                 near = spread_row(near_ref, edge, place)
@@ -596,8 +655,6 @@
         field[0] = field[1]
         return 0
 
-    for copy in copies:
-        copy.wait()
     fits = fits_ref[0]
 
     @pl.when(fits != 0)
@@ -606,6 +663,8 @@
 
     @pl.when(fits == 0)
     def _():
+        for copy in order:
+            copy.wait()
         lax.fori_loop(0, SUB, plain_step, 0)
 
     def leave(place, _):
@@ -641,7 +700,7 @@
     coarse_spectra,
     wind_speed,
     wind_heading,
-    active,
+    sea_mask,
     neighbours,
     edge_x,
     edge_y,
@@ -665,25 +724,39 @@
         out_specs=pl.BlockSpec(memory_space=pltpu.VMEM),
         scratch_shapes=[pltpu.VMEM((comp_total, LANES), f32)],
         compiler_params=params(),
-    )(first_point, spectra_in, coarse_spectra, jnp.tile(bound_cells, (1, 4)), jnp.tile(bound_weights, (1, 4)))
+    )(first_point, spectra_in, coarse_spectra, bound_cells, bound_weights)
     received = lax.all_to_all(send, "pts", split_axis=0, concat_axis=0, tiled=True)
 
-    spread = bound_points[:, None] == jnp.arange(grid_points, dtype=jnp.int32)[None, :]
-    select = jnp.pad(spread.astype(jnp.bfloat16), ((0, LANES - bound_count), (0, 0)))
-    select = select.reshape(LANES, blocks, LANES).transpose(1, 0, 2)
-    free = jnp.where(jnp.any(spread, axis=0), 0.0, active)
-    points = jnp.stack([wind_speed, wind_heading, active, free]).reshape(4, blocks, LANES)
-    near, edge_x, edge_y = [array.reshape(edge_count, blocks, LANES) for array in (neighbours, edge_x, edge_y)]
-    rows, dirs = row_tables(device_place), direction_tables()
+    by_block = (blocks, LANES)
     state_shape = jax.ShapeDtypeStruct((blocks, local_count, LANES), f32)
-    keep, growth = pl.pallas_call(
+    edge_shape = (edge_count, blocks, LANES)
+    keep, growth, rows, dirs, points, select, near, edge_x, edge_y = pl.pallas_call(
         setup_kernel,
-        out_shape=[state_shape] * 2,
-        in_specs=in_vmem(5),
-        out_specs=in_vmem(2),
+        out_shape=[
+            state_shape,
+            state_shape,
+            jax.ShapeDtypeStruct((6, local_count, LANES), f32),
+            jax.ShapeDtypeStruct((2, local_count, LANES), f32),
+            jax.ShapeDtypeStruct((3,) + by_block, f32),
+            jax.ShapeDtypeStruct((blocks, LANES, LANES), jnp.bfloat16),
+            jax.ShapeDtypeStruct(edge_shape, jnp.int32),
+            jax.ShapeDtypeStruct(edge_shape, f32),
+            jax.ShapeDtypeStruct(edge_shape, f32),
+        ],
+        in_specs=[pl.BlockSpec(memory_space=pltpu.SMEM)] * 2 + in_vmem(6),
+        out_specs=in_vmem(9),
         compiler_params=params(),
         cost_estimate=pl.CostEstimate(flops=100_000_000, bytes_accessed=4_000_000, transcendentals=1_000_000),
-    )(points, edge_x, edge_y, rows, dirs)
+    )(
+        device_place.astype(jnp.int32).reshape(1),
+        bound_points,
+        wind_speed.reshape(by_block),
+        wind_heading.reshape(by_block),
+        sea_mask.reshape(by_block),
+        neighbours,
+        edge_x,
+        edge_y,
+    )
 
     shapes = [
         ((blocks, blocks, GROUP_ROWS, LANES), jnp.int32),
@@ -703,8 +776,9 @@
         + [
             pltpu.VMEM((LANES, LANES), f32),
             pltpu.VMEM((2, LANES, LANES), f32),
-            pltpu.VMEM((2, 8 * edge_count, LISTED), f32),
-            pltpu.VMEM((16, LANES), f32),
+            pltpu.VMEM((2, 8 * edge_count, grid_points // 2), f32),
+            pltpu.VMEM((2 * LISTED // LANES, LANES), f32),
+            pltpu.VMEM(edge_shape, jnp.int32),
             pltpu.SemaphoreType.DMA((4,)),
         ],
         compiler_params=params(),
@@ -731,9 +805,10 @@
             + tables
             + [
                 pltpu.VMEM((blocks, 32, LANES), jnp.int32),
+                pltpu.VMEM((blocks, GROUP_ROWS, LANES), f32),
                 pltpu.VMEM((blocks, local_count, LANES), f32),
                 pltpu.VMEM((2 * LISTED // CHUNK, 2 * local_count, CHUNK), jnp.bfloat16),
-                pltpu.SemaphoreType.DMA((4,)),
+                pltpu.SemaphoreType.DMA((2, 4)),
             ],
             compiler_params=params(),
         )(
@@ -801,7 +876,7 @@
             coarse_spectra,
             wind_speed,
             wind_heading,
-            active,
+            sea_mask,
             neighbours,
             edge_x,
             edge_y,

time: 148 us -> 113 us (0.76)
  Pallas kernels: 88.3 us -> 60.3 us
  local copies, waits for them, and re-layouts: 9.24 us -> 1.76 us
  waiting for transfers between devices: 6.66 us -> 10.5 us
  other arithmetic: 3.76 us -> 1.36 us
  starting transfers between devices: 14.6 us -> 16.2 us
    pallas_call x2, Pallas kernels: 66.2 us -> 40.5 us  [fine(): pl.pallas_call(functools.partial(fine_kernel, is_first), out_shape=out_sh...]
    all_to_all x1, waiting for transfers between devices: 0.01 us -> 4.04 us  [whole_frequencies(): lax.all_to_all(send, 'pts', split_axis=0, concat_axis=0, tiled=True)]
    another operation x6 -> x0, local copies, waits for them, and re-layouts: 3.54 us -> none  [the longest x2 1.45 us: whole_frequencies(): jnp.tile(bound_cells, (1, 4))]
    pallas_call x1, Pallas kernels: 15.8 us -> 13.2 us  [whole_frequencies(): pl.pallas_call(plan_kernel, out_shape=[jax.ShapeDtypeStruct(shape, dtype)...]
    ppermute x4, starting transfers between devices: 7.18 us -> 8.8 us  [whole_frequencies(): sums = sums + lax.ppermute(sums, 'pts', pairs)]
    unnamed x18 -> x3, local copies, waits for them, and re-layouts: 3.24 us -> 1.76 us
  transfers between devices with their start and end apart: 5 -> 5, of which waited for: 4 -> 5; matrix products, arithmetic and copies ran while one was open for 5% -> 0% of each run, Pallas kernels for 13% -> 15%
where the time goes in v4:
time: 113 us; the launch traced here: 112 us
  Pallas kernels  60.3 us (53%)
  blocking collectives  22.1 us (20%)
  starting transfers between devices  16.2 us (14%)
  waiting for transfers between devices  10.5 us (9%)
  local copies, waits for them, and re-layouts  1.76 us (2%)
  other arithmetic  1.36 us (1%)
    pallas_call x2, Pallas kernels, fine(): pl.pallas_call(functools.partial(fine_kernel, is_first), out_shape=out_sh...  40.5 us
    all_to_all x1, blocking collectives, whole_frequencies(): lax.all_to_all(field, 'pts', split_axis=0, concat_axis=0, tiled=True)  22.1 us
    pallas_call x1, Pallas kernels, whole_frequencies(): pl.pallas_call(plan_kernel, out_shape=[jax.ShapeDtypeStruct(shape, dtype)...  13.2 us
    ppermute x4, starting transfers between devices, whole_frequencies(): sums = sums + lax.ppermute(sums, 'pts', pairs)  8.8 us
    all_to_all x1, starting transfers between devices, whole_frequencies(): lax.all_to_all(send, 'pts', split_axis=0, concat_axis=0, tiled=True)  7.39 us
    ppermute x4, waiting for transfers between devices, whole_frequencies(): sums = sums + lax.ppermute(sums, 'pts', pairs)  6.43 us
    all_to_all x1, waiting for transfers between devices, whole_frequencies(): lax.all_to_all(send, 'pts', split_axis=0, concat_axis=0, tiled=True)  4.04 us
    pallas_call x1, Pallas kernels, whole_frequencies(): pl.pallas_call(setup_kernel, out_shape=[state_shape, state_shape, jax.Sha...  3.56 us
  transfers between devices with their start and end apart: 5, of which 5 were waited for; matrix products, arithmetic and copies ran while one was open for 0% of the time, Pallas kernels for 15%

profile of v4, /device:TPU:0, one launch (start us, length us, event | category | flops | bytes accessed | tf_op | source)
XLA Modules:
  0.0 112.3 jit_solution(1233382051414871766)
XLA Ops:
  0.0 3.1 %shard_map.111 = f32[16,112,128]{2,1,0:T(8,128)} custom-call(s32[1]{0:T(128)} %bitcast.4.first_ref, f32[1152,128]{1,0:T(8,128)} %spectra_ref.1, f32[2,1152,128]{2,1,0:T(8,128)} %coarse_ref.1, s32[4,32]{1,0:T(4,128)} %cells_ref.1, f32[4,32]{1,0:T(4,128)} %weights_ref.1), custom_call_target="tpu_custom_call" | custom-call | tf_op jit(solution)/shard_map/pallas_call | solution.py:720
  3.1 7.4 %all-to-all-start = ((f32[16,112,128]{2,1,0:T(8,128)}), f32[16,112,128]{2,1,0:T(8,128)S(1)}, u32[]{:S(2)}, u32[]{:S(2)}) async-start(f32[16,112,128]{2,1,0:T(8,128)} %shard_map.111), calls=%async_computation | async-start | bytes 1835008 | tf_op jit(solution)/shard_map/all_to_all | solution.py:728
  10.5 3.6 %shard_map.109 = (f32[16,72,128]{2,1,0:T(8,128)}, f32[16,72,128]{2,1,0:T(8,128)}, f32[6,72,128]{2,1,0:T(8,128)}, f32[2,72,128]{2,1,0:T(8,128)}, f32[3,16,128]{2,...) custom-call(s32[1]{0:T(128)} %bitcast.place_ref, ...), custom_call_target="tpu_custom_call" | custom-call | flops 100000000 | bytes 4000000 | tf_op jit(solution)/shard_map/pallas_call | solution.py:733
  14.1 13.2 %shard_map.110 = (s32[16,16,8,128]{3,2,1,0:T(8,128)}, f32[16,16,40,128]{3,2,1,0:T(8,128)}, bf16[6,2048,256]{2,1,0:T(8,128)(2,1)}, bf16[8,768,256]{2,1,0:T(8,128)(2,1)}, f32[6,40,256]{2,1,0:T(8,128)}, /*index=5*/s32[1]{0:T(128)}) custom-call(s32[6,16,128]{2,1,0:T(8,128)} %get-tuple-element.24.near_ref, f32[6,16,128]{2,1,0:T(8,128)} %get-tuple-element.25.x_ref, ...), custom_call_target="tpu_custom_call" | custom-call | flops 1000000000 | bytes 20000000 | tf_op jit(solution)/shard_map/pallas_call | solution.py:768
  27.3 4.0 %all-to-all-done.state_ref = f32[16,112,128]{2,1,0:T(8,128)S(1)} async-done(((f32[16,112,128]{2,1,0:T(8,128)}), f32[16,112,128]{2,1,0:T(8,128)S(1)}, u32[]{:S(2)}, u32[]{:S(2)}) %all-to-all-start) | async-done | bytes 917536 | tf_op jit(solution)/shard_map/all_to_all | solution.py:728
  31.3 0.0 copy-start
  31.3 0.9 copy-done
  32.3 20.5 %shard_map.112 = (f32[16,72,128]{2,1,0:T(8,128)}, f32[16,2,128]{2,1,0:T(2,128)}, f32[16,72,128]{2,1,0:T(8,128)}, f32[16,72,128]{2,1,0:T(8,128)}) custom-call(s32[1]{0:T(128)} %get-tuple-element.29.fits_ref, f32[16,112,128]{2,1,0:T(8,128)} %copy-done, bf16[16,128,128]{2,1,0:T(8,128)(2,1)} %get-tuple-element.30.extra_ref, ...), custom_call_target="tpu_custom_call" | custom-call | tf_op jit(solution)/shard_map/pallas_call | solution.py:792
  52.7 0.5 collective-permute-start
  53.2 1.0 collective-permute-done
  54.3 0.7 add.12
  55.0 1.9 %collective-permute-start.1 = (f32[16,2,128]{2,1,0:T(2,128)S(1)}, f32[16,2,128]{2,1,0:T(2,128)S(1)}, u32[]{:S(2)}, u32[]{:S(2)}) collective-permute-start(f32[16,2,128]{2,1,0:T(2,128)S(1)} %add.12), channel_id=1, source_target_pairs={{0,2},{1,3},{2,0},{3,1},{4,6},{5,7},{6,4},{7,5},{8,10},{9,11},{10,... | collective-permute-start | bytes 49160 | tf_op jit(solution)/shard_map/ppermute | solution.py:838
  56.9 1.9 %collective-permute-done.1 = f32[16,2,128]{2,1,0:T(2,128)S(1)} collective-permute-done((f32[16,2,128]{2,1,0:T(2,128)S(1)}, f32[16,2,128]{2,1,0:T(2,128)S(1)}, u32[]{:S(2)}, u32[]{:S(2)}) %collective-permute-start.1) | collective-permute-done | bytes 16416 | tf_op jit(solution)/shard_map/ppermute | solution.py:838
  58.8 3.1 %collective-permute-start.2 = (f32[16,2,128]{2,1,0:T(2,128)S(1)}, f32[16,2,128]{2,1,0:T(2,128)S(1)}, u32[]{:S(2)}, u32[]{:S(2)}) collective-permute-start(f32[16,2,128]{2,1,0:T(2,128)S(1)} %add.13), channel_id=1, source_target_pairs={{0,4},{1,5},{2,6},{3,7},{4,0},{5,1},{6,2},{7,3},{8,12},{9,13},{10,... | collective-permute-start | bytes 49160 | tf_op jit(solution)/shard_map/ppermute | solution.py:838
  61.9 1.7 %collective-permute-done.2 = f32[16,2,128]{2,1,0:T(2,128)S(1)} collective-permute-done((f32[16,2,128]{2,1,0:T(2,128)S(1)}, f32[16,2,128]{2,1,0:T(2,128)S(1)}, u32[]{:S(2)}, u32[]{:S(2)}) %collective-permute-start.2) | collective-permute-done | bytes 16416 | tf_op jit(solution)/shard_map/ppermute | solution.py:838
  63.7 3.4 %collective-permute-start.3 = (f32[16,2,128]{2,1,0:T(2,128)S(1)}, f32[16,2,128]{2,1,0:T(2,128)S(1)}, u32[]{:S(2)}, u32[]{:S(2)}) collective-permute-start(f32[16,2,128]{2,1,0:T(2,128)S(1)} %add.14), channel_id=1, source_target_pairs={{0,8},{1,9},{2,10},{3,11},{4,12},{5,13},{6,14},{7,15},{8,0},{9,1},... | collective-permute-start | bytes 49160 | tf_op jit(solution)/shard_map/ppermute | solution.py:838
  67.0 1.7 %collective-permute-done.3 = f32[16,2,128]{2,1,0:T(2,128)S(1)} collective-permute-done((f32[16,2,128]{2,1,0:T(2,128)S(1)}, f32[16,2,128]{2,1,0:T(2,128)S(1)}, u32[]{:S(2)}, u32[]{:S(2)}) %collective-permute-start.3) | collective-permute-done | bytes 16416 | tf_op jit(solution)/shard_map/ppermute | solution.py:838
  68.7 0.6 add.15.extra_ref
  69.4 20.0 %shard_map.113 = f32[16,72,128]{2,1,0:T(8,128)} custom-call(s32[1]{0:T(128)} %get-tuple-element.29.fits_ref, f32[16,72,128]{2,1,0:T(8,128)} %get-tuple-element.39.state_ref, f32[16,2,128]{2,1,0:T(2,128)} %add.15.extra_ref, s32[6,16,128]{2,1,0:T(8,128)} %get-tuple-element.24.near_ref, f32[6,16,128]{2,1,0:T(8,128)} %get-tuple-element.25.x_ref, ...), custom_call_target="tpu_custom_call" | custom-call | tf_op jit(solution)/shard_map/pallas_call | solution.py:792
  89.4 22.1 %all_to_all.10 = f32[16,72,128]{2,1,0:T(8,128)S(1)} all-to-all(f32[16,72,128]{2,1,0:T(8,128)} %shard_map.113), channel_id=1, replica_groups=mesh['groups'=2,'pts'=16] {'pts'}, dimensions={0} | all-to-all | bytes 1179648 | tf_op jit(solution)/shard_map/all_to_all | solution.py:841
  111.5 0.8 copy.13
  (2 shorter events, 0.0 us)
Async XLA Ops:
  3.1 28.2 %all-to-all-start = ((f32[16,112,128]{2,1,0:T(8,128)}), f32[16,112,128]{2,1,0:T(8,128)S(1)}, u32[]{:S(2)}, u32[]{:S(2)}) async-start(f32[16,112,128]{2,1,0:T(8,128)} %shard_map.111), calls=%async_computation | async-start | bytes 1835008 | tf_op jit(solution)/shard_map/all_to_all | solution.py:728
  31.3 0.9 copy-start
  52.7 1.5 %collective-permute-start = (f32[16,2,128]{2,1,0:T(2,128)}, f32[16,2,128]{2,1,0:T(2,128)S(1)}, u32[]{:S(2)}, u32[]{:S(2)}) collective-permute-start(f32[16,2,128]{2,1,0:T(2,128)} %get-tuple-element.40), channel_id=1, source_target_pairs={{0,1},{1,0},{2,3},{3,2},{4,5},{5,4},{6,7},{7,6},{8,9},{9,8},{10,11... | collective-permute-start | bytes 49160 | tf_op jit(solution)/shard_map/ppermute | solution.py:838
  55.0 3.8 %collective-permute-start.1 = (f32[16,2,128]{2,1,0:T(2,128)S(1)}, f32[16,2,128]{2,1,0:T(2,128)S(1)}, u32[]{:S(2)}, u32[]{:S(2)}) collective-permute-start(f32[16,2,128]{2,1,0:T(2,128)S(1)} %add.12), channel_id=1, source_target_pairs={{0,2},{1,3},{2,0},{3,1},{4,6},{5,7},{6,4},{7,5},{8,10},{9,11},{10,... | collective-permute-start | bytes 49160 | tf_op jit(solution)/shard_map/ppermute | solution.py:838
  58.8 4.8 %collective-permute-start.2 = (f32[16,2,128]{2,1,0:T(2,128)S(1)}, f32[16,2,128]{2,1,0:T(2,128)S(1)}, u32[]{:S(2)}, u32[]{:S(2)}) collective-permute-start(f32[16,2,128]{2,1,0:T(2,128)S(1)} %add.13), channel_id=1, source_target_pairs={{0,4},{1,5},{2,6},{3,7},{4,0},{5,1},{6,2},{7,3},{8,12},{9,13},{10,... | collective-permute-start | bytes 49160 | tf_op jit(solution)/shard_map/ppermute | solution.py:838
  63.7 5.1 %collective-permute-start.3 = (f32[16,2,128]{2,1,0:T(2,128)S(1)}, f32[16,2,128]{2,1,0:T(2,128)S(1)}, u32[]{:S(2)}, u32[]{:S(2)}) collective-permute-start(f32[16,2,128]{2,1,0:T(2,128)S(1)} %add.14), channel_id=1, source_target_pairs={{0,8},{1,9},{2,10},{3,11},{4,12},{5,13},{6,14},{7,15},{8,0},{9,1},... | collective-permute-start | bytes 49160 | tf_op jit(solution)/shard_map/ppermute | solution.py:838

commit v5 on v4

--- a/solution.py
+++ b/solution.py
@@ -239,14 +239,12 @@
     y_ref,
     points_ref,
     dirs_ref,
-    first_out,
-    base_out,
+    first_ref,
+    normal_ref,
     gather_out,
     scatter_out,
     listed_ref,
     fits_ref,
-    first,
-    base,
     gather,
     scatter,
     marks,
@@ -280,19 +278,13 @@
             lanes = jnp.where(hit, near & (LANES - 1), lanes)
             x = jnp.where(hit, jnp.broadcast_to(x_ref[edge, pl.ds(place, 1), :], (blocks, LANES)), x)
             y = jnp.where(hit, jnp.broadcast_to(y_ref[edge, pl.ds(place, 1), :], (blocks, LANES)), y)
-        for source in range(blocks):
-            first[place, source] = jnp.broadcast_to(lanes[source : source + 1], (GROUP_ROWS, LANES))
-            x_row = jnp.broadcast_to(x[source : source + 1], (GROUP_ROWS, LANES))
-            y_row = jnp.broadcast_to(y[source : source + 1], (GROUP_ROWS, LANES))
-            for group, rows in enumerate((0, 1, 2, 3, 8)):
-                flow = dirs_ref[0, group_rows(rows), :] * x_row + dirs_ref[1, group_rows(rows), :] * y_row
-                base[place, source, group_rows(group), :] = jnp.minimum(flow, 0.0)
+        first_ref[place] = lanes
+        normal_ref[0, place] = x
+        normal_ref[1, place] = y
         return 0
 
     lax.fori_loop(0, blocks, block, 0)
-    copies = [pltpu.make_async_copy(first, first_out, sems.at[0]), pltpu.make_async_copy(base, base_out, sems.at[1])]
-    for copy in copies:
-        copy.start()
+    copies = []
 
     marks[...] = jnp.zeros_like(marks)
     for edge in range(edge_count):
@@ -334,7 +326,7 @@
         return 0
 
     lax.fori_loop(0, blocks, scatter_block, 0)
-    copies.append(pltpu.make_async_copy(scatter, scatter_out, sems.at[2]))
+    copies.append(pltpu.make_async_copy(scatter, scatter_out, sems.at[0]))
     copies[-1].start()
 
     chunks = blocks * LANES // (2 * CHUNK)
@@ -373,7 +365,7 @@
         return 0
 
     lax.fori_loop(0, 2 * LISTED // LANES, gather_block, 0)
-    copies.append(pltpu.make_async_copy(gather, gather_out, sems.at[3]))
+    copies.append(pltpu.make_async_copy(gather, gather_out, sems.at[1]))
     copies[-1].start()
     for copy in copies:
         copy.wait()
@@ -460,8 +452,8 @@
     growth_ref,
     rows_ref,
     listed_ref,
-    first_in,
-    base_in,
+    first_ref,
+    normal_ref,
     gather_in,
     scatter_in,
     *rest,
@@ -471,7 +463,7 @@
     else:
         start_ref, slope_ref, out_ref = rest[:3]
     scratch = rest[4:] if first else rest[3:]
-    field, words, speed, first_ref, base_ref, gather_ref, scatter_ref, pairs, ends, inflow_ref, terms, sems = scratch
+    field, words, speed, base_ref, gather_ref, scatter_ref, pairs, ends, inflow_ref, terms, moments, sems = scratch
     f32, bf16 = jnp.float32, jnp.bfloat16
     blocks = keep_ref.shape[0]
     half = blocks // 2
@@ -479,7 +471,6 @@
     first_step = 0 if first else SUB
     halves = []
     for side in range(2):
-        points = pl.ds(half * side, half)
         chunks = pl.ds(LISTED // CHUNK * side, LISTED // CHUNK)
         columns = pl.ds(half * LANES // CHUNK * side, half * LANES // CHUNK)
         halves.append(
@@ -487,15 +478,13 @@
                 pltpu.make_async_copy(source.at[part], target.at[part], sems.at[side, number])
                 for number, (source, target, part) in enumerate(
                     (
-                        (first_in, first_ref, points),
-                        (base_in, base_ref, points),
                         (gather_in, gather_ref, chunks),
                         (scatter_in, scatter_ref, columns),
                     )
                 )
             ]
         )
-    order = halves[0][:3] + halves[1][:3] + halves[0][3:] + halves[1][3:]
+    order = [halves[0][0], halves[1][0], halves[0][1], halves[1][1]]
     for copy in order:
         copy.start()
 
@@ -506,6 +495,12 @@
         rolled = [total] + [pltpu.roll(total, LANES - 32 * piece, 1) for piece in range(1, 4)]
         high, low = split_bf16(jnp.concatenate(rolled, axis=0))
         bound = jnp.concatenate([high, low], axis=0).astype(jnp.bfloat16)
+
+    else:
+        total = extra_ref[0]
+        for source in range(1, blocks):
+            total = total + extra_ref[source]
+        moments[...] = total
 
     def spread(place):
         values = jnp.dot(bound, extra_ref[place], preferred_element_type=jnp.float32)
@@ -527,21 +522,24 @@
             values = load_natural(state_ref, place)
             spread(place)
         else:
-            energy = jnp.broadcast_to(extra_ref[place, 0:1, :], (GROUP_ROWS, LANES))
-            inverse = jnp.broadcast_to(extra_ref[place, 1:2, :], (GROUP_ROWS, LANES))
-            loss = dissipation_rate(energy, inverse)
+            loss = dissipation_rate(spread_row(moments, place), spread_row(moments, blocks + place))
             values = [state_ref[place, group_rows(group), :] for group in range(GROUPS)]
         lower, upper, last = [jnp.exp(-rows_ref[2, group_rows(group), :] * loss) for group in (0, 4, 8)]
         decay = [lower] * 4 + [upper] * 4 + [last]
         for group in range(GROUPS):
             rows = group_rows(group)
             field[0, place, rows, :] = values[group] * growth_ref[place, rows, :] * decay[group]
+        for source in range(blocks):
+            x, y = spread_row(normal_ref, 0, place, source), spread_row(normal_ref, 1, place, source)
+            for group, number in enumerate((0, 1, 2, 3, 8)):
+                flow = dirs_ref[0, group_rows(number), :] * x + dirs_ref[1, group_rows(number), :] * y
+                base_ref[place, source, group_rows(group), :] = jnp.minimum(flow, 0.0)
         return 0
 
     lax.fori_loop(0, blocks, enter, 0)
 
     def boundary(place, rows, number):
-        time_frac = (number + (first_step + 1)).astype(f32) * (1.0 / (STEPS * SUB))
+        time_frac = jnp.asarray(number + (first_step + 1), jnp.int32).astype(f32) * (1.0 / (STEPS * SUB))
         return start_ref[place, rows, :] + time_frac * slope_ref[place, rows, :]
 
     def encode(group, top_code):
@@ -563,7 +561,7 @@
         for place in range(half * side, half * (side + 1)):
             inflow = [jnp.zeros((GROUP_ROWS, LANES), f32)] * GROUPS
             for source in range(blocks):
-                lanes = first_ref[place, source]
+                lanes = spread_row(first_ref, place, source)
                 for group in range(4):
                     base = base_ref[place, source, group_rows(group), :]
                     word = take_lanes(pairs[source, group_rows(group), :], lanes)
@@ -600,7 +598,7 @@
                         + boundary(place, rows, number)
                     )
 
-    def fine_step(number, _):
+    def fine_step(number, arrivals):
         for group in range(4):
             lower, upper = encode(group, 65535.0), encode(group + 4, 65535.0)
             for place in range(blocks):
@@ -612,19 +610,21 @@
                 both = jnp.concatenate([high, low], axis=0).astype(bf16)
                 words[pl.ds(16 * group, 16), pl.ds(LANES * place, LANES)] = both
 
-        def arrive(copies):
-            @pl.when(number == 0)
-            def _():
-                for copy in copies:
-                    copy.wait()
-
-        arrive(order[:3])
+        def arrive(count):
+            for copy in arrivals[:count]:
+                copy.wait()
+            del arrivals[:count]
+
+        arrive(1)
         collect(0)
-        arrive(order[3:7])
+        arrive(2)
         update(0, number)
         collect(1)
-        arrive(order[7:])
+        arrive(1)
         update(1, number)
+
+    def later_step(number, _):
+        fine_step(number, [])
         return 0
 
     def plain_step(number, _):
@@ -659,7 +659,8 @@
 
     @pl.when(fits != 0)
     def _():
-        lax.fori_loop(0, SUB, fine_step, 0)
+        fine_step(0, list(order))
+        lax.fori_loop(1, SUB, later_step, 0)
 
     @pl.when(fits == 0)
     def _():
@@ -678,13 +679,16 @@
                 energy = part if energy is None else energy + part
                 part = rows_ref[5, rows, :] * values[group]
                 inverse = part if inverse is None else inverse + part
-            sums_ref[place, 0:1, :] = jnp.sum(energy, axis=0, keepdims=True)
-            sums_ref[place, 1:2, :] = jnp.sum(inverse, axis=0, keepdims=True)
+            moments[pl.ds(place, 1), :] = jnp.sum(energy, axis=0, keepdims=True)
+            moments[pl.ds(blocks + place, 1), :] = jnp.sum(inverse, axis=0, keepdims=True)
         else:
             store_natural(out_ref, place, values)
         return 0
 
     lax.fori_loop(0, blocks, leave, 0)
+    if first:
+        for target in range(sums_ref.shape[0]):
+            sums_ref[target] = moments[...]
 
 
 def in_vmem(count):
@@ -759,18 +763,21 @@
     )
 
     shapes = [
-        ((blocks, blocks, GROUP_ROWS, LANES), jnp.int32),
-        ((blocks, blocks, 40, LANES), f32),
         ((2 * LISTED // CHUNK, grid_points, CHUNK), jnp.bfloat16),
         ((grid_points // CHUNK, LISTED, CHUNK), jnp.bfloat16),
     ]
     tables = [pltpu.VMEM(shape, dtype) for shape, dtype in shapes]
-    first_edge, base, gather, scatter, listed, fits = pl.pallas_call(
+    first_edge, normals, gather, scatter, listed, fits = pl.pallas_call(
         plan_kernel,
-        out_shape=[jax.ShapeDtypeStruct(shape, dtype) for shape, dtype in shapes]
+        out_shape=[
+            jax.ShapeDtypeStruct((blocks,) + by_block, jnp.int32),
+            jax.ShapeDtypeStruct((2, blocks) + by_block, f32),
+        ]
+        + [jax.ShapeDtypeStruct(shape, dtype) for shape, dtype in shapes]
         + [jax.ShapeDtypeStruct((2 * LISTED // CHUNK, 40, CHUNK), f32), jax.ShapeDtypeStruct((1,), jnp.int32)],
         in_specs=in_vmem(5),
-        out_specs=[pl.BlockSpec(memory_space=pl.ANY)] * 4
+        out_specs=in_vmem(2)
+        + [pl.BlockSpec(memory_space=pl.ANY)] * 2
         + [pl.BlockSpec(memory_space=pltpu.VMEM), pl.BlockSpec(memory_space=pltpu.SMEM)],
         scratch_shapes=tables
         + [
@@ -779,7 +786,7 @@
             pltpu.VMEM((2, 8 * edge_count, grid_points // 2), f32),
             pltpu.VMEM((2 * LISTED // LANES, LANES), f32),
             pltpu.VMEM(edge_shape, jnp.int32),
-            pltpu.SemaphoreType.DMA((4,)),
+            pltpu.SemaphoreType.DMA((2,)),
         ],
         compiler_params=params(),
         cost_estimate=pl.CostEstimate(flops=1_000_000_000, bytes_accessed=20_000_000, transcendentals=0),
@@ -788,13 +795,13 @@
     def fine(is_first, state, extra, bound):
         out_shape = [state_shape]
         if is_first:
-            out_shape += [jax.ShapeDtypeStruct((blocks, 2, LANES), f32), state_shape, state_shape]
+            out_shape += [jax.ShapeDtypeStruct((device_count, 2 * blocks, LANES), f32), state_shape, state_shape]
         return pl.pallas_call(
             functools.partial(fine_kernel, is_first),
             out_shape=out_shape,
             in_specs=[pl.BlockSpec(memory_space=pltpu.SMEM)]
-            + in_vmem(11)
-            + [pl.BlockSpec(memory_space=pl.ANY)] * 4
+            + in_vmem(13)
+            + [pl.BlockSpec(memory_space=pl.ANY)] * 2
             + in_vmem(len(bound)),
             out_specs=in_vmem(len(out_shape)),
             scratch_shapes=[
@@ -802,13 +809,15 @@
                 pltpu.VMEM((2 * local_count, grid_points), jnp.bfloat16),
                 pltpu.VMEM((local_count, LANES), f32),
             ]
+            + [pltpu.VMEM((blocks, blocks, 40, LANES), f32)]
             + tables
             + [
                 pltpu.VMEM((blocks, 32, LANES), jnp.int32),
                 pltpu.VMEM((blocks, GROUP_ROWS, LANES), f32),
                 pltpu.VMEM((blocks, local_count, LANES), f32),
                 pltpu.VMEM((2 * LISTED // CHUNK, 2 * local_count, CHUNK), jnp.bfloat16),
-                pltpu.SemaphoreType.DMA((2, 4)),
+                pltpu.VMEM((2 * blocks, LANES), f32),
+                pltpu.SemaphoreType.DMA((2, 2)),
             ],
             compiler_params=params(),
         )(
@@ -825,18 +834,14 @@
             rows,
             listed,
             first_edge,
-            base,
+            normals,
             gather,
             scatter,
             *bound,
         )
 
     field, sums, start, slope = fine(True, received, select, ())
-    distance = 1
-    while distance < device_count:
-        pairs = [(place, place ^ distance) for place in range(device_count)]
-        sums = sums + lax.ppermute(sums, "pts", pairs)
-        distance *= 2
+    sums = lax.all_to_all(sums, "pts", split_axis=0, concat_axis=0, tiled=True)
     (field,) = fine(False, field, sums, (start, slope))
     field = lax.all_to_all(field, "pts", split_axis=0, concat_axis=0, tiled=True)
     return field.reshape(comp_total, point_count)

time: 113 us -> 106 us (0.938)
  blocking collectives: 22.1 us -> 37.1 us
  starting transfers between devices: 16.2 us -> 7.39 us
  Pallas kernels: 60.3 us -> 54.2 us
  waiting for transfers between devices: 10.5 us -> 4.78 us
  other arithmetic: 1.36 us -> 0 us
    all_to_all x0 -> x1, blocking collectives: none -> 16.3 us  [whole_frequencies(): sums = lax.all_to_all(sums, 'pts', split_axis=0, concat_axis=0, tiled=True)]
    ppermute x4 -> x0, starting transfers between devices: 8.8 us -> none  [whole_frequencies(): sums = sums + lax.ppermute(sums, 'pts', pairs)]
    ppermute x4 -> x0, waiting for transfers between devices: 6.43 us -> none  [whole_frequencies(): sums = sums + lax.ppermute(sums, 'pts', pairs)]
    pallas_call x2, Pallas kernels: 40.5 us -> 35.1 us  [fine(): pl.pallas_call(functools.partial(fine_kernel, is_first), out_shape=out_sh...]
    add x4 -> x0, other arithmetic: 1.36 us -> none  [whole_frequencies(): sums = sums + lax.ppermute(sums, 'pts', pairs)]
    all_to_all x1, blocking collectives: 22.1 us -> 20.8 us  [whole_frequencies(): lax.all_to_all(field, 'pts', split_axis=0, concat_axis=0, tiled=True)]
  transfers between devices with their start and end apart: 5 -> 1, of which waited for: 5 -> 1; matrix products, arithmetic and copies ran while one was open for 0% -> 0% of each run, Pallas kernels for 15% -> 15%
where the time goes in v5:
time: 106 us; the launch traced here: 105 us
  Pallas kernels  54.2 us (51%)
  blocking collectives  37.1 us (35%)
  starting transfers between devices  7.39 us (7%)
  waiting for transfers between devices  4.78 us (5%)
  local copies, waits for them, and re-layouts  1.74 us (2%)
    pallas_call x2, Pallas kernels, fine(): pl.pallas_call(functools.partial(fine_kernel, is_first), out_shape=out_sh...  35.1 us
    all_to_all x1, blocking collectives, whole_frequencies(): lax.all_to_all(field, 'pts', split_axis=0, concat_axis=0, tiled=True)  20.8 us
    all_to_all x1, blocking collectives, whole_frequencies(): sums = lax.all_to_all(sums, 'pts', split_axis=0, concat_axis=0, tiled=True)  16.3 us
    pallas_call x1, Pallas kernels, whole_frequencies(): pl.pallas_call(plan_kernel, out_shape=[jax.ShapeDtypeStruct((blocks,) + b...  12.5 us
    all_to_all x1, starting transfers between devices, whole_frequencies(): lax.all_to_all(send, 'pts', split_axis=0, concat_axis=0, tiled=True)  7.39 us
    all_to_all x1, waiting for transfers between devices, whole_frequencies(): lax.all_to_all(send, 'pts', split_axis=0, concat_axis=0, tiled=True)  4.78 us
    pallas_call x1, Pallas kernels, whole_frequencies(): pl.pallas_call(setup_kernel, out_shape=[state_shape, state_shape, jax.Sha...  3.56 us
    pallas_call x1, Pallas kernels, whole_frequencies(): pl.pallas_call(pack_kernel, out_shape=jax.ShapeDtypeStruct((device_count,...  3.09 us
  transfers between devices with their start and end apart: 1, of which 1 were waited for; matrix products, arithmetic and copies ran while one was open for 0% of the time, Pallas kernels for 15%

profile of v5, /device:TPU:0, one launch (start us, length us, event | category | flops | bytes accessed | tf_op | source)
XLA Modules:
  0.0 105.3 jit_solution(12284269263896727136)
XLA Ops:
  0.0 3.1 %shard_map.111 = f32[16,112,128]{2,1,0:T(8,128)} custom-call(s32[1]{0:T(128)} %bitcast.4.first_ref, f32[1152,128]{1,0:T(8,128)} %spectra_ref.1, f32[2,1152,128]{2,1,0:T(8,128)} %coarse_ref.1, s32[4,32]{1,0:T(4,128)} %cells_ref.1, f32[4,32]{1,0:T(4,128)} %weights_ref.1), custom_call_target="tpu_custom_call" | custom-call | tf_op jit(solution)/shard_map/pallas_call | solution.py:724
  3.1 7.4 %all-to-all-start = ((f32[16,112,128]{2,1,0:T(8,128)}), f32[16,112,128]{2,1,0:T(8,128)S(1)}, u32[]{:S(2)}, u32[]{:S(2)}) async-start(f32[16,112,128]{2,1,0:T(8,128)} %shard_map.111), calls=%async_computation | async-start | bytes 1835008 | tf_op jit(solution)/shard_map/all_to_all | solution.py:732
  10.5 3.6 %shard_map.109 = (f32[16,72,128]{2,1,0:T(8,128)}, f32[16,72,128]{2,1,0:T(8,128)}, f32[6,72,128]{2,1,0:T(8,128)}, f32[2,72,128]{2,1,0:T(8,128)}, f32[3,16,128]{2,...) custom-call(s32[1]{0:T(128)} %bitcast.place_ref, ...), custom_call_target="tpu_custom_call" | custom-call | flops 100000000 | bytes 4000000 | tf_op jit(solution)/shard_map/pallas_call | solution.py:737
  14.0 12.5 %shard_map.110 = (s32[16,16,128]{2,1,0:T(8,128)}, f32[2,16,16,128]{3,2,1,0:T(8,128)}, bf16[6,2048,256]{2,1,0:T(8,128)(2,1)}, bf16[8,768,256]{2,1,0:T(8,128)(2,1)}, f32[6,40,256]{2,1,0:T(8,128)}, /*index=5*/s32[1]{0:T(128)}) custom-call(s32[6,16,128]{2,1,0:T(8,128)} %get-tuple-element.24.near_ref, f32[6,16,128]{2,1,0:T(8,128)} %get-tuple-element.25.x_ref, ...), custom_call_target="tpu_custom_call" | custom-call | flops 1000000000 | bytes 20000000 | tf_op jit(solution)/shard_map/pallas_call | solution.py:770
  26.5 4.8 %all-to-all-done.state_ref = f32[16,112,128]{2,1,0:T(8,128)S(1)} async-done(((f32[16,112,128]{2,1,0:T(8,128)}), f32[16,112,128]{2,1,0:T(8,128)S(1)}, u32[]{:S(2)}, u32[]{:S(2)}) %all-to-all-start) | async-done | bytes 917536 | tf_op jit(solution)/shard_map/all_to_all | solution.py:732
  31.3 0.0 copy-start
  31.3 0.9 copy-done
  32.2 18.4 %shard_map.112 = (f32[16,72,128]{2,1,0:T(8,128)}, f32[16,32,128]{2,1,0:T(8,128)}, f32[16,72,128]{2,1,0:T(8,128)}, f32[16,72,128]{2,1,0:T(8,128)}) custom-call(s32[1]{0:T(128)} %get-tuple-element.29.fits_ref, f32[16,112,128]{2,1,0:T(8,128)} %copy-done, bf16[16,128,128]{2,1,0:T(8,128)(2,1)} %get-tuple-element.30.extra_ref, ...), custom_call_target="tpu_custom_call" | custom-call | tf_op jit(solution)/shard_map/pallas_call | solution.py:799
  50.7 16.3 %all_to_all.15.extra_ref = f32[16,32,128]{2,1,0:T(8,128)} all-to-all(f32[16,32,128]{2,1,0:T(8,128)} %get-tuple-element.40), channel_id=1, replica_groups=mesh['groups'=2,'pts'=16] {'pts'}, dimensions={0} | all-to-all | bytes 524288 | tf_op jit(solution)/shard_map/all_to_all | solution.py:844
  67.0 16.7 %shard_map.113 = f32[16,72,128]{2,1,0:T(8,128)} custom-call(s32[1]{0:T(128)} %get-tuple-element.29.fits_ref, f32[16,72,128]{2,1,0:T(8,128)} %get-tuple-element.39.state_ref, f32[16,32,128]{2,1,0:T(8,128)} %all_to_all.15.extra_ref, s32[6,16,128]{2,1,0:T(8,128)} %get-tuple-element.24.near_ref, f32[6,16,128]{2,1,0:T(8,128)} %get-tuple-element.25.x_ref, ...), custom_call_target="tpu_custom_call" | custom-call | tf_op jit(solution)/shard_map/pallas_call | solution.py:799
  83.7 20.8 %all_to_all.16 = f32[16,72,128]{2,1,0:T(8,128)S(1)} all-to-all(f32[16,72,128]{2,1,0:T(8,128)} %shard_map.113), channel_id=1, replica_groups=mesh['groups'=2,'pts'=16] {'pts'}, dimensions={0} | all-to-all | bytes 1179648 | tf_op jit(solution)/shard_map/all_to_all | solution.py:846
  104.5 0.8 copy.13
Async XLA Ops:
  3.1 28.2 %all-to-all-start = ((f32[16,112,128]{2,1,0:T(8,128)}), f32[16,112,128]{2,1,0:T(8,128)S(1)}, u32[]{:S(2)}, u32[]{:S(2)}) async-start(f32[16,112,128]{2,1,0:T(8,128)} %shard_map.111), calls=%async_computation | async-start | bytes 1835008 | tf_op jit(solution)/shard_map/all_to_all | solution.py:732
  31.3 0.9 copy-start

commit v6 on v5

--- a/solution.py
+++ b/solution.py
@@ -241,18 +241,15 @@
     dirs_ref,
     first_ref,
     normal_ref,
-    gather_out,
-    scatter_out,
+    gather,
+    scatter,
     listed_ref,
     fits_ref,
-    gather,
-    scatter,
     marks,
     places,
     values,
     picked,
     homes,
-    sems,
 ):
     f32, bf16 = jnp.float32, jnp.bfloat16
     edge_count, blocks, _ = near_ref.shape
@@ -284,7 +281,6 @@
         return 0
 
     lax.fori_loop(0, blocks, block, 0)
-    copies = []
 
     marks[...] = jnp.zeros_like(marks)
     for edge in range(edge_count):
@@ -326,8 +322,6 @@
         return 0
 
     lax.fori_loop(0, blocks, scatter_block, 0)
-    copies.append(pltpu.make_async_copy(scatter, scatter_out, sems.at[0]))
-    copies[-1].start()
 
     chunks = blocks * LANES // (2 * CHUNK)
     for side in range(2):
@@ -365,10 +359,6 @@
         return 0
 
     lax.fori_loop(0, 2 * LISTED // LANES, gather_block, 0)
-    copies.append(pltpu.make_async_copy(gather, gather_out, sems.at[1]))
-    copies[-1].start()
-    for copy in copies:
-        copy.wait()
 
 
 def dissipation_rate(energy, inverse):
@@ -454,8 +444,8 @@
     listed_ref,
     first_ref,
     normal_ref,
-    gather_in,
-    scatter_in,
+    gather_ref,
+    scatter_ref,
     *rest,
 ):
     if first:
@@ -463,31 +453,12 @@
     else:
         start_ref, slope_ref, out_ref = rest[:3]
     scratch = rest[4:] if first else rest[3:]
-    field, words, speed, base_ref, gather_ref, scatter_ref, pairs, ends, inflow_ref, terms, moments, sems = scratch
+    field, words, speed, base_ref, pairs, ends, inflow_ref, terms, moments = scratch
     f32, bf16 = jnp.float32, jnp.bfloat16
     blocks = keep_ref.shape[0]
     half = blocks // 2
     edge_count = near_ref.shape[0]
     first_step = 0 if first else SUB
-    halves = []
-    for side in range(2):
-        chunks = pl.ds(LISTED // CHUNK * side, LISTED // CHUNK)
-        columns = pl.ds(half * LANES // CHUNK * side, half * LANES // CHUNK)
-        halves.append(
-            [
-                pltpu.make_async_copy(source.at[part], target.at[part], sems.at[side, number])
-                for number, (source, target, part) in enumerate(
-                    (
-                        (gather_in, gather_ref, chunks),
-                        (scatter_in, scatter_ref, columns),
-                    )
-                )
-            ]
-        )
-    order = [halves[0][0], halves[1][0], halves[0][1], halves[1][1]]
-    for copy in order:
-        copy.start()
-
     if first:
         total = state_ref[0, pl.ds(2 * NDIR, 40), :]
         for source in range(1, blocks):
@@ -598,7 +569,7 @@
                         + boundary(place, rows, number)
                     )
 
-    def fine_step(number, arrivals):
+    def fine_step(number, _):
         for group in range(4):
             lower, upper = encode(group, 65535.0), encode(group + 4, 65535.0)
             for place in range(blocks):
@@ -610,21 +581,10 @@
                 both = jnp.concatenate([high, low], axis=0).astype(bf16)
                 words[pl.ds(16 * group, 16), pl.ds(LANES * place, LANES)] = both
 
-        def arrive(count):
-            for copy in arrivals[:count]:
-                copy.wait()
-            del arrivals[:count]
-
-        arrive(1)
         collect(0)
-        arrive(2)
         update(0, number)
         collect(1)
-        arrive(1)
         update(1, number)
-
-    def later_step(number, _):
-        fine_step(number, [])
         return 0
 
     def plain_step(number, _):
@@ -659,13 +619,10 @@
 
     @pl.when(fits != 0)
     def _():
-        fine_step(0, list(order))
-        lax.fori_loop(1, SUB, later_step, 0)
+        lax.fori_loop(0, SUB, fine_step, 0)
 
     @pl.when(fits == 0)
     def _():
-        for copy in order:
-            copy.wait()
         lax.fori_loop(0, SUB, plain_step, 0)
 
     def leave(place, _):
@@ -695,8 +652,8 @@
     return [pl.BlockSpec(memory_space=pltpu.VMEM)] * count
 
 
-def params():
-    return pltpu.CompilerParams(vmem_limit_bytes=56 << 20)
+def params(mebibytes=16):
+    return pltpu.CompilerParams(vmem_limit_bytes=mebibytes << 20)
 
 
 def whole_frequencies(
@@ -766,7 +723,6 @@
         ((2 * LISTED // CHUNK, grid_points, CHUNK), jnp.bfloat16),
         ((grid_points // CHUNK, LISTED, CHUNK), jnp.bfloat16),
     ]
-    tables = [pltpu.VMEM(shape, dtype) for shape, dtype in shapes]
     first_edge, normals, gather, scatter, listed, fits = pl.pallas_call(
         plan_kernel,
         out_shape=[
@@ -776,19 +732,15 @@
         + [jax.ShapeDtypeStruct(shape, dtype) for shape, dtype in shapes]
         + [jax.ShapeDtypeStruct((2 * LISTED // CHUNK, 40, CHUNK), f32), jax.ShapeDtypeStruct((1,), jnp.int32)],
         in_specs=in_vmem(5),
-        out_specs=in_vmem(2)
-        + [pl.BlockSpec(memory_space=pl.ANY)] * 2
-        + [pl.BlockSpec(memory_space=pltpu.VMEM), pl.BlockSpec(memory_space=pltpu.SMEM)],
-        scratch_shapes=tables
-        + [
+        out_specs=in_vmem(5) + [pl.BlockSpec(memory_space=pltpu.SMEM)],
+        scratch_shapes=[
             pltpu.VMEM((LANES, LANES), f32),
             pltpu.VMEM((2, LANES, LANES), f32),
             pltpu.VMEM((2, 8 * edge_count, grid_points // 2), f32),
             pltpu.VMEM((2 * LISTED // LANES, LANES), f32),
             pltpu.VMEM(edge_shape, jnp.int32),
-            pltpu.SemaphoreType.DMA((2,)),
         ],
-        compiler_params=params(),
+        compiler_params=params(20),
         cost_estimate=pl.CostEstimate(flops=1_000_000_000, bytes_accessed=20_000_000, transcendentals=0),
     )(near, edge_x, edge_y, points, dirs)
 
@@ -800,26 +752,22 @@
             functools.partial(fine_kernel, is_first),
             out_shape=out_shape,
             in_specs=[pl.BlockSpec(memory_space=pltpu.SMEM)]
-            + in_vmem(13)
-            + [pl.BlockSpec(memory_space=pl.ANY)] * 2
-            + in_vmem(len(bound)),
+            + in_vmem(15 + len(bound)),
             out_specs=in_vmem(len(out_shape)),
             scratch_shapes=[
                 pltpu.VMEM((2, blocks, local_count, LANES), f32),
                 pltpu.VMEM((2 * local_count, grid_points), jnp.bfloat16),
                 pltpu.VMEM((local_count, LANES), f32),
             ]
-            + [pltpu.VMEM((blocks, blocks, 40, LANES), f32)]
-            + tables
             + [
+                pltpu.VMEM((blocks, blocks, 40, LANES), f32),
                 pltpu.VMEM((blocks, 32, LANES), jnp.int32),
                 pltpu.VMEM((blocks, GROUP_ROWS, LANES), f32),
                 pltpu.VMEM((blocks, local_count, LANES), f32),
                 pltpu.VMEM((2 * LISTED // CHUNK, 2 * local_count, CHUNK), jnp.bfloat16),
                 pltpu.VMEM((2 * blocks, LANES), f32),
-                pltpu.SemaphoreType.DMA((2, 2)),
             ],
-            compiler_params=params(),
+            compiler_params=params(28),
         )(
             fits,
             state,

time: 106 us -> 114 us (1.075)
  local copies, waits for them, and re-layouts: 1.74 us -> 26 us
  Pallas kernels: 54.2 us -> 42.8 us
  waiting for transfers between devices: 4.78 us -> 1.02 us
    unnamed x3 -> x69, local copies, waits for them, and re-layouts: 1.74 us -> 26 us
    pallas_call x2, Pallas kernels: 35.1 us -> 30.9 us  [fine(): pl.pallas_call(functools.partial(fine_kernel, is_first), out_shape=out_sh...]
    pallas_call x1, Pallas kernels: 12.5 us -> 8.33 us  [whole_frequencies(): pl.pallas_call(plan_kernel, out_shape=[jax.ShapeDtypeStruct((blocks,) + b...]
    all_to_all x1, waiting for transfers between devices: 4.78 us -> 1.02 us  [whole_frequencies(): lax.all_to_all(send, 'pts', split_axis=0, concat_axis=0, tiled=True)]
    pallas_call x1, Pallas kernels: 3.56 us -> 1.88 us  [whole_frequencies(): pl.pallas_call(setup_kernel, out_shape=[state_shape, state_shape, jax.Sha...]
    pallas_call x1, Pallas kernels: 3.09 us -> 1.75 us  [whole_frequencies(): pl.pallas_call(pack_kernel, out_shape=jax.ShapeDtypeStruct((device_count,...]
  transfers between devices with their start and end apart: 1 -> 1, of which waited for: 1 -> 1; matrix products, arithmetic and copies ran while one was open for 0% -> 0% of each run, Pallas kernels for 15% -> 9%
where the time goes in v6:
time: 114 us; the launch traced here: 113 us
  Pallas kernels  42.8 us (38%)
  blocking collectives  36.1 us (32%)
  local copies, waits for them, and re-layouts  26 us (23%)
  starting transfers between devices  7.43 us (7%)
    pallas_call x2, Pallas kernels, fine(): pl.pallas_call(functools.partial(fine_kernel, is_first), out_shape=out_sh...  30.9 us
    unnamed x69, local copies, waits for them, and re-layouts  26 us
    all_to_all x1, blocking collectives, whole_frequencies(): lax.all_to_all(field, 'pts', split_axis=0, concat_axis=0, tiled=True)  20.1 us
    all_to_all x1, blocking collectives, whole_frequencies(): sums = lax.all_to_all(sums, 'pts', split_axis=0, concat_axis=0, tiled=True)  16 us
    pallas_call x1, Pallas kernels, whole_frequencies(): pl.pallas_call(plan_kernel, out_shape=[jax.ShapeDtypeStruct((blocks,) + b...  8.33 us
    all_to_all x1, starting transfers between devices, whole_frequencies(): lax.all_to_all(send, 'pts', split_axis=0, concat_axis=0, tiled=True)  7.43 us
  transfers between devices with their start and end apart: 1, of which 1 were waited for; matrix products, arithmetic and copies ran while one was open for 0% of the time, Pallas kernels for 9%

profile of v6, /device:TPU:0, one launch (start us, length us, event | category | flops | bytes accessed | tf_op | source)
XLA Modules:
  0.0 113.5 jit_solution(13795079686407858623)
XLA Ops:
  0.0 1.3 %copy-done.7 = f32[2,1152,128]{2,1,0:T(8,128)S(1)} copy-done((f32[2,1152,128]{2,1,0:T(8,128)S(1)}, f32[2,1152,128]{2,1,0:T(8,128)}, u32[]{:S(2)}) %copy-start.7) | copy-done | bytes 1179672
  1.3 1.1 copy-done.12
  3.8 1.7 %shard_map.111 = f32[16,112,128]{2,1,0:T(8,128)} custom-call(s32[1]{0:T(128)} %bitcast.4.first_ref, f32[1152,128]{1,0:T(8,128)S(1)} %copy-done.12, f32[2,1152,128]{2,1,0:T(8,128)S(1)} %copy-done.7, s32[4,32]{1,0:T(4,128)S(1)} %copy-done.25, f32[4,32]{1,0:T(4,128)S(1)} %copy-done.26), custom_call_target="tpu_custom_call" | custom-call | tf_op jit(solution)/shard_map/pallas_call | solution.py:681
  5.5 7.4 %all-to-all-start = ((f32[16,112,128]{2,1,0:T(8,128)}), f32[16,112,128]{2,1,0:T(8,128)}, u32[]{:S(2)}, u32[]{:S(2)}) async-start(f32[16,112,128]{2,1,0:T(8,128)} %shard_map.111), calls=%async_computation | async-start | bytes 1835008 | tf_op jit(solution)/shard_map/all_to_all | solution.py:689
  13.0 1.9 %shard_map.109 = (f32[16,72,128]{2,1,0:T(8,128)S(1)}, f32[16,72,128]{2,1,0:T(8,128)S(1)}, f32[6,72,128]{2,1,0:T(8,128)S(1)}, f32[2,72,128]{2,1,0:T(8,128)S(1)}, ...) custom-call(s32[1]{0:T(128)} %bitcast.place_ref, ...), custom_call_target="tpu_custom_call" | custom-call | flops 100000000 | bytes 4000000 | tf_op jit(solution)/shard_map/pallas_call | solution.py:694
  14.9 0.8 copy-done.3
  15.7 0.9 copy-done.5
  17.3 0.8 copy-done.13
  18.1 8.3 %shard_map.110 = (s32[16,16,128]{2,1,0:T(8,128)S(1)}, f32[2,16,16,128]{3,2,1,0:T(8,128)S(1)}, bf16[6,2048,256]{2,1,0:T(8,128)(2,1)S(1)}, bf16[8,768,256]{2,1,0:T...) custom-call(s32[6,16,128]{2,1,0:T(8,128)S(1)} %get-tuple-element.24.near_ref, ...), custom_call_target="tpu_custom_call" | custom-call | flops 1000000000 | bytes 20000000 | tf_op jit(solution)/shard_map/pallas_call | solution.py:726
  26.4 2.6 %copy-done = bf16[6,2048,256]{2,1,0:T(8,128)(2,1)} copy-done((bf16[6,2048,256]{2,1,0:T(8,128)(2,1)}, bf16[6,2048,256]{2,1,0:T(8,128)(2,1)S(1)}, u32[]{:S(2)}) %copy-start) | copy-done | bytes 6291480
  32.8 1.0 all-to-all-done.state_ref
  33.8 2.8 %copy-done.1 = bf16[6,2048,256]{2,1,0:T(8,128)(2,1)S(1)} copy-done((bf16[6,2048,256]{2,1,0:T(8,128)(2,1)S(1)}, bf16[6,2048,256]{2,1,0:T(8,128)(2,1)}, u32[]{:S(2)}) %copy-start.1) | copy-done | bytes 6291480
  36.6 1.1 copy-done.4
  37.7 1.1 copy-done.6
  38.7 0.9 copy-done.9
  39.7 0.9 copy-done.11
  40.6 1.0 copy-done.14
  41.7 0.9 copy-done.16
  43.3 0.8 copy-done.20
  45.7 17.5 %shard_map.112 = (f32[16,72,128]{2,1,0:T(8,128)S(1)}, f32[16,32,128]{2,1,0:T(8,128)S(1)}, f32[16,72,128]{2,1,0:T(8,128)S(1)}, f32[16,72,128]{2,1,0:T(8,128)S(1)}) custom-call(s32[1]{0:T(128)} %get-tuple-element.29.fits_ref, f32[16,112,128]{2,1,0:T(8,128)} %all-to-all-done.state_ref, bf16[16,128,128]{2,1,0:T(8,128)(2,1)S(1)} %copy-done.14, ...), custom_call_target="tpu_custom_call" | custom-call | tf_op jit(solution)/shard_map/pallas_call | solution.py:751
  63.2 16.0 %all_to_all.15.extra_ref = f32[16,32,128]{2,1,0:T(8,128)S(1)} all-to-all(f32[16,32,128]{2,1,0:T(8,128)S(1)} %get-tuple-element.40), channel_id=1, replica_groups=mesh['groups'=2,'pts'=16] {'pts'}, dimensions={0} | all-to-all | bytes 524288 | tf_op jit(solution)/shard_map/all_to_all | solution.py:792
  79.2 13.4 %shard_map.113 = f32[16,72,128]{2,1,0:T(8,128)S(1)} custom-call(s32[1]{0:T(128)} %get-tuple-element.29.fits_ref, f32[16,72,128]{2,1,0:T(8,128)S(1)} %get-tuple-element.39.state_ref, f32[16,32,128]{2,1,0:T(8,128)S(1)} %all_to_all.15.extra_ref, s32[6,16,128]{2,1,0:T(8,128)S(1)} %copy-done.18, f32[6,16,128]{2,1,0:T(8,128)S(1)} %copy-done.20, ...), custom_call_target="tpu_custom_call" | custom-call | tf_op jit(solution)/shard_map/pallas_call | solution.py:751
  92.6 20.1 %all_to_all.16 = f32[16,72,128]{2,1,0:T(8,128)S(1)} all-to-all(f32[16,72,128]{2,1,0:T(8,128)S(1)} %shard_map.113), channel_id=1, replica_groups=mesh['groups'=2,'pts'=16] {'pts'}, dimensions={0} | all-to-all | bytes 1179648 | tf_op jit(solution)/shard_map/all_to_all | solution.py:794
  112.6 0.8 copy.13
  (54 shorter events, 8.2 us)
Async XLA Ops:
  0.0 12.9 %copy-start.33 = (s32[32]{0:T(128)S(1)}, s32[32]{0:T(128)}, u32[]{:S(2)}) copy-start(s32[32]{0:T(128)} %bound_ref.1) | copy-start | bytes 388
  0.0 12.9 %copy-start.30 = (f32[2048]{0:T(1024)S(1)}, f32[2048]{0:T(1024)}, u32[]{:S(2)}) copy-start(f32[2048]{0:T(1024)} %param.13) | copy-start | bytes 24580
  0.0 1.3 %copy-start.7 = (f32[2,1152,128]{2,1,0:T(8,128)S(1)}, f32[2,1152,128]{2,1,0:T(8,128)}, u32[]{:S(2)}) copy-start(f32[2,1152,128]{2,1,0:T(8,128)} %coarse_ref.1) | copy-start | bytes 3538948
  1.3 1.1 copy-start.12
  3.7 9.2 %copy-start.27 = (s32[6,2048]{1,0:T(8,128)S(1)}, s32[6,2048]{1,0:T(8,128)}, u32[]{:S(2)}) copy-start(s32[6,2048]{1,0:T(8,128)} %near_in.1) | copy-start | bytes 147460
  3.7 9.2 %copy-start.28 = (f32[6,2048]{1,0:T(8,128)S(1)}, f32[6,2048]{1,0:T(8,128)}, u32[]{:S(2)}) copy-start(f32[6,2048]{1,0:T(8,128)} %x_in.1) | copy-start | bytes 147460
  3.7 9.2 %copy-start.29 = (f32[6,2048]{1,0:T(8,128)S(1)}, f32[6,2048]{1,0:T(8,128)}, u32[]{:S(2)}) copy-start(f32[6,2048]{1,0:T(8,128)} %y_in.1) | copy-start | bytes 147460
  3.7 9.3 %copy-start.31 = (f32[2048]{0:T(1024)S(1)}, f32[2048]{0:T(1024)}, u32[]{:S(2)}) copy-start(f32[2048]{0:T(1024)} %param.14) | copy-start | bytes 24580
  3.7 9.3 %copy-start.32 = (s32[2048]{0:T(1024)S(1)}, s32[2048]{0:T(1024)}, u32[]{:S(2)}) copy-start(s32[2048]{0:T(1024)} %param.15) | copy-start | bytes 24580
  5.5 28.3 %all-to-all-start = ((f32[16,112,128]{2,1,0:T(8,128)}), f32[16,112,128]{2,1,0:T(8,128)}, u32[]{:S(2)}, u32[]{:S(2)}) async-start(f32[16,112,128]{2,1,0:T(8,128)} %shard_map.111), calls=%async_computation | async-start | bytes 1835008 | tf_op jit(solution)/shard_map/all_to_all | solution.py:689
  14.9 0.8 copy-start.3
  15.7 0.9 copy-start.5
  17.3 0.8 copy-start.13
  26.4 2.6 %copy-start = (bf16[6,2048,256]{2,1,0:T(8,128)(2,1)}, bf16[6,2048,256]{2,1,0:T(8,128)(2,1)S(1)}, u32[]{:S(2)}) copy-start(bf16[6,2048,256]{2,1,0:T(8,128)(2,1)S(1)} %get-tuple-element.37.gather_ref) | copy-start | bytes 18874372
  33.8 2.8 %copy-start.1 = (bf16[6,2048,256]{2,1,0:T(8,128)(2,1)S(1)}, bf16[6,2048,256]{2,1,0:T(8,128)(2,1)}, u32[]{:S(2)}) copy-start(bf16[6,2048,256]{2,1,0:T(8,128)(2,1)} %copy-done) | copy-start | bytes 18874372
  36.6 1.1 copy-start.4
  37.7 1.1 copy-start.6
  38.7 0.9 copy-start.9
  39.7 0.9 copy-start.11
  40.6 1.0 copy-start.14
  41.7 0.9 copy-start.16
  42.5 0.8 copy-start.18
  43.3 0.8 copy-start.20
  45.7 33.5 %copy-start.2 = (bf16[6,2048,256]{2,1,0:T(8,128)(2,1)S(1)}, bf16[6,2048,256]{2,1,0:T(8,128)(2,1)}, u32[]{:S(2)}) copy-start(bf16[6,2048,256]{2,1,0:T(8,128)(2,1)} %copy-done) | copy-start | bytes 18874372
  (11 other events, 7.3 us)

commit v7 on v6

--- a/solution.py
+++ b/solution.py
@@ -372,6 +372,10 @@
     return high, values - high
 
 
+def two_terms(values):
+    return jnp.concatenate(split_bf16(values), axis=0).astype(jnp.bfloat16)
+
+
 def pack_kernel(first_ref, spectra_ref, coarse_ref, cells_ref, weights_ref, send_ref, shares):
     destinations = send_ref.shape[0]
     f32 = jnp.float32
@@ -444,8 +448,8 @@
     listed_ref,
     first_ref,
     normal_ref,
-    gather_ref,
-    scatter_ref,
+    gather_in,
+    scatter_in,
     *rest,
 ):
     if first:
@@ -453,7 +457,14 @@
     else:
         start_ref, slope_ref, out_ref = rest[:3]
     scratch = rest[4:] if first else rest[3:]
-    field, words, speed, base_ref, pairs, ends, inflow_ref, terms, moments = scratch
+    field, words, speed, base_ref, gather_ref, scatter_ref, pairs, ends, inflow_ref, terms, moments, sems = scratch
+    copies = [
+        pltpu.make_async_copy(source.at[part], target.at[part], sems.at[kind, part])
+        for kind, (source, target) in enumerate(((gather_in, gather_ref), (scatter_in, scatter_ref)))
+        for part in range(target.shape[0])
+    ]
+    for copy in copies:
+        copy.start()
     f32, bf16 = jnp.float32, jnp.bfloat16
     blocks = keep_ref.shape[0]
     half = blocks // 2
@@ -499,7 +510,9 @@
         decay = [lower] * 4 + [upper] * 4 + [last]
         for group in range(GROUPS):
             rows = group_rows(group)
-            field[0, place, rows, :] = values[group] * growth_ref[place, rows, :] * decay[group]
+            value = values[group] * growth_ref[place, rows, :] * decay[group]
+            field[0, place, rows, :] = value
+            words[0, pl.ds(16 * group, 16), pl.ds(pl.multiple_of(LANES * place, LANES), LANES)] = two_terms(value)
         for source in range(blocks):
             x, y = spread_row(normal_ref, 0, place, source), spread_row(normal_ref, 1, place, source)
             for group, number in enumerate((0, 1, 2, 3, 8)):
@@ -522,9 +535,9 @@
         speed[rows, :] = rows_ref[3, rows, :] * (top * (1.0 / top_code))
         return [(value * scale + 0.5).astype(jnp.int32) for value in values]
 
-    def collect(side):
+    def collect(side, now):
         for chunk in range(LISTED // CHUNK * side, LISTED // CHUNK * (side + 1)):
-            found = jnp.dot(words[...], gather_ref[chunk], preferred_element_type=f32)
+            found = jnp.dot(words[now], gather_ref[chunk], preferred_element_type=f32)
             for group in range(GROUPS):
                 value = found[16 * group : 16 * group + 8] + found[16 * group + 8 : 16 * group + 16]
                 high, low = split_bf16(value * listed_ref[chunk, group_rows(BASE_GROUP[group]), :])
@@ -545,7 +558,7 @@
                 factor = speed[group_rows(group), :] if group < 8 else rows_ref[3, group_rows(8), :]
                 inflow_ref[place, group_rows(group), :] = factor * inflow[group]
 
-    def update(side, number):
+    def update(side, number, later):
         parts = LISTED // CHUNK
         for chunk in range(half // 2 * side, half // 2 * (side + 1)):
             moved = None
@@ -562,29 +575,28 @@
                 for group in range(GROUPS):
                     rows = group_rows(group)
                     more = moved[16 * group : 16 * group + 8, lanes] + moved[16 * group + 8 : 16 * group + 16, lanes]
-                    field[0, place, rows, :] = (
+                    value = (
                         field[0, place, rows, :] * keep_ref[place, rows, :]
                         - inflow_ref[place, rows, :]
                         - rows_ref[3, rows, :] * more
                         + boundary(place, rows, number)
                     )
+                    field[0, place, rows, :] = value
+                    words[later, pl.ds(16 * group, 16), pl.ds(LANES * place, LANES)] = two_terms(value)
 
     def fine_step(number, _):
+        now = lax.rem(number, 2)
         for group in range(4):
             lower, upper = encode(group, 65535.0), encode(group + 4, 65535.0)
             for place in range(blocks):
                 pairs[place, group_rows(group), :] = (upper[place] << 16) | lower[place]
         for place in range(blocks):
             ends[place] = field[0, place, group_rows(8), :]
-            for group in range(GROUPS):
-                high, low = split_bf16(field[0, place, group_rows(group), :])
-                both = jnp.concatenate([high, low], axis=0).astype(bf16)
-                words[pl.ds(16 * group, 16), pl.ds(LANES * place, LANES)] = both
-
-        collect(0)
-        update(0, number)
-        collect(1)
-        update(1, number)
+
+        collect(0, now)
+        update(0, number, 1 - now)
+        collect(1, now)
+        update(1, number, 1 - now)
         return 0
 
     def plain_step(number, _):
@@ -615,6 +627,8 @@
         field[0] = field[1]
         return 0
 
+    for copy in copies:
+        copy.wait()
     fits = fits_ref[0]
 
     @pl.when(fits != 0)
@@ -652,7 +666,7 @@
     return [pl.BlockSpec(memory_space=pltpu.VMEM)] * count
 
 
-def params(mebibytes=16):
+def params(mebibytes=56):
     return pltpu.CompilerParams(vmem_limit_bytes=mebibytes << 20)
 
 
@@ -740,7 +754,7 @@
             pltpu.VMEM((2 * LISTED // LANES, LANES), f32),
             pltpu.VMEM(edge_shape, jnp.int32),
         ],
-        compiler_params=params(20),
+        compiler_params=params(),
         cost_estimate=pl.CostEstimate(flops=1_000_000_000, bytes_accessed=20_000_000, transcendentals=0),
     )(near, edge_x, edge_y, points, dirs)
 
@@ -752,22 +766,28 @@
             functools.partial(fine_kernel, is_first),
             out_shape=out_shape,
             in_specs=[pl.BlockSpec(memory_space=pltpu.SMEM)]
-            + in_vmem(15 + len(bound)),
+            + in_vmem(13)
+            + [pl.BlockSpec(memory_space=pl.ANY)] * 2
+            + in_vmem(len(bound)),
             out_specs=in_vmem(len(out_shape)),
             scratch_shapes=[
                 pltpu.VMEM((2, blocks, local_count, LANES), f32),
-                pltpu.VMEM((2 * local_count, grid_points), jnp.bfloat16),
+                pltpu.VMEM((2, 2 * local_count, grid_points), jnp.bfloat16),
                 pltpu.VMEM((local_count, LANES), f32),
             ]
             + [
                 pltpu.VMEM((blocks, blocks, 40, LANES), f32),
+            ]
+            + [pltpu.VMEM(shape, dtype) for shape, dtype in shapes]
+            + [
                 pltpu.VMEM((blocks, 32, LANES), jnp.int32),
                 pltpu.VMEM((blocks, GROUP_ROWS, LANES), f32),
                 pltpu.VMEM((blocks, local_count, LANES), f32),
                 pltpu.VMEM((2 * LISTED // CHUNK, 2 * local_count, CHUNK), jnp.bfloat16),
                 pltpu.VMEM((2 * blocks, LANES), f32),
+                pltpu.SemaphoreType.DMA((2, 8)),
             ],
-            compiler_params=params(28),
+            compiler_params=params(56),
         )(
             fits,
             state,

time: 114 us -> 108 us (0.947)
  local copies, waits for them, and re-layouts: 26 us -> 1.74 us
  Pallas kernels: 42.8 us -> 56.1 us
  waiting for transfers between devices: 1.02 us -> 4.65 us
    unnamed x69 -> x3, local copies, waits for them, and re-layouts: 26 us -> 1.74 us
    pallas_call x2, Pallas kernels: 30.9 us -> 36.8 us  [fine(): pl.pallas_call(functools.partial(fine_kernel, is_first), out_shape=out_sh...]
    pallas_call x1, Pallas kernels: 8.33 us -> 12.6 us  [whole_frequencies(): pl.pallas_call(plan_kernel, out_shape=[jax.ShapeDtypeStruct((blocks,) + b...]
    all_to_all x1, waiting for transfers between devices: 1.02 us -> 4.65 us  [whole_frequencies(): lax.all_to_all(send, 'pts', split_axis=0, concat_axis=0, tiled=True)]
    pallas_call x1, Pallas kernels: 1.88 us -> 3.56 us  [whole_frequencies(): pl.pallas_call(setup_kernel, out_shape=[state_shape, state_shape, jax.Sha...]
    pallas_call x1, Pallas kernels: 1.75 us -> 3.09 us  [whole_frequencies(): pl.pallas_call(pack_kernel, out_shape=jax.ShapeDtypeStruct((device_count,...]
  transfers between devices with their start and end apart: 1 -> 1, of which waited for: 1 -> 1; matrix products, arithmetic and copies ran while one was open for 0% -> 0% of each run, Pallas kernels for 9% -> 15%
where the time goes in v7:
time: 108 us; the launch traced here: 107 us
  Pallas kernels  56.1 us (52%)
  blocking collectives  37.2 us (34%)
  starting transfers between devices  7.39 us (7%)
  waiting for transfers between devices  4.65 us (4%)
  local copies, waits for them, and re-layouts  1.74 us (2%)
    pallas_call x2, Pallas kernels, fine(): pl.pallas_call(functools.partial(fine_kernel, is_first), out_shape=out_sh...  36.8 us
    all_to_all x1, blocking collectives, whole_frequencies(): lax.all_to_all(field, 'pts', split_axis=0, concat_axis=0, tiled=True)  20.8 us
    all_to_all x1, blocking collectives, whole_frequencies(): sums = lax.all_to_all(sums, 'pts', split_axis=0, concat_axis=0, tiled=True)  16.4 us
    pallas_call x1, Pallas kernels, whole_frequencies(): pl.pallas_call(plan_kernel, out_shape=[jax.ShapeDtypeStruct((blocks,) + b...  12.6 us
    all_to_all x1, starting transfers between devices, whole_frequencies(): lax.all_to_all(send, 'pts', split_axis=0, concat_axis=0, tiled=True)  7.39 us
    all_to_all x1, waiting for transfers between devices, whole_frequencies(): lax.all_to_all(send, 'pts', split_axis=0, concat_axis=0, tiled=True)  4.65 us
    pallas_call x1, Pallas kernels, whole_frequencies(): pl.pallas_call(setup_kernel, out_shape=[state_shape, state_shape, jax.Sha...  3.56 us
    pallas_call x1, Pallas kernels, whole_frequencies(): pl.pallas_call(pack_kernel, out_shape=jax.ShapeDtypeStruct((device_count,...  3.09 us
  transfers between devices with their start and end apart: 1, of which 1 were waited for; matrix products, arithmetic and copies ran while one was open for 0% of the time, Pallas kernels for 15%

profile of v7, /device:TPU:0, one launch (start us, length us, event | category | flops | bytes accessed | tf_op | source)
XLA Modules:
  0.0 107.0 jit_solution(72818867775790212)
XLA Ops:
  0.0 3.1 %shard_map.111 = f32[16,112,128]{2,1,0:T(8,128)} custom-call(s32[1]{0:T(128)} %bitcast.4.first_ref, f32[1152,128]{1,0:T(8,128)} %spectra_ref.1, f32[2,1152,128]{2,1,0:T(8,128)} %coarse_ref.1, s32[4,32]{1,0:T(4,128)} %cells_ref.1, f32[4,32]{1,0:T(4,128)} %weights_ref.1), custom_call_target="tpu_custom_call" | custom-call | tf_op jit(solution)/shard_map/pallas_call | solution.py:695
  3.1 7.4 %all-to-all-start = ((f32[16,112,128]{2,1,0:T(8,128)}), f32[16,112,128]{2,1,0:T(8,128)S(1)}, u32[]{:S(2)}, u32[]{:S(2)}) async-start(f32[16,112,128]{2,1,0:T(8,128)} %shard_map.111), calls=%async_computation | async-start | bytes 1835008 | tf_op jit(solution)/shard_map/all_to_all | solution.py:703
  10.5 3.6 %shard_map.109 = (f32[16,72,128]{2,1,0:T(8,128)}, f32[16,72,128]{2,1,0:T(8,128)}, f32[6,72,128]{2,1,0:T(8,128)}, f32[2,72,128]{2,1,0:T(8,128)}, f32[3,16,128]{2,...) custom-call(s32[1]{0:T(128)} %bitcast.place_ref, ...), custom_call_target="tpu_custom_call" | custom-call | flops 100000000 | bytes 4000000 | tf_op jit(solution)/shard_map/pallas_call | solution.py:708
  14.0 12.6 %shard_map.110 = (s32[16,16,128]{2,1,0:T(8,128)}, f32[2,16,16,128]{3,2,1,0:T(8,128)}, bf16[6,2048,256]{2,1,0:T(8,128)(2,1)}, bf16[8,768,256]{2,1,0:T(8,128)(2,1)}, f32[6,40,256]{2,1,0:T(8,128)}, /*index=5*/s32[1]{0:T(128)}) custom-call(s32[6,16,128]{2,1,0:T(8,128)} %get-tuple-element.24.near_ref, f32[6,16,128]{2,1,0:T(8,128)} %get-tuple-element.25.x_ref, ...), custom_call_target="tpu_custom_call" | custom-call | flops 1000000000 | bytes 20000000 | tf_op jit(solution)/shard_map/pallas_call | solution.py:740
  26.6 4.7 %all-to-all-done.state_ref = f32[16,112,128]{2,1,0:T(8,128)S(1)} async-done(((f32[16,112,128]{2,1,0:T(8,128)}), f32[16,112,128]{2,1,0:T(8,128)S(1)}, u32[]{:S(2)}, u32[]{:S(2)}) %all-to-all-start) | async-done | bytes 917536 | tf_op jit(solution)/shard_map/all_to_all | solution.py:703
  31.3 0.0 copy-start
  31.3 0.9 copy-done
  32.2 18.7 %shard_map.112 = (f32[16,72,128]{2,1,0:T(8,128)}, f32[16,32,128]{2,1,0:T(8,128)}, f32[16,72,128]{2,1,0:T(8,128)}, f32[16,72,128]{2,1,0:T(8,128)}) custom-call(s32[1]{0:T(128)} %get-tuple-element.29.fits_ref, f32[16,112,128]{2,1,0:T(8,128)} %copy-done, bf16[16,128,128]{2,1,0:T(8,128)(2,1)} %get-tuple-element.30.extra_ref, ...), custom_call_target="tpu_custom_call" | custom-call | tf_op jit(solution)/shard_map/pallas_call | solution.py:765
  50.9 16.4 %all_to_all.15.extra_ref = f32[16,32,128]{2,1,0:T(8,128)} all-to-all(f32[16,32,128]{2,1,0:T(8,128)} %get-tuple-element.40), channel_id=1, replica_groups=mesh['groups'=2,'pts'=16] {'pts'}, dimensions={0} | all-to-all | bytes 524288 | tf_op jit(solution)/shard_map/all_to_all | solution.py:812
  67.3 18.1 %shard_map.113 = f32[16,72,128]{2,1,0:T(8,128)} custom-call(s32[1]{0:T(128)} %get-tuple-element.29.fits_ref, f32[16,72,128]{2,1,0:T(8,128)} %get-tuple-element.39.state_ref, f32[16,32,128]{2,1,0:T(8,128)} %all_to_all.15.extra_ref, s32[6,16,128]{2,1,0:T(8,128)} %get-tuple-element.24.near_ref, f32[6,16,128]{2,1,0:T(8,128)} %get-tuple-element.25.x_ref, ...), custom_call_target="tpu_custom_call" | custom-call | tf_op jit(solution)/shard_map/pallas_call | solution.py:765
  85.4 20.8 %all_to_all.16 = f32[16,72,128]{2,1,0:T(8,128)S(1)} all-to-all(f32[16,72,128]{2,1,0:T(8,128)} %shard_map.113), channel_id=1, replica_groups=mesh['groups'=2,'pts'=16] {'pts'}, dimensions={0} | all-to-all | bytes 1179648 | tf_op jit(solution)/shard_map/all_to_all | solution.py:814
  106.2 0.8 copy.13
Async XLA Ops:
  3.1 28.2 %all-to-all-start = ((f32[16,112,128]{2,1,0:T(8,128)}), f32[16,112,128]{2,1,0:T(8,128)S(1)}, u32[]{:S(2)}, u32[]{:S(2)}) async-start(f32[16,112,128]{2,1,0:T(8,128)} %shard_map.111), calls=%async_computation | async-start | bytes 1835008 | tf_op jit(solution)/shard_map/all_to_all | solution.py:703
  31.3 0.9 copy-start
